TPU v7x, 32 devices: a whole 2x2x4 slice. The times are simulated.
32 devices in a mesh: section: 4 (over z), dp: 8 (over y, x, core).
Axes of the slice: x: 2, y: 2, z: 4, core: 2. Of those that a mesh axis runs over, the one named last changes fastest.
Arguments:
- tokens: bfloat16 [2048, 4096], P('dp'), may hold values from -48 to 48
- orig_weight: bfloat16 [1024, 4096], P(('section', 'dp')), may hold values from -6 to 6
- keep_flags: int32 [64], replicated, may hold values from 0 to 1, as said below
Outputs:
- corrected: bfloat16 [1024, 4096], P(('section', 'dp'))
Inputs may be any that keep to these rules, and one draw needn't show every extreme that they name: `keep_flags`: exactly 12 of the 64 flags are 1.
All inputs are finite; a program needn't handle non-finite values.
Results may differ from a plain program's by a relative error of at most 0.003.
Values may be sent and summed in bfloat16 or wider, within the bound.
No kernel may reach another device: no remote copies, remote signals or barrier semaphores. Data moves between devices by JAX's collectives and lax.ppermute only.
A program may use at most 64 MiB of HBM per device.

v0:
```python
import functools

import jax
import jax.numpy as jnp
from jax import lax
from jax.experimental import pallas as pl
from jax.experimental.pallas import tpu as pltpu
from jax.sharding import PartitionSpec as P

KEEP_BLK = 12
PANEL = 128
SUB = 8
EXTRA = 16
VMEM_LIMIT = 32 * 1024 * 1024
NT = (((1,), (1,)), ((), ()))
NN = (((1,), (0,)), ((), ()))


def split3(x):
    hi = x.astype(jnp.bfloat16)
    rest = x - hi.astype(jnp.float32)
    mid = rest.astype(jnp.bfloat16)
    low = (rest - mid.astype(jnp.float32)).astype(jnp.bfloat16)
    return hi, mid, low


def dot32(a, b, dims):
    return lax.dot_general(a, b, dims, preferred_element_type=jnp.float32)


def kept_blocks(flags_ref, index_ref):
    count = jnp.int32(0)
    for b in range(flags_ref.shape[0]):
        index_ref[count] = b
        count = count + flags_ref[b]


def select_kernel(side_ref, flags_in_ref, tokens_ref, out_ref, half_ref, *scratch):
    flags_ref, index_ref, held_ref, sem, flags_sem = scratch
    rows, features = tokens_ref.shape
    blocks = flags_ref.shape[0]
    width = features // blocks
    per_tile = 128 // width
    chunks = sem.shape[0]
    step = rows // chunks
    fetch = pltpu.make_async_copy(flags_in_ref, flags_ref, flags_sem)
    fetch.start()
    reads = []
    for c in range(chunks):
        part = pl.ds(c * step, step)
        reads.append(pltpu.make_async_copy(tokens_ref.at[part, :], held_ref.at[part, :], sem.at[c]))
        reads[-1].start()
    fetch.wait()
    kept_blocks(flags_ref, index_ref)
    row = lax.broadcasted_iota(jnp.int32, (width, 128), 0)
    lane = lax.broadcasted_iota(jnp.int32, (width, 128), 1)
    total = jnp.zeros((step, 128), jnp.float32)
    for c in range(chunks):
        reads[c].wait()
        part = slice(c * step, (c + 1) * step)
        for i in range(KEEP_BLK):
            b = index_ref[i]
            start = pl.multiple_of((b // per_tile) * 128, 128)
            pick = jnp.where(lane == row + (b % per_tile) * width, 1.0, 0.0).astype(jnp.bfloat16)
            picked = dot32(pick, held_ref[part, pl.ds(start, 128)], NT)
            out_ref[i * width:(i + 1) * width, part] = picked.astype(jnp.bfloat16)
        for f in range(features // 128):
            piece = held_ref[part, f * 128:(f + 1) * 128].astype(jnp.float32)
            total += piece * piece
    squares = jnp.sum(total)
    hi, mid, low = split3(jnp.full((EXTRA, rows), squares, jnp.float32))
    row = lax.broadcasted_iota(jnp.int32, (EXTRA, rows), 0)
    carried = jnp.where(
        row == 0,
        hi.astype(jnp.float32),
        jnp.where(row == 1, mid.astype(jnp.float32), jnp.where(row == 2, low.astype(jnp.float32), 0.0)),
    )
    kept = KEEP_BLK * width
    out_ref[kept:, :] = carried.astype(jnp.bfloat16)
    half = kept // 2
    half_ref[:half, :] = out_ref[pl.ds(pl.multiple_of(side_ref[0] * half, half), half), :]
    half_ref[half:, :] = carried.astype(jnp.bfloat16)


def select_kept(side, tokens, keep_flags):
    rows, features = tokens.shape
    blocks = keep_flags.shape[0]
    kept = KEEP_BLK * (features // blocks)
    chunks = rows // 128
    return pl.pallas_call(
        select_kernel,
        out_shape=[
            jax.ShapeDtypeStruct((kept + EXTRA, rows), jnp.bfloat16),
            jax.ShapeDtypeStruct((kept // 2 + EXTRA, rows), jnp.bfloat16),
        ],
        in_specs=[pl.BlockSpec(memory_space=pltpu.SMEM)] + [pl.BlockSpec(memory_space=pltpu.HBM)] * 2,
        out_specs=[pl.BlockSpec(memory_space=pltpu.VMEM)] * 2,
        scratch_shapes=[
            pltpu.SMEM((blocks,), jnp.int32),
            pltpu.SMEM((blocks + 1,), jnp.int32),
            pltpu.VMEM((rows, features), jnp.bfloat16),
            pltpu.SemaphoreType.DMA((chunks,)),
            pltpu.SemaphoreType.DMA,
        ],
        compiler_params=pltpu.CompilerParams(vmem_limit_bytes=VMEM_LIMIT),
        name="select_kept",
    )(side, keep_flags, tokens)


def lane_column(x, c):
    return jnp.broadcast_to(x[:, c:c + 1], (SUB, 128))


def sublane_row(x, t):
    return jnp.broadcast_to(x[t:t + 1, :], (SUB, 128))


def tree_sum(terms):
    while len(terms) > 1:
        pairs = [terms[i] + terms[i + 1] for i in range(0, len(terms) - 1, 2)]
        terms = pairs + terms[len(terms) - len(terms) % 2:]
    return terms[0]


def block_entries(block, base):
    entry = {}
    for j in range(SUB):
        column = lane_column(block, base + j)
        for i in range(j + 1):
            entry[i, j] = sublane_row(column, i)
    return entry


def solve_small(entry, rows, cross, ahead):
    entry, rows, cross, ahead = dict(entry), list(rows), list(cross), list(ahead)
    lower = {}
    for t in range(0, SUB, 2):
        u = t + 1
        a, b, c = entry[t, t], entry[t, u], entry[u, u]
        first = pl.reciprocal(a, approx=True)
        second = a * pl.reciprocal(a * c - b * b, approx=True)
        lower[u, t] = b * first
        later = range(u + 1, SUB)
        rest = {}
        for j in later:
            lower[j, t] = entry[t, j] * first
            rest[j] = entry[u, j] - b * lower[j, t]
        for j in later:
            for i in range(u + 1, j + 1):
                partial = entry[i, j] - entry[t, i] * lower[j, t]
                entry[i, j] = partial - (rest[i] * rest[j]) * second
        for j in later:
            lower[j, u] = rest[j] * second
        for part in (cross, rows):
            if part:
                part[u] = part[u] - lower[u, t] * part[t]
                for j in later:
                    part[j] = (part[j] - lower[j, t] * part[t]) - lower[j, u] * part[u]
        if cross:
            left, right = cross[t] * first, cross[u] * second
            for j in range(SUB):
                ahead[j] = (ahead[j] - left * sublane_row(cross[t], j)) - right * sublane_row(cross[u], j)
        rows[t] = rows[t] * first
        rows[u] = rows[u] * second
    following = {(i, j): sublane_row(ahead[j], i) for j in range(SUB) for i in range(j + 1) if cross}
    for t in reversed(range(SUB)):
        for j in range(t):
            rows[j] = rows[j] - lower[t, j] * rows[t]
    return rows, following


def factor_panel(block, beside=()):
    size = block.shape[0]
    count = size // SUB
    sub = lax.broadcasted_iota(jnp.int32, (SUB, 128), 0)
    lane = lax.broadcasted_iota(jnp.int32, (SUB, 128), 1)
    rows = [block[i * SUB:(i + 1) * SUB, :] for i in range(count)]
    entry = block_entries(rows[0], 0)
    lower, scaled = [], []
    done = 0
    for s in range(count):
        base = s * SUB
        inside = (lane >= base) & (lane < base + SUB)
        cross, ahead = [], []
        if s + 1 < count:
            cross = [lane_column(rows[s + 1], base + j) for j in range(SUB)]
            ahead = [lane_column(rows[s + 1], base + SUB + j) for j in range(SUB)]
        pivot_rows = jnp.where(inside, jnp.where(lane == sub + base, 1.0, 0.0), rows[s])
        spread, entry = solve_small(entry, [sublane_row(pivot_rows, j) for j in range(SUB)], cross, ahead)
        for i in range(s + 1, count):
            columns = cross if i == s + 1 else [lane_column(rows[i], base + j) for j in range(SUB)]
            change = tree_sum([columns[j] * spread[j] for j in range(SUB)])
            rows[i] = jnp.where(inside, 0.0, rows[i]) - change
        new = spread[SUB - 1]
        for j in range(SUB - 1):
            new = jnp.where(sub == j, spread[j], new)
        lower.append(jnp.where(lane < base + SUB, pivot_rows, 0.0))
        scaled.append(jnp.where(lane < base + SUB, new, 0.0))
        until = len(beside) * (s + 1) // count
        for task in beside[done:until]:
            task()
        done = until
    return jnp.concatenate(lower, axis=0), jnp.concatenate(scaled, axis=0)


def wide_left(x):
    hi, mid, low = split3(x)
    return jnp.concatenate([hi, hi, mid, hi, mid, low], axis=1)


def wide_right(x):
    hi, mid, low = split3(x)
    return jnp.concatenate([hi, mid, hi, low, mid, hi], axis=0)


def wide_across(x):
    hi, mid, low = split3(x)
    return jnp.concatenate([hi, mid, hi, low, mid, hi], axis=1)


def spans(low, high):
    first = low + (high - low) % 256
    starts = ([low] if first > low else []) + list(range(first, high, 256))
    return list(zip(starts, starts[1:] + [high]))


def settle_tasks(p, state, lower_ref, scaled_ref):
    a_ref, offset, _, w_ref, left_ref, right_ref = state
    kept = w_ref.shape[1]
    at = p * PANEL
    low = at + PANEL
    here = slice(at - offset, low - offset)
    rest = slice(low - offset, kept - offset)

    def make_w(c, d):
        value = dot32(wide_left(scaled_ref[...]), wide_right(a_ref[here, c - offset:d - offset]), NN)
        right_ref[:, c:d] = wide_right(value)

    def make_left():
        value = dot32(wide_left(a_ref[rest, here]), wide_across(lower_ref[...]), NT)
        left_ref[low:, :] = wide_left(value)

    def update(c, d):
        a_ref[rest, c - offset:d - offset] -= dot32(left_ref[low:, :], right_ref[:, c:d], NN)

    def place(c, d):
        a_ref[here, c - offset:d - offset] = dot32(wide_left(lower_ref[...].T), right_ref[:, c:d], NN)

    ranges = spans(low, kept)
    tasks = [functools.partial(make_w, c, d) for c, d in ranges] + [make_left]
    tasks += [functools.partial(update, c, d) for c, d in ranges]
    return tasks + [functools.partial(place, c, d) for c, d in ranges]


def panel(p, state, factors_ref, beside):
    a_ref, offset, next_ref = state[:3]
    at = p * PANEL - offset
    here, after = slice(at, at + PANEL), slice(at + PANEL, at + 2 * PANEL)
    lower, scaled = factor_panel(next_ref[...], beside)
    left = dot32(wide_left(a_ref[after, here]), wide_across(lower), NT)
    right = dot32(wide_left(scaled), wide_right(a_ref[here, after]), NN)
    next_ref[...] = a_ref[after, after] - dot32(wide_left(left), wide_right(right), NN)
    factors_ref[0] = lower
    factors_ref[1] = scaled


def factors_shape(count):
    return jax.ShapeDtypeStruct((count, 2, PANEL, PANEL), jnp.float32)


def work_scratch(kept):
    return [
        pltpu.VMEM((8, kept), jnp.float32),
        pltpu.VMEM((kept, 6 * PANEL), jnp.bfloat16),
        pltpu.VMEM((6 * PANEL, kept), jnp.bfloat16),
    ]


def flat(pieces):
    return [part for piece in pieces for part in (piece if isinstance(piece, tuple) else (piece,))]


def place_pieces(pieces, refs, side, all_ref, sem):
    refs = list(refs)
    moves = []
    at = 0
    for piece in pieces:
        if isinstance(piece, tuple):
            width = piece[0].shape[1]
            cols = pl.ds(at, width)
            half = piece[0].shape[0] - EXTRA
            mine, other = refs.pop(0), refs.pop(0)
            low = pl.multiple_of(side * half, half)
            high = pl.multiple_of((1 - side) * half, half)
            moves.append((mine.at[:half, :], all_ref.at[pl.ds(low, half), cols]))
            moves.append((other.at[:half, :], all_ref.at[pl.ds(high, half), cols]))
            moves.append((mine.at[half:, :], all_ref.at[pl.ds(2 * half, EXTRA), cols]))
        else:
            width = piece.shape[1]
            moves.append((refs.pop(0), all_ref.at[:, pl.ds(at, width)]))
        at += width
    copies = [pltpu.make_async_copy(a, b, sem.at[k]) for k, (a, b) in enumerate(moves)]
    for copy in copies:
        copy.start()
    return copies


def piece_scratch(pieces, kept):
    tokens = sum((piece[0] if isinstance(piece, tuple) else piece).shape[1] for piece in pieces)
    return pltpu.VMEM((kept + EXTRA, tokens), jnp.bfloat16), pltpu.SemaphoreType.DMA((3 * len(pieces),))


def gram_columns(all_ref, kept, at, tile):
    tokens = all_ref.shape[1]
    acc = None
    for c in range(0, tokens, 2048):
        d = min(c + 2048, tokens)
        part = dot32(all_ref[:kept, c:d], all_ref[at:at + tile, c:d], NT)
        acc = part if acc is None else acc + part
    return acc


def square_sum(all_ref, kept, rows):
    total = jnp.float32(0.0)
    for k in range(0, all_ref.shape[1], rows):
        total = total + jnp.sum(all_ref[kept:, k:k + 1].astype(jnp.float32))
    return total


def early_gram(pieces):
    kept_extra, rows = pieces[0].shape
    kept = kept_extra - EXTRA
    count = len(pieces)
    scratch = piece_scratch(pieces, kept)

    def body(*refs):
        out_ref, squares_ref, all_ref, sem = refs[count:]
        for copy in place_pieces(pieces, refs[:count], 0, all_ref, sem):
            copy.wait()
        squares_ref[...] = jnp.full(squares_ref.shape, square_sum(all_ref, kept, rows), jnp.float32)
        for at in range(0, kept, 256):
            out_ref[:, at:at + 256] = gram_columns(all_ref, kept, at, 256)

    return pl.pallas_call(
        body,
        out_shape=[
            jax.ShapeDtypeStruct((kept, kept), jnp.float32),
            jax.ShapeDtypeStruct((8, 128), jnp.float32),
        ],
        in_specs=[pl.BlockSpec(memory_space=pl.ANY)] * count,
        out_specs=[pl.BlockSpec(memory_space=pltpu.VMEM)] * 2,
        scratch_shapes=list(scratch),
        compiler_params=pltpu.CompilerParams(vmem_limit_bytes=VMEM_LIMIT),
        name="early_gram",
    )(*pieces)


def first_kernel(features, rows, last, early_ref, squares_ref, *refs):
    a_ref, scale_ref, factors_ref, next_ref, all_ref, w_ref, left_ref, right_ref = refs[-8:]
    kept = a_ref.shape[0]
    total = squares_ref[...] + square_sum(all_ref, kept, rows)
    scale_ref[...] = 1.0 / (0.01 * total / features)
    scale = scale_ref[0:1, 0:1]

    def gram(at, tile):
        row = lax.broadcasted_iota(jnp.int32, (kept, tile), 0)
        lane = lax.broadcasted_iota(jnp.int32, (kept, tile), 1)
        value = early_ref[:, at:at + tile] + gram_columns(all_ref, kept, at, tile)
        a_ref[:, at:at + tile] = value * scale + jnp.where(row == lane + at, 1.0, 0.0)

    gram(0, 256)
    next_ref[...] = a_ref[:PANEL, :PANEL]
    state = (a_ref, 0, next_ref, w_ref, left_ref, right_ref)
    for p in range(last):
        if p:
            tasks = settle_tasks(p - 1, state, factors_ref.at[p - 1, 0], factors_ref.at[p - 1, 1])
        else:
            tasks = [functools.partial(gram, at, 256) for at in range(256, kept, 256)]
        panel(p, state, factors_ref.at[p], tasks)


def first_part(side, early, squares, pieces, rows, features, last):
    kept = early.shape[0]
    count = len(flat(pieces))
    all_scratch, sem_scratch = piece_scratch(pieces, kept)
    vmem = pl.BlockSpec(memory_space=pltpu.VMEM)

    def body(*refs):
        side_ref, refs, sem = refs[0], refs[1:-1], refs[-1]
        for copy in place_pieces(pieces, refs[2:count + 2], side_ref[0], refs[count + 6], sem):
            copy.wait()
        first_kernel(float(features), rows, last, *refs)

    return pl.pallas_call(
        body,
        out_shape=[
            jax.ShapeDtypeStruct((kept, kept), jnp.float32),
            jax.ShapeDtypeStruct((8, 128), jnp.float32),
            factors_shape(last),
            jax.ShapeDtypeStruct((PANEL, PANEL), jnp.float32),
        ],
        in_specs=[pl.BlockSpec(memory_space=pltpu.SMEM)] + [vmem] * 2 + [pl.BlockSpec(memory_space=pl.ANY)] * count,
        out_specs=[vmem] * 4,
        scratch_shapes=[
            all_scratch,
            *work_scratch(kept),
            sem_scratch,
        ],
        compiler_params=pltpu.CompilerParams(vmem_limit_bytes=VMEM_LIMIT),
        name="gram_and_first_panels",
    )(side, early, squares, *flat(pieces))


def dot_small(x, y, dims=NN):
    rows = x.shape[0]
    hi, mid, low = split3(x)
    yhi, ymid, ylow = split3(y)
    first = dot32(jnp.concatenate([hi, mid, low], axis=0), yhi, dims)
    second = dot32(jnp.concatenate([hi, mid], axis=0), ymid, dims)
    third = dot32(hi, ylow, dims)
    small = first[2 * rows:] + second[rows:] + third
    return small + (first[rows:2 * rows] + second[:rows]) + first[:rows]


def middle_kernel(first, last, start_ref, early_ref, start_next_ref, a_ref, factors_ref, next_ref, *work):
    kept = start_ref.shape[0]
    offset = kept - a_ref.shape[0]
    a_ref[...] = start_ref[offset:, offset:]
    next_ref[...] = start_next_ref[...]
    state = (a_ref, offset, next_ref, *work)
    for p in range(first, last):
        source = early_ref.at[p - 1] if p == first else factors_ref.at[p - 1 - first]
        panel(p, state, factors_ref.at[p - first], settle_tasks(p - 1, state, source.at[0], source.at[1]))


def middle_part(a, factors, follow, first, last):
    kept = a.shape[0]
    left = kept - (first - 1) * PANEL
    vmem = pl.BlockSpec(memory_space=pltpu.VMEM)
    return pl.pallas_call(
        functools.partial(middle_kernel, first, last),
        out_shape=[
            jax.ShapeDtypeStruct((left, left), jnp.float32),
            factors_shape(last - first),
            jax.ShapeDtypeStruct((PANEL, PANEL), jnp.float32),
        ],
        in_specs=[vmem] * 3,
        out_specs=[vmem] * 3,
        scratch_shapes=work_scratch(kept),
        compiler_params=pltpu.CompilerParams(vmem_limit_bytes=VMEM_LIMIT),
        name="middle_panels",
    )(a, factors, follow)


def last_kernel(chips, begin, middle, copies, flags_ref, *refs):
    projected, refs = refs[:chips], refs[chips:]
    scale_ref, whole_ref, early_ref, start_ref, mid_ref, start_next_ref = refs[:6]
    out_ref, index_ref, wide_out_ref, all_ref, late_ref, a_ref, next_ref = refs[-10:-3]
    work = refs[-3:]
    own, features = out_ref.shape
    blocks = flags_ref.shape[0]
    width = features // blocks
    per_tile = 128 // width
    kept = whole_ref.shape[0]
    last = kept // PANEL - 1
    at = last * PANEL
    kept_blocks(flags_ref, index_ref)
    wide_out_ref[...] = jnp.zeros((own, features), jnp.float32)
    offset = kept - a_ref.shape[0]
    cut = start_ref.shape[0] - a_ref.shape[0]
    a_ref[...] = start_ref[cut:, cut:]
    next_ref[...] = start_next_ref[...]
    state = (a_ref, offset, next_ref, *work)
    held = {}

    def factor(p):
        source, skip = a_ref, offset
        if p < begin - 1:
            source, skip = whole_ref, 0
        elif p < middle - 1:
            source, skip = start_ref, kept - start_ref.shape[0]
        low = p * PANEL - skip
        return source[low:low + PANEL, low + PANEL:]

    def factors(p):
        if p < begin:
            return early_ref.at[p]
        return mid_ref.at[p - begin] if p < middle else late_ref.at[p - middle]

    def settle(p):
        return settle_tasks(p, state, factors(p).at[0], factors(p).at[1])

    def make_right():
        whole = jnp.concatenate([part[...] for part in projected], axis=1)
        right = dot32(jnp.concatenate(split3(whole), axis=0), all_ref[:kept, :], NT)
        held["right"] = right[:own] + right[own:2 * own] + right[2 * own:]

    def forward(p):
        right = held["right"]
        held["z", p] = right[:, :PANEL]
        held["right"] = right[:, PANEL:] - dot_small(right[:, :PANEL], factor(p))

    def scaled(p):
        held["zd", p] = dot_small(dot_small(held["z", p], factors(p)[0], NT), factors(p)[1])

    def backward(p):
        if p == last:
            row = lax.broadcasted_iota(jnp.int32, (own + PANEL, PANEL), 0)
            lane = lax.broadcasted_iota(jnp.int32, (own + PANEL, PANEL), 1)
            held["back"] = jnp.where(row == lane + own, 1.0, 0.0)
        else:
            base = jnp.concatenate([held["zd", p], jnp.zeros((PANEL, PANEL), jnp.float32)], axis=0)
            value = base - dot_small(held["back"], factor(p), NT)
            held["back"] = jnp.concatenate([value, held["back"]], axis=1)

    for copy in copies:
        copy.wait()
    for p in range(middle, last):
        tasks = settle(p - 1)
        if p == last - 1:
            tasks = [make_right] + [functools.partial(forward, q) for q in range(p - 1)] + tasks
            tasks += [functools.partial(forward, p - 1)] + [functools.partial(scaled, q) for q in range(p)]
        panel(p, state, late_ref.at[p - middle], tasks)
    tasks = settle(last - 1)
    tasks += [functools.partial(forward, last - 1), functools.partial(scaled, last - 1)]
    tasks += [functools.partial(backward, p) for p in reversed(range(last + 1))]
    lower, upper = factor_panel(next_ref[...], tasks)
    tail = dot_small(dot_small(held["right"], lower, NT), upper)
    scale = scale_ref[0:1, 0:1]
    front = held["back"][:own, :at] + dot_small(tail, held["back"][own:, :at])
    answer = [front[:, c:c + PANEL] * scale for c in range(0, at, PANEL)] + [tail * scale]
    place = lax.broadcasted_iota(jnp.int32, (own, 128), 1) // width
    for i in range(KEEP_BLK):
        b = index_ref[i]
        start = pl.multiple_of((b // per_tile) * 128, 128)
        inner = b % per_tile
        source = answer[i // per_tile]
        moved = pltpu.roll(source, width, 1)
        value = jnp.where(inner == i % per_tile, source, moved)
        old = wide_out_ref[:, pl.ds(start, 128)]
        wide_out_ref[:, pl.ds(start, 128)] = jnp.where(place == inner, value, old)
    out_ref[...] = wide_out_ref[...].astype(jnp.bfloat16)


def last_part(keep_flags, side, projected, begun, pieces, features, begin, middle):
    own = projected[0].shape[0]
    blocks = keep_flags.shape[0]
    chips = len(projected)
    kept = begun[1].shape[0]
    count = len(flat(pieces))
    all_scratch, sem_scratch = piece_scratch(pieces, kept)
    left = kept - (middle - 1) * PANEL
    vmem = pl.BlockSpec(memory_space=pltpu.VMEM)
    anywhere = pl.BlockSpec(memory_space=pl.ANY)

    def body(*refs):
        refs, sem = refs[:-1], refs[-1]
        side_ref, refs = refs[0], refs[1:]
        ins = 1 + chips + len(begun)
        copies = place_pieces(pieces, refs[ins:ins + count], side_ref[0], refs[ins + count + 3], sem)
        last_kernel(chips, begin, middle, copies, *refs)

    return pl.pallas_call(
        body,
        out_shape=jax.ShapeDtypeStruct((own, features), jnp.bfloat16),
        in_specs=[pl.BlockSpec(memory_space=pltpu.SMEM)] * 2 + [vmem] * (chips + len(begun)) + [anywhere] * count,
        out_specs=vmem,
        scratch_shapes=[
            pltpu.SMEM((blocks + 1,), jnp.int32),
            pltpu.VMEM((own, features), jnp.float32),
            all_scratch,
            pltpu.VMEM((kept // PANEL - 1 - middle, 2, PANEL, PANEL), jnp.float32),
            pltpu.VMEM((left, left), jnp.float32),
            pltpu.VMEM((PANEL, PANEL), jnp.float32),
            *work_scratch(kept),
            sem_scratch,
        ],
        compiler_params=pltpu.CompilerParams(vmem_limit_bytes=VMEM_LIMIT),
        name="last_panels_and_solution",
    )(side, keep_flags, *projected, *begun, *flat(pieces))


def solution(mesh):
    n = mesh.shape["dp"]
    others = range(2, n, 2)

    def swap(x, k):
        return lax.ppermute(x, "dp", [(d, d ^ k) for d in range(n)])

    def level(x):
        return lax.ppermute(x, "section", [(d, d ^ 1) for d in range(mesh.shape["section"])])

    def gather_kept(kept, half):
        if n != 8 or mesh.shape["section"] % 2:
            same = [kept] + [swap(kept, k) for k in others]
            pieces = [part for piece in same for part in (piece, swap(piece, 1))]
            return pieces, early_gram(pieces[:2]), same[-1]
        far = swap(half, 6)
        near = [swap(kept, 2), swap(kept, 4)]
        sibling = swap(kept, 1)
        other = level(far)
        far_sibling = swap(far, 1)
        early = early_gram([kept, sibling])
        near, early, far_sibling = lax.optimization_barrier((near, early, far_sibling))
        near_sibling = [swap(piece, 1) for piece in near]
        other_sibling = swap(other, 1)
        pieces = [kept, sibling, near[0], near_sibling[0], near[1], near_sibling[1]]
        return pieces + [(far, other), (far_sibling, other_sibling)], early, near

    def on_device(tokens, orig_weight, keep_flags):
        features = tokens.shape[1]
        own = orig_weight.shape[0]
        rows = tokens.shape[0]
        side = jnp.full((1,), lax.axis_index("section") % 2, jnp.int32)
        kept, half = select_kept(side, tokens, keep_flags)
        panels = (kept.shape[0] - EXTRA) // PANEL
        begin = panels // 2
        middle = begin + 1
        tokens, kept = lax.optimization_barrier((tokens, kept))
        pieces, early, arrived = gather_kept(kept, half)
        orig_weight, arrived = lax.optimization_barrier((orig_weight, arrived))
        sibling = swap(tokens, 1)
        weights = [orig_weight] + [swap(orig_weight, k) for k in others]
        a, scale, factors, follow = first_part(side, *early, pieces[2:], rows, features, begin)
        a, weights, sibling = lax.optimization_barrier((a, weights, sibling))
        stacked = jnp.concatenate(weights, axis=0)
        projected = [
            lax.dot_general(stacked, part, NT, preferred_element_type=jnp.float32) for part in (tokens, sibling)
        ]
        projected, a = lax.optimization_barrier((jnp.concatenate(projected, axis=1), a))
        parts = [projected[i * own:(i + 1) * own] for i in range(n // 2)]
        parts = [parts[0]] + [swap(part, k) for part, k in zip(parts[1:], others)]
        rest, more, follow = middle_part(a, factors, follow, begin, middle)
        begun = (scale, a, factors, rest, more, follow)
        return last_part(keep_flags, side, parts, begun, pieces, features, begin, middle)

    in_specs = (P("dp", None), P(("section", "dp"), None), P())
    out_specs = P(("section", "dp"), None)
    return jax.shard_map(on_device, mesh=mesh, in_specs=in_specs, out_specs=out_specs, check_vma=False)
```

profile of v0, /device:TPU:0, one launch (start us, length us, event | category | flops | bytes accessed | tf_op | source)
XLA Modules:
  0.0 60.6 jit_solution(5427645982357480421)
XLA Ops:
  0.0 0.0 copy-start
  0.0 0.7 %copy-done = s32[64]{0:T(128)S(1)} copy-done((s32[64]{0:T(128)S(1)}, s32[64]{0:T(128)}, u32[]{:S(2)}) %copy-start) | copy-done | bytes 280
  0.7 0.0 copy-start.2
  0.7 2.4 %select_kept.1 = (bf16[784,256]{1,0:T(8,128)(2,1)S(1)}, bf16[400,256]{1,0:T(8,128)(2,1)S(1)}) custom-call(s32[1]{0:T(128)} %bitcast.side_ref.refs_0_, s32[64]{0:T(128)S(1)} %copy-done, bf16[256,4096]{1,0:T(8,128)(2,1)} %tokens_ref.1), custom_call_target="tpu_custom_call" | custom-call | tf_op jit(solution)/shard_map/select_kept/pallas_call | solution.py:90
  3.1 0.5 collective-permute-start.12
  3.6 3.5 %collective-permute-start.3 = (bf16[400,256]{1,0:T(8,128)(2,1)S(1)}, bf16[400,256]{1,0:T(8,128)(2,1)S(1)}, u32[]{:S(2)}, u32[]{:S(2)}) collective-permute-start(bf16[400,256]{1,0:T(8,128)(2,1)S(1)} %get-tuple-element.36), channel_id=1, source_target_pairs={{0,6},{1,7},{2,4},{3,5},{4,2},{5,3},{6,0},{7,1},{8,14},{9,15},{10,... | collective-permute-start | bytes 614408 | tf_op jit(solution)/shard_map/ppermute | solution.py:588
  7.1 0.2 collective-permute-start.2
  7.3 0.5 collective-permute-start
  7.8 0.3 collective-permute-start.1
  8.1 5.0 %collective-permute-done.3.refs_7_.refs_18_ = bf16[400,256]{1,0:T(8,128)(2,1)S(1)} collective-permute-done((bf16[400,256]{1,0:T(8,128)(2,1)S(1)}, bf16[400,256]{1,0:T(8,128)(2,1)S(1)}, u32[]{:S(2)}, u32[]{:S(2)}) %collective-permute-start.3) | collective-permute-done | bytes 204832 | tf_op jit(solution)/shard_map/ppermute | solution.py:588
  13.1 0.0 collective-permute-start.4
  13.1 0.0 collective-permute-done.2.refs_1_.refs_13_
  13.1 2.0 %collective-permute-start.7 = (bf16[400,256]{1,0:T(8,128)(2,1)S(1)}, bf16[400,256]{1,0:T(8,128)(2,1)S(1)}, u32[]{:S(2)}, u32[]{:S(2)}) collective-permute-start(bf16[400,256]{1,0:T(8,128)(2,1)S(1)} %collective-permute-done.3.refs_7_.refs_18_), channel_id=1, source_target_pairs={{0,8},{8,0},{16,24},{24,16},{1,9},{9,1},{17,25},{25,17},{2,10},{10... | collective-permute-start | bytes 614408 | tf_op jit(solution)/shard_map/ppermute | solution.py:591
  15.1 0.9 %early_gram.1 = (f32[768,768]{1,0:T(8,128)S(1)}, f32[8,128]{1,0:T(8,128)S(1)}) custom-call(bf16[784,256]{1,0:T(8,128)(2,1)S(1)} %get-tuple-element.33.refs_0_.refs_12_, bf16[784,256]{1,0:T(8,128)(2,1)S(1)} %collective-permute-done.2.refs_1_.refs_13_), custom_call_target="tpu_custom_call" | custom-call | tf_op jit(solution)/shard_map/early_gram/pallas_call | solution.py:344
  16.0 5.7 %collective-permute-done.refs_3_.refs_14_ = bf16[784,256]{1,0:T(8,128)(2,1)S(1)} collective-permute-done((bf16[784,256]{1,0:T(8,128)(2,1)S(1)}, bf16[784,256]{1,0:T(8,128)(2,1)S(1)}, u32[]{:S(2)}, u32[]{:S(2)}) %collective-permute-start) | collective-permute-done | bytes 401440 | tf_op jit(solution)/shard_map/ppermute | solution.py:588
  21.7 0.0 collective-permute-done.1.refs_5_.refs_16_
  21.7 0.0 collective-permute-done.4.refs_9_.refs_20_
  21.7 0.0 collective-permute-start.5
  21.7 0.0 collective-permute-done.7.refs_8_.refs_19_
  21.7 0.5 collective-permute-start.8
  22.2 0.1 collective-permute-start.6
  22.3 0.0 copy-done.2
  22.3 1.4 %collective-permute-start.10 = (bf16[32,4096]{1,0:T(8,128)(2,1)S(1)}, bf16[32,4096]{1,0:T(8,128)(2,1)S(1)}, u32[]{:S(2)}, u32[]{:S(2)}) collective-permute-start(bf16[32,4096]{1,0:T(8,128)(2,1)S(1)} %copy-done.2), channel_id=1, source_target_pairs={{0,4},{1,5},{2,6},{3,7},{4,0},{5,1},{6,2},{7,3},{8,12},{9,13},{10,... | collective-permute-start | bytes 786440 | tf_op jit(solution)/shard_map/ppermute | solution.py:588
  23.7 0.0 collective-permute-done.8.refs_10_.refs_21_
  23.7 2.3 %collective-permute-start.11 = (bf16[32,4096]{1,0:T(8,128)(2,1)S(1)}, bf16[32,4096]{1,0:T(8,128)(2,1)S(1)}, u32[]{:S(2)}, u32[]{:S(2)}) collective-permute-start(bf16[32,4096]{1,0:T(8,128)(2,1)S(1)} %copy-done.2), channel_id=1, source_target_pairs={{0,6},{1,7},{2,4},{3,5},{4,2},{5,3},{6,0},{7,1},{8,14},{9,15},{10,... | collective-permute-start | bytes 786440 | tf_op jit(solution)/shard_map/ppermute | solution.py:588
  26.1 0.0 collective-permute-done.5.refs_4_.refs_15_
  26.1 0.5 collective-permute-start.9
  26.6 0.0 collective-permute-done.6.refs_6_.refs_17_
  26.6 12.5 %gram_and_first_panels.1 = (f32[768,768]{1,0:T(8,128)S(1)}, f32[8,128]{1,0:T(8,128)S(1)}, f32[3,2,128,128]{3,2,1,0:T(8,128)S(1)}, f32[128,128]{1,0:T(8,128)S(1)}) custom-call(s32[1]{0:T(128)} %bitcast.side_ref.refs_0_, f32[768,768]{1,0:T(8,128)S(1)} %get-tuple-element.37.refs_1_, f32[8,128]{1,0:T(8,128)S(1)} %get-tuple-element.38.refs_2_, ...), custom_call_target="tpu_custom_call" | custom-call | tf_op jit(solution)/shard_map/gram_and_first_panels/pallas_call | solution.py:394
  39.1 0.0 collective-permute-done.10
  39.1 0.0 collective-permute-done.11
  39.1 0.0 collective-permute-done.9
  39.1 0.0 collective-permute-done.12
  39.3 2.4 %fusion.1 = f32[128,256]{1,0:T(8,128)S(1)} fusion(bf16[128,4096]{1,0:T(8,128)(2,1)S(1)} %constant_dynamic-update-slice_fusion, bf16[256,4096]{1,0:T(8,128)(2,1)} %tokens_ref.1), kind=kOutput, calls=%fused_computation.6 | convolution fusion | flops 268435456 | bytes 3276800 | tf_op jit(solution)/shard_map/dot_general | solution.py:628
  41.7 0.8 %fusion.2 = f32[128,256]{1,0:T(8,128)S(1)} fusion(bf16[128,4096]{1,0:T(8,128)(2,1)S(1)} %constant_dynamic-update-slice_fusion, bf16[256,4096]{1,0:T(8,128)(2,1)S(1)} %collective-permute-done.12), kind=kOutput, calls=%fused_computation.7 | convolution fusion | flops 268435456 | bytes 3276800 | tf_op jit(solution)/shard_map/dot_general | solution.py:628
  42.5 0.0 copy-start.1
  42.6 1.5 %collective-permute-start.13 = (f32[32,512]{1,0:T(8,128)S(1)}, f32[32,512]{1,0:T(8,128)S(1)}, u32[]{:S(2)}, u32[]{:S(2)}) collective-permute-start(f32[32,512]{1,0:T(8,128)S(1)} %get-tuple-element.61), channel_id=1, source_target_pairs={{0,2},{1,3},{2,0},{3,1},{4,6},{5,7},{6,4},{7,5},{8,10},{9,11},{10,... | collective-permute-start | bytes 196616 | tf_op jit(solution)/shard_map/ppermute | solution.py:588
  44.1 0.6 %collective-permute-start.14 = (f32[32,512]{1,0:T(8,128)S(1)}, f32[32,512]{1,0:T(8,128)S(1)}, u32[]{:S(2)}, u32[]{:S(2)}) collective-permute-start(f32[32,512]{1,0:T(8,128)S(1)} %get-tuple-element.60), channel_id=1, source_target_pairs={{0,4},{1,5},{2,6},{3,7},{4,0},{5,1},{6,2},{7,3},{8,12},{9,13},{10,... | collective-permute-start | bytes 196616 | tf_op jit(solution)/shard_map/ppermute | solution.py:588
  44.8 1.4 %collective-permute-start.15 = (f32[32,512]{1,0:T(8,128)S(1)}, f32[32,512]{1,0:T(8,128)S(1)}, u32[]{:S(2)}, u32[]{:S(2)}) collective-permute-start(f32[32,512]{1,0:T(8,128)S(1)} %get-tuple-element.59), channel_id=1, source_target_pairs={{0,6},{1,7},{2,4},{3,5},{4,2},{5,3},{6,0},{7,1},{8,14},{9,15},{10,... | collective-permute-start | bytes 196616 | tf_op jit(solution)/shard_map/ppermute | solution.py:588
  46.2 4.1 %middle_panels.1 = (f32[512,512]{1,0:T(8,128)S(1)}, f32[1,2,128,128]{3,2,1,0:T(8,128)S(1)}, f32[128,128]{1,0:T(8,128)S(1)}) custom-call(f32[768,768]{1,0:T(8,128)S(1)} %get-tuple-element.53.start_ref.refs_7_, f32[3,2,128,128]{3,2,1,0:T(8,128)S(1)} %get-tuple-element.54.early_ref.refs_8_, f32[128,128]{1,0:T(8,128)S(1)} %get-tuple-element.55.start_next_ref), custom_call_target="tpu_custom_call" | custom-call | tf_op jit(solution)/shard_map/middle_panels/pallas_call | solution.py:440
  50.3 0.0 collective-permute-done.13.refs_3_
  50.3 0.0 collective-permute-done.14.refs_4_
  50.3 0.0 collective-permute-done.15.refs_5_
  50.3 0.0 copy-done.1
  50.3 10.1 %last_panels_and_solution.1 = bf16[32,4096]{1,0:T(8,128)(2,1)} custom-call(s32[1]{0:T(128)} %bitcast.side_ref.refs_0_, s32[64]{0:T(128)S(1)} %copy-done.1, f32[32,512]{1,0:T(8,128)S(1)} %get-tuple-element.62.refs_2_, f32[32,512]{1,0:T(8,128)S(1)} %collective-permute-done.13.refs_3_, f32[32,512]{1,0:T(8,128)S(1)} %collective-permute-done.14.refs_4_, ...), custom_call_target="tpu_custom_call" | custom-call | tf_op jit(solution)/shard_map/last_panels_and_solution/pallas_call | solution.py:563
  (6 shorter events, 0.1 us)
Async XLA Ops:
  0.0 0.7 %copy-start = (s32[64]{0:T(128)S(1)}, s32[64]{0:T(128)}, u32[]{:S(2)}) copy-start(s32[64]{0:T(128)} %refs_1_.1) | copy-start | bytes 772
  0.7 21.6 %copy-start.2 = (bf16[32,4096]{1,0:T(8,128)(2,1)S(1)}, bf16[32,4096]{1,0:T(8,128)(2,1)}, u32[]{:S(2)}) copy-start(bf16[32,4096]{1,0:T(8,128)(2,1)} %param.4) | copy-start | bytes 786436
  3.1 36.1 %collective-permute-start.12 = (bf16[256,4096]{1,0:T(8,128)(2,1)}, bf16[256,4096]{1,0:T(8,128)(2,1)S(1)}, u32[]{:S(2)}, u32[]{:S(2)}) collective-permute-start(bf16[256,4096]{1,0:T(8,128)(2,1)} %tokens_ref.1), channel_id=1, source_target_pairs={{0,1},{1,0},{2,3},{3,2},{4,5},{5,4},{6,7},{7,6},{8,9},{9,8},{10,11... | collective-permute-start | bytes 6291464 | tf_op jit(solution)/shard_map/ppermute | solution.py:588
  3.6 9.5 %collective-permute-start.3 = (bf16[400,256]{1,0:T(8,128)(2,1)S(1)}, bf16[400,256]{1,0:T(8,128)(2,1)S(1)}, u32[]{:S(2)}, u32[]{:S(2)}) collective-permute-start(bf16[400,256]{1,0:T(8,128)(2,1)S(1)} %get-tuple-element.36), channel_id=1, source_target_pairs={{0,6},{1,7},{2,4},{3,5},{4,2},{5,3},{6,0},{7,1},{8,14},{9,15},{10,... | collective-permute-start | bytes 614408 | tf_op jit(solution)/shard_map/ppermute | solution.py:588
  7.1 6.0 %collective-permute-start.2 = (bf16[784,256]{1,0:T(8,128)(2,1)S(1)}, bf16[784,256]{1,0:T(8,128)(2,1)S(1)}, u32[]{:S(2)}, u32[]{:S(2)}) collective-permute-start(bf16[784,256]{1,0:T(8,128)(2,1)S(1)} %get-tuple-element.33.refs_0_.refs_12_), channel_id=1, source_target_pairs={{0,1},{1,0},{2,3},{3,2},{4,5},{5,4},{6,7},{7,6},{8,9},{9,8},{10,11... | collective-permute-start | bytes 1204232 | tf_op jit(solution)/shard_map/ppermute | solution.py:588
  7.3 14.4 %collective-permute-start = (bf16[784,256]{1,0:T(8,128)(2,1)S(1)}, bf16[784,256]{1,0:T(8,128)(2,1)S(1)}, u32[]{:S(2)}, u32[]{:S(2)}) collective-permute-start(bf16[784,256]{1,0:T(8,128)(2,1)S(1)} %get-tuple-element.33.refs_0_.refs_12_), channel_id=1, source_target_pairs={{0,2},{1,3},{2,0},{3,1},{4,6},{5,7},{6,4},{7,5},{8,10},{9,11},{10,... | collective-permute-start | bytes 1204232 | tf_op jit(solution)/shard_map/ppermute | solution.py:588
  7.8 13.9 %collective-permute-start.1 = (bf16[784,256]{1,0:T(8,128)(2,1)S(1)}, bf16[784,256]{1,0:T(8,128)(2,1)S(1)}, u32[]{:S(2)}, u32[]{:S(2)}) collective-permute-start(bf16[784,256]{1,0:T(8,128)(2,1)S(1)} %get-tuple-element.33.refs_0_.refs_12_), channel_id=1, source_target_pairs={{0,4},{1,5},{2,6},{3,7},{4,0},{5,1},{6,2},{7,3},{8,12},{9,13},{10,... | collective-permute-start | bytes 1204232 | tf_op jit(solution)/shard_map/ppermute | solution.py:588
  13.1 8.6 %collective-permute-start.4 = (bf16[400,256]{1,0:T(8,128)(2,1)S(1)}, bf16[400,256]{1,0:T(8,128)(2,1)S(1)}, u32[]{:S(2)}, u32[]{:S(2)}) collective-permute-start(bf16[400,256]{1,0:T(8,128)(2,1)S(1)} %collective-permute-done.3.refs_7_.refs_18_), channel_id=1, source_target_pairs={{0,1},{1,0},{2,3},{3,2},{4,5},{5,4},{6,7},{7,6},{8,9},{9,8},{10,11... | collective-permute-start | bytes 614408 | tf_op jit(solution)/shard_map/ppermute | solution.py:588
  13.1 8.6 %collective-permute-start.7 = (bf16[400,256]{1,0:T(8,128)(2,1)S(1)}, bf16[400,256]{1,0:T(8,128)(2,1)S(1)}, u32[]{:S(2)}, u32[]{:S(2)}) collective-permute-start(bf16[400,256]{1,0:T(8,128)(2,1)S(1)} %collective-permute-done.3.refs_7_.refs_18_), channel_id=1, source_target_pairs={{0,8},{8,0},{16,24},{24,16},{1,9},{9,1},{17,25},{25,17},{2,10},{10... | collective-permute-start | bytes 614408 | tf_op jit(solution)/shard_map/ppermute | solution.py:591
  21.7 4.4 %collective-permute-start.5 = (bf16[784,256]{1,0:T(8,128)(2,1)S(1)}, bf16[784,256]{1,0:T(8,128)(2,1)S(1)}, u32[]{:S(2)}, u32[]{:S(2)}) collective-permute-start(bf16[784,256]{1,0:T(8,128)(2,1)S(1)} %collective-permute-done.refs_3_.refs_14_), channel_id=1, source_target_pairs={{0,1},{1,0},{2,3},{3,2},{4,5},{5,4},{6,7},{7,6},{8,9},{9,8},{10,11... | collective-permute-start | bytes 1204232 | tf_op jit(solution)/shard_map/ppermute | solution.py:588
  21.7 2.0 %collective-permute-start.8 = (bf16[400,256]{1,0:T(8,128)(2,1)S(1)}, bf16[400,256]{1,0:T(8,128)(2,1)S(1)}, u32[]{:S(2)}, u32[]{:S(2)}) collective-permute-start(bf16[400,256]{1,0:T(8,128)(2,1)S(1)} %collective-permute-done.7.refs_8_.refs_19_), channel_id=1, source_target_pairs={{0,1},{1,0},{2,3},{3,2},{4,5},{5,4},{6,7},{7,6},{8,9},{9,8},{10,11... | collective-permute-start | bytes 614408 | tf_op jit(solution)/shard_map/ppermute | solution.py:588
  22.2 4.4 %collective-permute-start.6 = (bf16[784,256]{1,0:T(8,128)(2,1)S(1)}, bf16[784,256]{1,0:T(8,128)(2,1)S(1)}, u32[]{:S(2)}, u32[]{:S(2)}) collective-permute-start(bf16[784,256]{1,0:T(8,128)(2,1)S(1)} %collective-permute-done.1.refs_5_.refs_16_), channel_id=1, source_target_pairs={{0,1},{1,0},{2,3},{3,2},{4,5},{5,4},{6,7},{7,6},{8,9},{9,8},{10,11... | collective-permute-start | bytes 1204232 | tf_op jit(solution)/shard_map/ppermute | solution.py:588
  22.3 16.8 %collective-permute-start.10 = (bf16[32,4096]{1,0:T(8,128)(2,1)S(1)}, bf16[32,4096]{1,0:T(8,128)(2,1)S(1)}, u32[]{:S(2)}, u32[]{:S(2)}) collective-permute-start(bf16[32,4096]{1,0:T(8,128)(2,1)S(1)} %copy-done.2), channel_id=1, source_target_pairs={{0,4},{1,5},{2,6},{3,7},{4,0},{5,1},{6,2},{7,3},{8,12},{9,13},{10,... | collective-permute-start | bytes 786440 | tf_op jit(solution)/shard_map/ppermute | solution.py:588
  23.7 15.4 %collective-permute-start.11 = (bf16[32,4096]{1,0:T(8,128)(2,1)S(1)}, bf16[32,4096]{1,0:T(8,128)(2,1)S(1)}, u32[]{:S(2)}, u32[]{:S(2)}) collective-permute-start(bf16[32,4096]{1,0:T(8,128)(2,1)S(1)} %copy-done.2), channel_id=1, source_target_pairs={{0,6},{1,7},{2,4},{3,5},{4,2},{5,3},{6,0},{7,1},{8,14},{9,15},{10,... | collective-permute-start | bytes 786440 | tf_op jit(solution)/shard_map/ppermute | solution.py:588
  26.1 13.1 %collective-permute-start.9 = (bf16[32,4096]{1,0:T(8,128)(2,1)S(1)}, bf16[32,4096]{1,0:T(8,128)(2,1)S(1)}, u32[]{:S(2)}, u32[]{:S(2)}) collective-permute-start(bf16[32,4096]{1,0:T(8,128)(2,1)S(1)} %copy-done.2), channel_id=1, source_target_pairs={{0,2},{1,3},{2,0},{3,1},{4,6},{5,7},{6,4},{7,5},{8,10},{9,11},{10,... | collective-permute-start | bytes 786440 | tf_op jit(solution)/shard_map/ppermute | solution.py:588
  42.5 7.8 %copy-start.1 = (s32[64]{0:T(128)S(1)}, s32[64]{0:T(128)}, u32[]{:S(2)}) copy-start(s32[64]{0:T(128)} %refs_1_.1) | copy-start | bytes 772
  42.6 7.7 %collective-permute-start.13 = (f32[32,512]{1,0:T(8,128)S(1)}, f32[32,512]{1,0:T(8,128)S(1)}, u32[]{:S(2)}, u32[]{:S(2)}) collective-permute-start(f32[32,512]{1,0:T(8,128)S(1)} %get-tuple-element.61), channel_id=1, source_target_pairs={{0,2},{1,3},{2,0},{3,1},{4,6},{5,7},{6,4},{7,5},{8,10},{9,11},{10,... | collective-permute-start | bytes 196616 | tf_op jit(solution)/shard_map/ppermute | solution.py:588
  44.1 6.1 %collective-permute-start.14 = (f32[32,512]{1,0:T(8,128)S(1)}, f32[32,512]{1,0:T(8,128)S(1)}, u32[]{:S(2)}, u32[]{:S(2)}) collective-permute-start(f32[32,512]{1,0:T(8,128)S(1)} %get-tuple-element.60), channel_id=1, source_target_pairs={{0,4},{1,5},{2,6},{3,7},{4,0},{5,1},{6,2},{7,3},{8,12},{9,13},{10,... | collective-permute-start | bytes 196616 | tf_op jit(solution)/shard_map/ppermute | solution.py:588
  44.8 5.5 %collective-permute-start.15 = (f32[32,512]{1,0:T(8,128)S(1)}, f32[32,512]{1,0:T(8,128)S(1)}, u32[]{:S(2)}, u32[]{:S(2)}) collective-permute-start(f32[32,512]{1,0:T(8,128)S(1)} %get-tuple-element.59), channel_id=1, source_target_pairs={{0,6},{1,7},{2,4},{3,5},{4,2},{5,3},{6,0},{7,1},{8,14},{9,15},{10,... | collective-permute-start | bytes 196616 | tf_op jit(solution)/shard_map/ppermute | solution.py:588
where the time goes:
time: 60.8 us; the launch traced here: 60.6 us
  Pallas kernels  30 us (49%)
  starting transfers between devices  15.4 us (25%)
  waiting for transfers between devices  10.7 us (18%)
  matrix products  3.26 us (5%)
  local copies, waits for them, and re-layouts  0.76 us (1%)
    ppermute x15, starting transfers between devices, swap(): return lax.ppermute(x, 'dp', [(d, d ^ k) for d in range(n)])  13.5 us
    pallas_call x1, Pallas kernels, first_part(): pl.pallas_call(body, out_shape=[jax.ShapeDtypeStruct((kept, kept), jnp.fl...  12.5 us
    ppermute x15, waiting for transfers between devices, swap(): return lax.ppermute(x, 'dp', [(d, d ^ k) for d in range(n)])  10.7 us
    pallas_call x1, Pallas kernels, last_part(): pl.pallas_call(body, out_shape=jax.ShapeDtypeStruct((own, features), jnp....  10.1 us
    pallas_call x1, Pallas kernels, middle_part(): pl.pallas_call(functools.partial(middle_kernel, first, last), out_shape=[...  4.12 us
    dot_general x2, matrix products, on_device(): lax.dot_general(stacked, part, NT, preferred_element_type=jnp.float32)  3.26 us
    pallas_call x1, Pallas kernels, select_kept(): pl.pallas_call(select_kernel, out_shape=[jax.ShapeDtypeStruct((kept + EXT...  2.39 us
    ppermute x1, starting transfers between devices, level(): lax.ppermute(x, 'section', [(d, d ^ 1) for d in range(mesh.shape['section...  1.97 us
  transfers between devices with their start and end apart: 16, of which 2 were waited for; matrix products, arithmetic and copies ran while one was open for 0% of the time, Pallas kernels for 29%

commit v1 on v0

--- a/solution.py
+++ b/solution.py
@@ -131,8 +131,9 @@
     return entry
 
 
-def solve_small(entry, rows, cross, ahead):
-    entry, rows, cross, ahead = dict(entry), list(rows), list(cross), list(ahead)
+def solve_small(entry, rows, cross, beyond, ahead):
+    entry, rows, ahead = dict(entry), list(rows), list(ahead)
+    cross, beyond = list(cross), list(beyond)
     lower = {}
     for t in range(0, SUB, 2):
         u = t + 1
@@ -151,7 +152,7 @@
                 entry[i, j] = partial - (rest[i] * rest[j]) * second
         for j in later:
             lower[j, u] = rest[j] * second
-        for part in (cross, rows):
+        for part in (cross, beyond, rows):
             if part:
                 part[u] = part[u] - lower[u, t] * part[t]
                 for j in later:
@@ -163,10 +164,11 @@
         rows[t] = rows[t] * first
         rows[u] = rows[u] * second
     following = {(i, j): sublane_row(ahead[j], i) for j in range(SUB) for i in range(j + 1) if cross}
+    forward = list(rows)
     for t in reversed(range(SUB)):
         for j in range(t):
             rows[j] = rows[j] - lower[t, j] * rows[t]
-    return rows, following
+    return rows, forward, cross, beyond, following
 
 
 def factor_panel(block, beside=()):
@@ -181,15 +183,21 @@
     for s in range(count):
         base = s * SUB
         inside = (lane >= base) & (lane < base + SUB)
-        cross, ahead = [], []
+        cross, beyond, ahead = [], [], []
+        if s + 2 < count:
+            beyond = [lane_column(rows[s + 2], base + j) for j in range(SUB)]
         if s + 1 < count:
             cross = [lane_column(rows[s + 1], base + j) for j in range(SUB)]
             ahead = [lane_column(rows[s + 1], base + SUB + j) for j in range(SUB)]
         pivot_rows = jnp.where(inside, jnp.where(lane == sub + base, 1.0, 0.0), rows[s])
-        spread, entry = solve_small(entry, [sublane_row(pivot_rows, j) for j in range(SUB)], cross, ahead)
+        spread_in = [sublane_row(pivot_rows, j) for j in range(SUB)]
+        spread, forward, cross, beyond, entry = solve_small(entry, spread_in, cross, beyond, ahead)
         for i in range(s + 1, count):
-            columns = cross if i == s + 1 else [lane_column(rows[i], base + j) for j in range(SUB)]
-            change = tree_sum([columns[j] * spread[j] for j in range(SUB)])
+            if i <= s + 2:
+                columns, lines = (cross if i == s + 1 else beyond), forward
+            else:
+                columns, lines = [lane_column(rows[i], base + j) for j in range(SUB)], spread
+            change = tree_sum([columns[j] * lines[j] for j in range(SUB)])
             rows[i] = jnp.where(inside, 0.0, rows[i]) - change
         new = spread[SUB - 1]
         for j in range(SUB - 1):
@@ -327,32 +335,37 @@
     return total
 
 
-def early_gram(pieces):
+def early_gram(pieces, source):
     kept_extra, rows = pieces[0].shape
     kept = kept_extra - EXTRA
     count = len(pieces)
     scratch = piece_scratch(pieces, kept)
 
     def body(*refs):
-        out_ref, squares_ref, all_ref, sem = refs[count:]
-        for copy in place_pieces(pieces, refs[:count], 0, all_ref, sem):
+        source_ref, out_ref, squares_ref, held_ref, all_ref, sem, held_sem = refs[count:]
+        copies = place_pieces(pieces, refs[:count], 0, all_ref, sem)
+        fetch = pltpu.make_async_copy(source_ref, held_ref, held_sem)
+        fetch.start()
+        for copy in copies:
             copy.wait()
         squares_ref[...] = jnp.full(squares_ref.shape, square_sum(all_ref, kept, rows), jnp.float32)
         for at in range(0, kept, 256):
             out_ref[:, at:at + 256] = gram_columns(all_ref, kept, at, 256)
+        fetch.wait()
 
     return pl.pallas_call(
         body,
         out_shape=[
             jax.ShapeDtypeStruct((kept, kept), jnp.float32),
             jax.ShapeDtypeStruct((8, 128), jnp.float32),
+            jax.ShapeDtypeStruct(source.shape, source.dtype),
         ],
-        in_specs=[pl.BlockSpec(memory_space=pl.ANY)] * count,
-        out_specs=[pl.BlockSpec(memory_space=pltpu.VMEM)] * 2,
-        scratch_shapes=list(scratch),
+        in_specs=[pl.BlockSpec(memory_space=pl.ANY)] * (count + 1),
+        out_specs=[pl.BlockSpec(memory_space=pltpu.VMEM)] * 3,
+        scratch_shapes=[*scratch, pltpu.SemaphoreType.DMA],
         compiler_params=pltpu.CompilerParams(vmem_limit_bytes=VMEM_LIMIT),
         name="early_gram",
-    )(*pieces)
+    )(*pieces, source)
 
 
 def first_kernel(features, rows, last, early_ref, squares_ref, *refs):
@@ -368,14 +381,17 @@
         value = early_ref[:, at:at + tile] + gram_columns(all_ref, kept, at, tile)
         a_ref[:, at:at + tile] = value * scale + jnp.where(row == lane + at, 1.0, 0.0)
 
-    gram(0, 256)
-    next_ref[...] = a_ref[:PANEL, :PANEL]
+    block = slice(0, PANEL)
+    corner = early_ref[block, block] + dot32(all_ref[block, :], all_ref[block, :], NT)
+    row = lax.broadcasted_iota(jnp.int32, (PANEL, PANEL), 0)
+    lane = lax.broadcasted_iota(jnp.int32, (PANEL, PANEL), 1)
+    next_ref[...] = corner * scale + jnp.where(row == lane, 1.0, 0.0)
     state = (a_ref, 0, next_ref, w_ref, left_ref, right_ref)
     for p in range(last):
         if p:
             tasks = settle_tasks(p - 1, state, factors_ref.at[p - 1, 0], factors_ref.at[p - 1, 1])
         else:
-            tasks = [functools.partial(gram, at, 256) for at in range(256, kept, 256)]
+            tasks = [functools.partial(gram, at, 256) for at in range(0, kept, 256)]
         panel(p, state, factors_ref.at[p], tasks)
 
 
@@ -513,13 +529,15 @@
             value = base - dot_small(held["back"], factor(p), NT)
             held["back"] = jnp.concatenate([value, held["back"]], axis=1)
 
-    for copy in copies:
-        copy.wait()
+    def await_pieces():
+        for copy in copies:
+            copy.wait()
+
     for p in range(middle, last):
         tasks = settle(p - 1)
         if p == last - 1:
-            tasks = [make_right] + [functools.partial(forward, q) for q in range(p - 1)] + tasks
-            tasks += [functools.partial(forward, p - 1)] + [functools.partial(scaled, q) for q in range(p)]
+            tasks += [await_pieces, make_right] + [functools.partial(forward, q) for q in range(p)]
+            tasks += [functools.partial(scaled, q) for q in range(p)]
         panel(p, state, late_ref.at[p - middle], tasks)
     tasks = settle(last - 1)
     tasks += [functools.partial(forward, last - 1), functools.partial(scaled, last - 1)]
@@ -590,22 +608,25 @@
     def level(x):
         return lax.ppermute(x, "section", [(d, d ^ 1) for d in range(mesh.shape["section"])])
 
-    def gather_kept(kept, half):
+    def gather_kept(kept, half, tokens):
         if n != 8 or mesh.shape["section"] % 2:
             same = [kept] + [swap(kept, k) for k in others]
             pieces = [part for piece in same for part in (piece, swap(piece, 1))]
-            return pieces, early_gram(pieces[:2]), same[-1]
+            *early, held = early_gram(pieces[:2], tokens)
+            return pieces, early, same[-1], held, swap(tokens, 1)
         far = swap(half, 6)
         near = [swap(kept, 2), swap(kept, 4)]
         sibling = swap(kept, 1)
         other = level(far)
         far_sibling = swap(far, 1)
-        early = early_gram([kept, sibling])
+        tokens_sibling = swap(tokens, 1)
+        *early, held = early_gram([kept, sibling], tokens)
         near, early, far_sibling = lax.optimization_barrier((near, early, far_sibling))
         near_sibling = [swap(piece, 1) for piece in near]
         other_sibling = swap(other, 1)
         pieces = [kept, sibling, near[0], near_sibling[0], near[1], near_sibling[1]]
-        return pieces + [(far, other), (far_sibling, other_sibling)], early, near
+        pieces += [(far, other), (far_sibling, other_sibling)]
+        return pieces, early, near, held, tokens_sibling
 
     def on_device(tokens, orig_weight, keep_flags):
         features = tokens.shape[1]
@@ -617,9 +638,8 @@
         begin = panels // 2
         middle = begin + 1
         tokens, kept = lax.optimization_barrier((tokens, kept))
-        pieces, early, arrived = gather_kept(kept, half)
+        pieces, early, arrived, tokens, sibling = gather_kept(kept, half, tokens)
         orig_weight, arrived = lax.optimization_barrier((orig_weight, arrived))
-        sibling = swap(tokens, 1)
         weights = [orig_weight] + [swap(orig_weight, k) for k in others]
         a, scale, factors, follow = first_part(side, *early, pieces[2:], rows, features, begin)
         a, weights, sibling = lax.optimization_barrier((a, weights, sibling))

time: 60.8 us -> 59 us (0.970)
  matrix products: 3.26 us -> 1.71 us
  waiting for transfers between devices: 10.7 us -> 9.97 us
    dot_general x2, matrix products: 3.26 us -> 1.71 us  [on_device(): lax.dot_general(stacked, part, NT, preferred_element_type=jnp.float32)]
    pallas_call x1, Pallas kernels: 0.94 us -> 1.71 us  [early_gram(): pl.pallas_call(body, out_shape=[jax.ShapeDtypeStruct((kept, kept), jnp.fl...]
    ppermute x15, waiting for transfers between devices: 10.7 us -> 9.96 us  [swap(): return lax.ppermute(x, 'dp', [(d, d ^ k) for d in range(n)])]
  transfers between devices with their start and end apart: 16 -> 16, of which waited for: 2 -> 2; matrix products, arithmetic and copies ran while one was open for 0% -> 0% of each run, Pallas kernels for 29% -> 30%
where the time goes in v1:
time: 59 us; the launch traced here: 58.8 us
  Pallas kernels  30.6 us (52%)
  starting transfers between devices  15.4 us (26%)
  waiting for transfers between devices  9.97 us (17%)
  matrix products  1.71 us (3%)
  local copies, waits for them, and re-layouts  0.76 us (1%)
    ppermute x15, starting transfers between devices, swap(): return lax.ppermute(x, 'dp', [(d, d ^ k) for d in range(n)])  13.5 us
    pallas_call x1, Pallas kernels, first_part(): pl.pallas_call(body, out_shape=[jax.ShapeDtypeStruct((kept, kept), jnp.fl...  11.9 us
    pallas_call x1, Pallas kernels, last_part(): pl.pallas_call(body, out_shape=jax.ShapeDtypeStruct((own, features), jnp....  10.6 us
    ppermute x15, waiting for transfers between devices, swap(): return lax.ppermute(x, 'dp', [(d, d ^ k) for d in range(n)])  9.96 us
    pallas_call x1, Pallas kernels, middle_part(): pl.pallas_call(functools.partial(middle_kernel, first, last), out_shape=[...  3.95 us
    pallas_call x1, Pallas kernels, select_kept(): pl.pallas_call(select_kernel, out_shape=[jax.ShapeDtypeStruct((kept + EXT...  2.39 us
    ppermute x1, starting transfers between devices, level(): lax.ppermute(x, 'section', [(d, d ^ 1) for d in range(mesh.shape['section...  1.97 us
    pallas_call x1, Pallas kernels, early_gram(): pl.pallas_call(body, out_shape=[jax.ShapeDtypeStruct((kept, kept), jnp.fl...  1.71 us
  transfers between devices with their start and end apart: 16, of which 2 were waited for; matrix products, arithmetic and copies ran while one was open for 0% of the time, Pallas kernels for 30%

profile of v1, /device:TPU:0, one launch (start us, length us, event | category | flops | bytes accessed | tf_op | source)
XLA Modules:
  0.0 58.8 jit_solution(8144946731122230490)
XLA Ops:
  0.0 0.0 copy-start
  0.0 0.7 %copy-done = s32[64]{0:T(128)S(1)} copy-done((s32[64]{0:T(128)S(1)}, s32[64]{0:T(128)}, u32[]{:S(2)}) %copy-start) | copy-done | bytes 280
  0.7 0.0 copy-start.2
  0.7 2.4 %select_kept.1 = (bf16[784,256]{1,0:T(8,128)(2,1)S(1)}, bf16[400,256]{1,0:T(8,128)(2,1)S(1)}) custom-call(s32[1]{0:T(128)} %bitcast.side_ref.refs_0_, s32[64]{0:T(128)S(1)} %copy-done, bf16[256,4096]{1,0:T(8,128)(2,1)} %refs_2_), custom_call_target="tpu_custom_call" | custom-call | tf_op jit(solution)/shard_map/select_kept/pallas_call | solution.py:90
  3.1 0.5 collective-permute-start.12
  3.6 3.5 %collective-permute-start.3 = (bf16[400,256]{1,0:T(8,128)(2,1)S(1)}, bf16[400,256]{1,0:T(8,128)(2,1)S(1)}, u32[]{:S(2)}, u32[]{:S(2)}) collective-permute-start(bf16[400,256]{1,0:T(8,128)(2,1)S(1)} %get-tuple-element.38), channel_id=1, source_target_pairs={{0,6},{1,7},{2,4},{3,5},{4,2},{5,3},{6,0},{7,1},{8,14},{9,15},{10,... | collective-permute-start | bytes 614408 | tf_op jit(solution)/shard_map/ppermute | solution.py:606
  7.1 0.2 collective-permute-start.2
  7.3 0.5 collective-permute-start
  7.8 0.3 collective-permute-start.1
  8.1 5.0 %collective-permute-done.3.refs_7_.refs_18_ = bf16[400,256]{1,0:T(8,128)(2,1)S(1)} collective-permute-done((bf16[400,256]{1,0:T(8,128)(2,1)S(1)}, bf16[400,256]{1,0:T(8,128)(2,1)S(1)}, u32[]{:S(2)}, u32[]{:S(2)}) %collective-permute-start.3) | collective-permute-done | bytes 204832 | tf_op jit(solution)/shard_map/ppermute | solution.py:606
  13.1 0.0 collective-permute-start.4
  13.1 0.0 collective-permute-done.2.refs_1_.refs_13_
  13.1 2.0 %collective-permute-start.7 = (bf16[400,256]{1,0:T(8,128)(2,1)S(1)}, bf16[400,256]{1,0:T(8,128)(2,1)S(1)}, u32[]{:S(2)}, u32[]{:S(2)}) collective-permute-start(bf16[400,256]{1,0:T(8,128)(2,1)S(1)} %collective-permute-done.3.refs_7_.refs_18_), channel_id=1, source_target_pairs={{0,8},{8,0},{16,24},{24,16},{1,9},{9,1},{17,25},{25,17},{2,10},{10... | collective-permute-start | bytes 614408 | tf_op jit(solution)/shard_map/ppermute | solution.py:609
  15.1 1.7 %early_gram.1 = (f32[768,768]{1,0:T(8,128)S(1)}, f32[8,128]{1,0:T(8,128)S(1)}, bf16[256,4096]{1,0:T(8,128)(2,1)S(1)}) custom-call(bf16[784,256]{1,0:T(8,128)(2,1)S(1)} %get-tuple-element.34.refs_0_.refs_12_, bf16[784,256]{1,0:T(8,128)(2,1)S(1)} %collective-permute-done.2.refs_1_.refs_13_, bf16[256,4096]{1,0:T(8,128)(2,1)} %refs_2_), custom_call_target="tpu_custom_call" | custom-call | tf_op jit(solution)/shard_map/early_gram/pallas_call | solution.py:356
  16.8 4.9 %collective-permute-done.refs_3_.refs_14_ = bf16[784,256]{1,0:T(8,128)(2,1)S(1)} collective-permute-done((bf16[784,256]{1,0:T(8,128)(2,1)S(1)}, bf16[784,256]{1,0:T(8,128)(2,1)S(1)}, u32[]{:S(2)}, u32[]{:S(2)}) %collective-permute-start) | collective-permute-done | bytes 401440 | tf_op jit(solution)/shard_map/ppermute | solution.py:606
  21.7 0.0 collective-permute-done.1.refs_5_.refs_16_
  21.7 0.0 collective-permute-done.4.refs_9_.refs_20_
  21.7 0.0 collective-permute-start.5
  21.7 0.0 collective-permute-done.7.refs_8_.refs_19_
  21.7 0.5 collective-permute-start.8
  22.2 0.1 collective-permute-start.6
  22.3 0.0 copy-done.2
  22.3 1.4 %collective-permute-start.10 = (bf16[32,4096]{1,0:T(8,128)(2,1)S(1)}, bf16[32,4096]{1,0:T(8,128)(2,1)S(1)}, u32[]{:S(2)}, u32[]{:S(2)}) collective-permute-start(bf16[32,4096]{1,0:T(8,128)(2,1)S(1)} %copy-done.2), channel_id=1, source_target_pairs={{0,4},{1,5},{2,6},{3,7},{4,0},{5,1},{6,2},{7,3},{8,12},{9,13},{10,... | collective-permute-start | bytes 786440 | tf_op jit(solution)/shard_map/ppermute | solution.py:606
  23.7 0.0 collective-permute-done.8.refs_10_.refs_21_
  23.7 2.3 %collective-permute-start.11 = (bf16[32,4096]{1,0:T(8,128)(2,1)S(1)}, bf16[32,4096]{1,0:T(8,128)(2,1)S(1)}, u32[]{:S(2)}, u32[]{:S(2)}) collective-permute-start(bf16[32,4096]{1,0:T(8,128)(2,1)S(1)} %copy-done.2), channel_id=1, source_target_pairs={{0,6},{1,7},{2,4},{3,5},{4,2},{5,3},{6,0},{7,1},{8,14},{9,15},{10,... | collective-permute-start | bytes 786440 | tf_op jit(solution)/shard_map/ppermute | solution.py:606
  26.1 0.0 collective-permute-done.5.refs_4_.refs_15_
  26.1 0.5 collective-permute-start.9
  26.6 0.0 collective-permute-done.6.refs_6_.refs_17_
  26.6 11.9 %gram_and_first_panels.1 = (f32[768,768]{1,0:T(8,128)S(1)}, f32[8,128]{1,0:T(8,128)S(1)}, f32[3,2,128,128]{3,2,1,0:T(8,128)S(1)}, f32[128,128]{1,0:T(8,128)S(1)}) custom-call(s32[1]{0:T(128)} %bitcast.side_ref.refs_0_, f32[768,768]{1,0:T(8,128)S(1)} %get-tuple-element.39.refs_1_, f32[8,128]{1,0:T(8,128)S(1)} %get-tuple-element.40.refs_2_, ...), custom_call_target="tpu_custom_call" | custom-call | tf_op jit(solution)/shard_map/gram_and_first_panels/pallas_call | solution.py:410
  38.5 0.0 collective-permute-done.10
  38.5 0.0 collective-permute-done.11
  38.6 0.0 collective-permute-done.9
  38.6 0.0 collective-permute-done.12
  38.7 0.9 %fusion.1 = f32[128,256]{1,0:T(8,128)S(1)} fusion(bf16[128,4096]{1,0:T(8,128)(2,1)S(1)} %constant_dynamic-update-slice_fusion, bf16[256,4096]{1,0:T(8,128)(2,1)S(1)} %get-tuple-element.50), kind=kOutput, calls=%fused_computation.6 | convolution fusion | flops 268435456 | bytes 3276800 | tf_op jit(solution)/shard_map/dot_general | solution.py:648
  39.6 0.8 %fusion.2 = f32[128,256]{1,0:T(8,128)S(1)} fusion(bf16[128,4096]{1,0:T(8,128)(2,1)S(1)} %constant_dynamic-update-slice_fusion, bf16[256,4096]{1,0:T(8,128)(2,1)S(1)} %collective-permute-done.12), kind=kOutput, calls=%fused_computation.7 | convolution fusion | flops 268435456 | bytes 3276800 | tf_op jit(solution)/shard_map/dot_general | solution.py:648
  40.4 0.0 copy-start.1
  40.5 1.6 %collective-permute-start.13 = (f32[32,512]{1,0:T(8,128)S(1)}, f32[32,512]{1,0:T(8,128)S(1)}, u32[]{:S(2)}, u32[]{:S(2)}) collective-permute-start(f32[32,512]{1,0:T(8,128)S(1)} %get-tuple-element.63), channel_id=1, source_target_pairs={{0,2},{1,3},{2,0},{3,1},{4,6},{5,7},{6,4},{7,5},{8,10},{9,11},{10,... | collective-permute-start | bytes 196616 | tf_op jit(solution)/shard_map/ppermute | solution.py:606
  42.0 0.6 %collective-permute-start.14 = (f32[32,512]{1,0:T(8,128)S(1)}, f32[32,512]{1,0:T(8,128)S(1)}, u32[]{:S(2)}, u32[]{:S(2)}) collective-permute-start(f32[32,512]{1,0:T(8,128)S(1)} %get-tuple-element.62), channel_id=1, source_target_pairs={{0,4},{1,5},{2,6},{3,7},{4,0},{5,1},{6,2},{7,3},{8,12},{9,13},{10,... | collective-permute-start | bytes 196616 | tf_op jit(solution)/shard_map/ppermute | solution.py:606
  42.6 1.4 %collective-permute-start.15 = (f32[32,512]{1,0:T(8,128)S(1)}, f32[32,512]{1,0:T(8,128)S(1)}, u32[]{:S(2)}, u32[]{:S(2)}) collective-permute-start(f32[32,512]{1,0:T(8,128)S(1)} %get-tuple-element.61), channel_id=1, source_target_pairs={{0,6},{1,7},{2,4},{3,5},{4,2},{5,3},{6,0},{7,1},{8,14},{9,15},{10,... | collective-permute-start | bytes 196616 | tf_op jit(solution)/shard_map/ppermute | solution.py:606
  44.0 3.9 %middle_panels.1 = (f32[512,512]{1,0:T(8,128)S(1)}, f32[1,2,128,128]{3,2,1,0:T(8,128)S(1)}, f32[128,128]{1,0:T(8,128)S(1)}) custom-call(f32[768,768]{1,0:T(8,128)S(1)} %get-tuple-element.55.start_ref.refs_7_, f32[3,2,128,128]{3,2,1,0:T(8,128)S(1)} %get-tuple-element.56.early_ref.refs_8_, f32[128,128]{1,0:T(8,128)S(1)} %get-tuple-element.57.start_next_ref), custom_call_target="tpu_custom_call" | custom-call | tf_op jit(solution)/shard_map/middle_panels/pallas_call | solution.py:456
  48.0 0.0 collective-permute-done.13.refs_3_
  48.0 0.0 collective-permute-done.14.refs_4_
  48.0 0.0 collective-permute-done.15.refs_5_
  48.0 0.0 copy-done.1
  48.0 10.6 %last_panels_and_solution.1 = bf16[32,4096]{1,0:T(8,128)(2,1)} custom-call(s32[1]{0:T(128)} %bitcast.side_ref.refs_0_, s32[64]{0:T(128)S(1)} %copy-done.1, f32[32,512]{1,0:T(8,128)S(1)} %get-tuple-element.64.refs_2_, f32[32,512]{1,0:T(8,128)S(1)} %collective-permute-done.13.refs_3_, f32[32,512]{1,0:T(8,128)S(1)} %collective-permute-done.14.refs_4_, ...), custom_call_target="tpu_custom_call" | custom-call | tf_op jit(solution)/shard_map/last_panels_and_solution/pallas_call | solution.py:581
  (6 shorter events, 0.1 us)
Async XLA Ops:
  0.0 0.7 %copy-start = (s32[64]{0:T(128)S(1)}, s32[64]{0:T(128)}, u32[]{:S(2)}) copy-start(s32[64]{0:T(128)} %refs_1_.1) | copy-start | bytes 772
  0.7 21.6 %copy-start.2 = (bf16[32,4096]{1,0:T(8,128)(2,1)S(1)}, bf16[32,4096]{1,0:T(8,128)(2,1)}, u32[]{:S(2)}) copy-start(bf16[32,4096]{1,0:T(8,128)(2,1)} %param.4) | copy-start | bytes 786436
  3.1 35.5 %collective-permute-start.12 = (bf16[256,4096]{1,0:T(8,128)(2,1)}, bf16[256,4096]{1,0:T(8,128)(2,1)S(1)}, u32[]{:S(2)}, u32[]{:S(2)}) collective-permute-start(bf16[256,4096]{1,0:T(8,128)(2,1)} %refs_2_), channel_id=1, source_target_pairs={{0,1},{1,0},{2,3},{3,2},{4,5},{5,4},{6,7},{7,6},{8,9},{9,8},{10,11... | collective-permute-start | bytes 6291464 | tf_op jit(solution)/shard_map/ppermute | solution.py:606
  3.6 9.5 %collective-permute-start.3 = (bf16[400,256]{1,0:T(8,128)(2,1)S(1)}, bf16[400,256]{1,0:T(8,128)(2,1)S(1)}, u32[]{:S(2)}, u32[]{:S(2)}) collective-permute-start(bf16[400,256]{1,0:T(8,128)(2,1)S(1)} %get-tuple-element.38), channel_id=1, source_target_pairs={{0,6},{1,7},{2,4},{3,5},{4,2},{5,3},{6,0},{7,1},{8,14},{9,15},{10,... | collective-permute-start | bytes 614408 | tf_op jit(solution)/shard_map/ppermute | solution.py:606
  7.1 6.0 %collective-permute-start.2 = (bf16[784,256]{1,0:T(8,128)(2,1)S(1)}, bf16[784,256]{1,0:T(8,128)(2,1)S(1)}, u32[]{:S(2)}, u32[]{:S(2)}) collective-permute-start(bf16[784,256]{1,0:T(8,128)(2,1)S(1)} %get-tuple-element.34.refs_0_.refs_12_), channel_id=1, source_target_pairs={{0,1},{1,0},{2,3},{3,2},{4,5},{5,4},{6,7},{7,6},{8,9},{9,8},{10,11... | collective-permute-start | bytes 1204232 | tf_op jit(solution)/shard_map/ppermute | solution.py:606
  7.3 14.4 %collective-permute-start = (bf16[784,256]{1,0:T(8,128)(2,1)S(1)}, bf16[784,256]{1,0:T(8,128)(2,1)S(1)}, u32[]{:S(2)}, u32[]{:S(2)}) collective-permute-start(bf16[784,256]{1,0:T(8,128)(2,1)S(1)} %get-tuple-element.34.refs_0_.refs_12_), channel_id=1, source_target_pairs={{0,2},{1,3},{2,0},{3,1},{4,6},{5,7},{6,4},{7,5},{8,10},{9,11},{10,... | collective-permute-start | bytes 1204232 | tf_op jit(solution)/shard_map/ppermute | solution.py:606
  7.8 13.9 %collective-permute-start.1 = (bf16[784,256]{1,0:T(8,128)(2,1)S(1)}, bf16[784,256]{1,0:T(8,128)(2,1)S(1)}, u32[]{:S(2)}, u32[]{:S(2)}) collective-permute-start(bf16[784,256]{1,0:T(8,128)(2,1)S(1)} %get-tuple-element.34.refs_0_.refs_12_), channel_id=1, source_target_pairs={{0,4},{1,5},{2,6},{3,7},{4,0},{5,1},{6,2},{7,3},{8,12},{9,13},{10,... | collective-permute-start | bytes 1204232 | tf_op jit(solution)/shard_map/ppermute | solution.py:606
  13.1 8.6 %collective-permute-start.4 = (bf16[400,256]{1,0:T(8,128)(2,1)S(1)}, bf16[400,256]{1,0:T(8,128)(2,1)S(1)}, u32[]{:S(2)}, u32[]{:S(2)}) collective-permute-start(bf16[400,256]{1,0:T(8,128)(2,1)S(1)} %collective-permute-done.3.refs_7_.refs_18_), channel_id=1, source_target_pairs={{0,1},{1,0},{2,3},{3,2},{4,5},{5,4},{6,7},{7,6},{8,9},{9,8},{10,11... | collective-permute-start | bytes 614408 | tf_op jit(solution)/shard_map/ppermute | solution.py:606
  13.1 8.6 %collective-permute-start.7 = (bf16[400,256]{1,0:T(8,128)(2,1)S(1)}, bf16[400,256]{1,0:T(8,128)(2,1)S(1)}, u32[]{:S(2)}, u32[]{:S(2)}) collective-permute-start(bf16[400,256]{1,0:T(8,128)(2,1)S(1)} %collective-permute-done.3.refs_7_.refs_18_), channel_id=1, source_target_pairs={{0,8},{8,0},{16,24},{24,16},{1,9},{9,1},{17,25},{25,17},{2,10},{10... | collective-permute-start | bytes 614408 | tf_op jit(solution)/shard_map/ppermute | solution.py:609
  21.7 4.4 %collective-permute-start.5 = (bf16[784,256]{1,0:T(8,128)(2,1)S(1)}, bf16[784,256]{1,0:T(8,128)(2,1)S(1)}, u32[]{:S(2)}, u32[]{:S(2)}) collective-permute-start(bf16[784,256]{1,0:T(8,128)(2,1)S(1)} %collective-permute-done.refs_3_.refs_14_), channel_id=1, source_target_pairs={{0,1},{1,0},{2,3},{3,2},{4,5},{5,4},{6,7},{7,6},{8,9},{9,8},{10,11... | collective-permute-start | bytes 1204232 | tf_op jit(solution)/shard_map/ppermute | solution.py:606
  21.7 2.0 %collective-permute-start.8 = (bf16[400,256]{1,0:T(8,128)(2,1)S(1)}, bf16[400,256]{1,0:T(8,128)(2,1)S(1)}, u32[]{:S(2)}, u32[]{:S(2)}) collective-permute-start(bf16[400,256]{1,0:T(8,128)(2,1)S(1)} %collective-permute-done.7.refs_8_.refs_19_), channel_id=1, source_target_pairs={{0,1},{1,0},{2,3},{3,2},{4,5},{5,4},{6,7},{7,6},{8,9},{9,8},{10,11... | collective-permute-start | bytes 614408 | tf_op jit(solution)/shard_map/ppermute | solution.py:606
  22.2 4.4 %collective-permute-start.6 = (bf16[784,256]{1,0:T(8,128)(2,1)S(1)}, bf16[784,256]{1,0:T(8,128)(2,1)S(1)}, u32[]{:S(2)}, u32[]{:S(2)}) collective-permute-start(bf16[784,256]{1,0:T(8,128)(2,1)S(1)} %collective-permute-done.1.refs_5_.refs_16_), channel_id=1, source_target_pairs={{0,1},{1,0},{2,3},{3,2},{4,5},{5,4},{6,7},{7,6},{8,9},{9,8},{10,11... | collective-permute-start | bytes 1204232 | tf_op jit(solution)/shard_map/ppermute | solution.py:606
  22.3 16.2 %collective-permute-start.10 = (bf16[32,4096]{1,0:T(8,128)(2,1)S(1)}, bf16[32,4096]{1,0:T(8,128)(2,1)S(1)}, u32[]{:S(2)}, u32[]{:S(2)}) collective-permute-start(bf16[32,4096]{1,0:T(8,128)(2,1)S(1)} %copy-done.2), channel_id=1, source_target_pairs={{0,4},{1,5},{2,6},{3,7},{4,0},{5,1},{6,2},{7,3},{8,12},{9,13},{10,... | collective-permute-start | bytes 786440 | tf_op jit(solution)/shard_map/ppermute | solution.py:606
  23.7 14.8 %collective-permute-start.11 = (bf16[32,4096]{1,0:T(8,128)(2,1)S(1)}, bf16[32,4096]{1,0:T(8,128)(2,1)S(1)}, u32[]{:S(2)}, u32[]{:S(2)}) collective-permute-start(bf16[32,4096]{1,0:T(8,128)(2,1)S(1)} %copy-done.2), channel_id=1, source_target_pairs={{0,6},{1,7},{2,4},{3,5},{4,2},{5,3},{6,0},{7,1},{8,14},{9,15},{10,... | collective-permute-start | bytes 786440 | tf_op jit(solution)/shard_map/ppermute | solution.py:606
  26.1 12.5 %collective-permute-start.9 = (bf16[32,4096]{1,0:T(8,128)(2,1)S(1)}, bf16[32,4096]{1,0:T(8,128)(2,1)S(1)}, u32[]{:S(2)}, u32[]{:S(2)}) collective-permute-start(bf16[32,4096]{1,0:T(8,128)(2,1)S(1)} %copy-done.2), channel_id=1, source_target_pairs={{0,2},{1,3},{2,0},{3,1},{4,6},{5,7},{6,4},{7,5},{8,10},{9,11},{10,... | collective-permute-start | bytes 786440 | tf_op jit(solution)/shard_map/ppermute | solution.py:606
  40.4 7.6 %copy-start.1 = (s32[64]{0:T(128)S(1)}, s32[64]{0:T(128)}, u32[]{:S(2)}) copy-start(s32[64]{0:T(128)} %refs_1_.1) | copy-start | bytes 772
  40.5 7.5 %collective-permute-start.13 = (f32[32,512]{1,0:T(8,128)S(1)}, f32[32,512]{1,0:T(8,128)S(1)}, u32[]{:S(2)}, u32[]{:S(2)}) collective-permute-start(f32[32,512]{1,0:T(8,128)S(1)} %get-tuple-element.63), channel_id=1, source_target_pairs={{0,2},{1,3},{2,0},{3,1},{4,6},{5,7},{6,4},{7,5},{8,10},{9,11},{10,... | collective-permute-start | bytes 196616 | tf_op jit(solution)/shard_map/ppermute | solution.py:606
  42.0 6.0 %collective-permute-start.14 = (f32[32,512]{1,0:T(8,128)S(1)}, f32[32,512]{1,0:T(8,128)S(1)}, u32[]{:S(2)}, u32[]{:S(2)}) collective-permute-start(f32[32,512]{1,0:T(8,128)S(1)} %get-tuple-element.62), channel_id=1, source_target_pairs={{0,4},{1,5},{2,6},{3,7},{4,0},{5,1},{6,2},{7,3},{8,12},{9,13},{10,... | collective-permute-start | bytes 196616 | tf_op jit(solution)/shard_map/ppermute | solution.py:606
  42.6 5.4 %collective-permute-start.15 = (f32[32,512]{1,0:T(8,128)S(1)}, f32[32,512]{1,0:T(8,128)S(1)}, u32[]{:S(2)}, u32[]{:S(2)}) collective-permute-start(f32[32,512]{1,0:T(8,128)S(1)} %get-tuple-element.61), channel_id=1, source_target_pairs={{0,6},{1,7},{2,4},{3,5},{4,2},{5,3},{6,0},{7,1},{8,14},{9,15},{10,... | collective-permute-start | bytes 196616 | tf_op jit(solution)/shard_map/ppermute | solution.py:606

commit v2 on v1

--- a/solution.py
+++ b/solution.py
@@ -368,8 +368,8 @@
     )(*pieces, source)
 
 
-def first_kernel(features, rows, last, early_ref, squares_ref, *refs):
-    a_ref, scale_ref, factors_ref, next_ref, all_ref, w_ref, left_ref, right_ref = refs[-8:]
+def first_kernel(features, rows, last, fetch, squares_ref, *refs):
+    a_ref, scale_ref, factors_ref, next_ref, all_ref, corner_ref, w_ref, left_ref, right_ref = refs[-9:]
     kept = a_ref.shape[0]
     total = squares_ref[...] + square_sum(all_ref, kept, rows)
     scale_ref[...] = 1.0 / (0.01 * total / features)
@@ -378,11 +378,11 @@
     def gram(at, tile):
         row = lax.broadcasted_iota(jnp.int32, (kept, tile), 0)
         lane = lax.broadcasted_iota(jnp.int32, (kept, tile), 1)
-        value = early_ref[:, at:at + tile] + gram_columns(all_ref, kept, at, tile)
+        value = a_ref[:, at:at + tile] + gram_columns(all_ref, kept, at, tile)
         a_ref[:, at:at + tile] = value * scale + jnp.where(row == lane + at, 1.0, 0.0)
 
     block = slice(0, PANEL)
-    corner = early_ref[block, block] + dot32(all_ref[block, :], all_ref[block, :], NT)
+    corner = corner_ref[...] + dot32(all_ref[block, :], all_ref[block, :], NT)
     row = lax.broadcasted_iota(jnp.int32, (PANEL, PANEL), 0)
     lane = lax.broadcasted_iota(jnp.int32, (PANEL, PANEL), 1)
     next_ref[...] = corner * scale + jnp.where(row == lane, 1.0, 0.0)
@@ -391,7 +391,7 @@
         if p:
             tasks = settle_tasks(p - 1, state, factors_ref.at[p - 1, 0], factors_ref.at[p - 1, 1])
         else:
-            tasks = [functools.partial(gram, at, 256) for at in range(0, kept, 256)]
+            tasks = [fetch.wait] + [functools.partial(gram, at, 256) for at in range(0, kept, 256)]
         panel(p, state, factors_ref.at[p], tasks)
 
 
@@ -400,12 +400,20 @@
     count = len(flat(pieces))
     all_scratch, sem_scratch = piece_scratch(pieces, kept)
     vmem = pl.BlockSpec(memory_space=pltpu.VMEM)
+    anywhere = pl.BlockSpec(memory_space=pl.ANY)
 
     def body(*refs):
-        side_ref, refs, sem = refs[0], refs[1:-1], refs[-1]
-        for copy in place_pieces(pieces, refs[2:count + 2], side_ref[0], refs[count + 6], sem):
+        side_ref, early_ref, refs, sem, early_sem = refs[0], refs[1], refs[2:-2], refs[-2], refs[-1]
+        a_ref, all_ref, corner_ref = refs[count + 1], refs[count + 5], refs[count + 6]
+        block = pl.ds(0, PANEL)
+        corner = pltpu.make_async_copy(early_ref.at[block, block], corner_ref, early_sem.at[0])
+        corner.start()
+        copies = place_pieces(pieces, refs[1:count + 1], side_ref[0], all_ref, sem)
+        fetch = pltpu.make_async_copy(early_ref, a_ref, early_sem.at[1])
+        fetch.start()
+        for copy in [corner, *copies]:
             copy.wait()
-        first_kernel(float(features), rows, last, *refs)
+        first_kernel(float(features), rows, last, fetch, *refs)
 
     return pl.pallas_call(
         body,
@@ -415,12 +423,14 @@
             factors_shape(last),
             jax.ShapeDtypeStruct((PANEL, PANEL), jnp.float32),
         ],
-        in_specs=[pl.BlockSpec(memory_space=pltpu.SMEM)] + [vmem] * 2 + [pl.BlockSpec(memory_space=pl.ANY)] * count,
+        in_specs=[pl.BlockSpec(memory_space=pltpu.SMEM), anywhere, vmem] + [anywhere] * count,
         out_specs=[vmem] * 4,
         scratch_shapes=[
             all_scratch,
+            pltpu.VMEM((PANEL, PANEL), jnp.float32),
             *work_scratch(kept),
             sem_scratch,
+            pltpu.SemaphoreType.DMA((2,)),
         ],
         compiler_params=pltpu.CompilerParams(vmem_limit_bytes=VMEM_LIMIT),
         name="gram_and_first_panels",
@@ -439,9 +449,13 @@
 
 
 def middle_kernel(first, last, start_ref, early_ref, start_next_ref, a_ref, factors_ref, next_ref, *work):
+    *work, sem = work
     kept = start_ref.shape[0]
     offset = kept - a_ref.shape[0]
-    a_ref[...] = start_ref[offset:, offset:]
+    live = pl.ds(offset, kept - offset)
+    fetch = pltpu.make_async_copy(start_ref.at[live, live], a_ref, sem)
+    fetch.start()
+    fetch.wait()
     next_ref[...] = start_next_ref[...]
     state = (a_ref, offset, next_ref, *work)
     for p in range(first, last):
@@ -460,9 +474,9 @@
             factors_shape(last - first),
             jax.ShapeDtypeStruct((PANEL, PANEL), jnp.float32),
         ],
-        in_specs=[vmem] * 3,
+        in_specs=[pl.BlockSpec(memory_space=pl.ANY)] + [vmem] * 2,
         out_specs=[vmem] * 3,
-        scratch_shapes=work_scratch(kept),
+        scratch_shapes=[*work_scratch(kept), pltpu.SemaphoreType.DMA],
         compiler_params=pltpu.CompilerParams(vmem_limit_bytes=VMEM_LIMIT),
         name="middle_panels",
     )(a, factors, follow)
@@ -471,8 +485,9 @@
 def last_kernel(chips, begin, middle, copies, flags_ref, *refs):
     projected, refs = refs[:chips], refs[chips:]
     scale_ref, whole_ref, early_ref, start_ref, mid_ref, start_next_ref = refs[:6]
-    out_ref, index_ref, wide_out_ref, all_ref, late_ref, a_ref, next_ref = refs[-10:-3]
-    work = refs[-3:]
+    out_ref, index_ref, wide_out_ref, all_ref, late_ref, a_ref, next_ref = refs[-13:-6]
+    top_ref, mid_rows_ref, *work = refs[-6:-1]
+    sem = refs[-1]
     own, features = out_ref.shape
     blocks = flags_ref.shape[0]
     width = features // blocks
@@ -484,7 +499,14 @@
     wide_out_ref[...] = jnp.zeros((own, features), jnp.float32)
     offset = kept - a_ref.shape[0]
     cut = start_ref.shape[0] - a_ref.shape[0]
-    a_ref[...] = start_ref[cut:, cut:]
+    live = pl.ds(cut, a_ref.shape[0])
+    fetches = [
+        pltpu.make_async_copy(start_ref.at[live, live], a_ref, sem.at[0]),
+        pltpu.make_async_copy(start_ref.at[pl.ds(0, cut), :], mid_rows_ref, sem.at[1]),
+        pltpu.make_async_copy(whole_ref.at[pl.ds(0, top_ref.shape[0]), :], top_ref, sem.at[2]),
+    ]
+    for fetch in fetches:
+        fetch.start()
     next_ref[...] = start_next_ref[...]
     state = (a_ref, offset, next_ref, *work)
     held = {}
@@ -492,9 +514,9 @@
     def factor(p):
         source, skip = a_ref, offset
         if p < begin - 1:
-            source, skip = whole_ref, 0
+            source, skip = top_ref, 0
         elif p < middle - 1:
-            source, skip = start_ref, kept - start_ref.shape[0]
+            source, skip = mid_rows_ref, kept - start_ref.shape[0]
         low = p * PANEL - skip
         return source[low:low + PANEL, low + PANEL:]
 
@@ -529,15 +551,13 @@
             value = base - dot_small(held["back"], factor(p), NT)
             held["back"] = jnp.concatenate([value, held["back"]], axis=1)
 
-    def await_pieces():
-        for copy in copies:
-            copy.wait()
-
+    for copy in fetches + copies:
+        copy.wait()
     for p in range(middle, last):
         tasks = settle(p - 1)
         if p == last - 1:
-            tasks += [await_pieces, make_right] + [functools.partial(forward, q) for q in range(p)]
-            tasks += [functools.partial(scaled, q) for q in range(p)]
+            tasks = [make_right] + [functools.partial(forward, q) for q in range(p - 1)] + tasks
+            tasks += [functools.partial(forward, p - 1)] + [functools.partial(scaled, q) for q in range(p)]
         panel(p, state, late_ref.at[p - middle], tasks)
     tasks = settle(last - 1)
     tasks += [functools.partial(forward, last - 1), functools.partial(scaled, last - 1)]
@@ -581,7 +601,10 @@
     return pl.pallas_call(
         body,
         out_shape=jax.ShapeDtypeStruct((own, features), jnp.bfloat16),
-        in_specs=[pl.BlockSpec(memory_space=pltpu.SMEM)] * 2 + [vmem] * (chips + len(begun)) + [anywhere] * count,
+        in_specs=[pl.BlockSpec(memory_space=pltpu.SMEM)] * 2
+        + [vmem] * (chips + 1)
+        + [anywhere, vmem, anywhere, vmem, vmem]
+        + [anywhere] * count,
         out_specs=vmem,
         scratch_shapes=[
             pltpu.SMEM((blocks + 1,), jnp.int32),
@@ -590,7 +613,10 @@
             pltpu.VMEM((kept // PANEL - 1 - middle, 2, PANEL, PANEL), jnp.float32),
             pltpu.VMEM((left, left), jnp.float32),
             pltpu.VMEM((PANEL, PANEL), jnp.float32),
+            pltpu.VMEM(((begin - 1) * PANEL, kept), jnp.float32),
+            pltpu.VMEM(((middle - begin) * PANEL, kept - (begin - 1) * PANEL), jnp.float32),
             *work_scratch(kept),
+            pltpu.SemaphoreType.DMA((3,)),
             sem_scratch,
         ],
         compiler_params=pltpu.CompilerParams(vmem_limit_bytes=VMEM_LIMIT),

time: 59 us -> 59 us (level)
  no operation moved by 1% of the time
where the time goes in v2:
time: 59 us; the launch traced here: 58.8 us
  Pallas kernels  30.6 us (52%)
  starting transfers between devices  15.4 us (26%)
  waiting for transfers between devices  9.94 us (17%)
  matrix products  1.71 us (3%)
  local copies, waits for them, and re-layouts  0.76 us (1%)
    ppermute x15, starting transfers between devices, swap(): return lax.ppermute(x, 'dp', [(d, d ^ k) for d in range(n)])  13.5 us
    pallas_call x1, Pallas kernels, first_part(): pl.pallas_call(body, out_shape=[jax.ShapeDtypeStruct((kept, kept), jnp.fl...  12.1 us
    pallas_call x1, Pallas kernels, last_part(): pl.pallas_call(body, out_shape=jax.ShapeDtypeStruct((own, features), jnp....  10.4 us
    ppermute x15, waiting for transfers between devices, swap(): return lax.ppermute(x, 'dp', [(d, d ^ k) for d in range(n)])  9.94 us
    pallas_call x1, Pallas kernels, middle_part(): pl.pallas_call(functools.partial(middle_kernel, first, last), out_shape=[...  4.03 us
    pallas_call x1, Pallas kernels, select_kept(): pl.pallas_call(select_kernel, out_shape=[jax.ShapeDtypeStruct((kept + EXT...  2.4 us
    ppermute x1, starting transfers between devices, level(): lax.ppermute(x, 'section', [(d, d ^ 1) for d in range(mesh.shape['section...  1.97 us
    pallas_call x1, Pallas kernels, early_gram(): pl.pallas_call(body, out_shape=[jax.ShapeDtypeStruct((kept, kept), jnp.fl...  1.71 us
  transfers between devices with their start and end apart: 16, of which 2 were waited for; matrix products, arithmetic and copies ran while one was open for 0% of the time, Pallas kernels for 30%

profile of v2, /device:TPU:0, one launch (start us, length us, event | category | flops | bytes accessed | tf_op | source)
XLA Modules:
  0.0 58.8 jit_solution(2605517271438821394)
XLA Ops:
  0.0 0.0 copy-start
  0.0 0.7 %copy-done = s32[64]{0:T(128)S(1)} copy-done((s32[64]{0:T(128)S(1)}, s32[64]{0:T(128)}, u32[]{:S(2)}) %copy-start) | copy-done | bytes 280
  0.7 0.0 copy-start.2
  0.7 2.4 %select_kept.1 = (bf16[784,256]{1,0:T(8,128)(2,1)S(1)}, bf16[400,256]{1,0:T(8,128)(2,1)S(1)}) custom-call(s32[1]{0:T(128)} %bitcast.side_ref.refs_0_, s32[64]{0:T(128)S(1)} %copy-done, bf16[256,4096]{1,0:T(8,128)(2,1)} %refs_2_), custom_call_target="tpu_custom_call" | custom-call | tf_op jit(solution)/shard_map/select_kept/pallas_call | solution.py:90
  3.1 0.5 collective-permute-start.12
  3.6 3.5 %collective-permute-start.3 = (bf16[400,256]{1,0:T(8,128)(2,1)S(1)}, bf16[400,256]{1,0:T(8,128)(2,1)S(1)}, u32[]{:S(2)}, u32[]{:S(2)}) collective-permute-start(bf16[400,256]{1,0:T(8,128)(2,1)S(1)} %get-tuple-element.38), channel_id=1, source_target_pairs={{0,6},{1,7},{2,4},{3,5},{4,2},{5,3},{6,0},{7,1},{8,14},{9,15},{10,... | collective-permute-start | bytes 614408 | tf_op jit(solution)/shard_map/ppermute | solution.py:632
  7.1 0.2 collective-permute-start.2
  7.3 0.5 collective-permute-start
  7.8 0.3 collective-permute-start.1
  8.1 5.0 %collective-permute-done.3.refs_7_.refs_18_ = bf16[400,256]{1,0:T(8,128)(2,1)S(1)} collective-permute-done((bf16[400,256]{1,0:T(8,128)(2,1)S(1)}, bf16[400,256]{1,0:T(8,128)(2,1)S(1)}, u32[]{:S(2)}, u32[]{:S(2)}) %collective-permute-start.3) | collective-permute-done | bytes 204832 | tf_op jit(solution)/shard_map/ppermute | solution.py:632
  13.1 0.0 collective-permute-start.4
  13.1 0.0 collective-permute-done.2.refs_1_.refs_13_
  13.1 2.0 %collective-permute-start.7 = (bf16[400,256]{1,0:T(8,128)(2,1)S(1)}, bf16[400,256]{1,0:T(8,128)(2,1)S(1)}, u32[]{:S(2)}, u32[]{:S(2)}) collective-permute-start(bf16[400,256]{1,0:T(8,128)(2,1)S(1)} %collective-permute-done.3.refs_7_.refs_18_), channel_id=1, source_target_pairs={{0,8},{8,0},{16,24},{24,16},{1,9},{9,1},{17,25},{25,17},{2,10},{10... | collective-permute-start | bytes 614408 | tf_op jit(solution)/shard_map/ppermute | solution.py:635
  15.1 1.7 %early_gram.1 = (f32[768,768]{1,0:T(8,128)S(1)}, f32[8,128]{1,0:T(8,128)S(1)}, bf16[256,4096]{1,0:T(8,128)(2,1)S(1)}) custom-call(bf16[784,256]{1,0:T(8,128)(2,1)S(1)} %get-tuple-element.34.refs_0_.refs_12_, bf16[784,256]{1,0:T(8,128)(2,1)S(1)} %collective-permute-done.2.refs_1_.refs_13_, bf16[256,4096]{1,0:T(8,128)(2,1)} %refs_2_), custom_call_target="tpu_custom_call" | custom-call | tf_op jit(solution)/shard_map/early_gram/pallas_call | solution.py:356
  16.8 4.9 %collective-permute-done.refs_3_.refs_14_ = bf16[784,256]{1,0:T(8,128)(2,1)S(1)} collective-permute-done((bf16[784,256]{1,0:T(8,128)(2,1)S(1)}, bf16[784,256]{1,0:T(8,128)(2,1)S(1)}, u32[]{:S(2)}, u32[]{:S(2)}) %collective-permute-start) | collective-permute-done | bytes 401440 | tf_op jit(solution)/shard_map/ppermute | solution.py:632
  21.7 0.0 collective-permute-done.1.refs_5_.refs_16_
  21.7 0.0 collective-permute-done.4.refs_9_.refs_20_
  21.7 0.0 collective-permute-start.5
  21.7 0.0 collective-permute-done.7.refs_8_.refs_19_
  21.7 0.5 collective-permute-start.8
  22.2 0.1 collective-permute-start.6
  22.3 0.0 copy-done.2
  22.3 1.4 %collective-permute-start.10 = (bf16[32,4096]{1,0:T(8,128)(2,1)S(1)}, bf16[32,4096]{1,0:T(8,128)(2,1)S(1)}, u32[]{:S(2)}, u32[]{:S(2)}) collective-permute-start(bf16[32,4096]{1,0:T(8,128)(2,1)S(1)} %copy-done.2), channel_id=1, source_target_pairs={{0,4},{1,5},{2,6},{3,7},{4,0},{5,1},{6,2},{7,3},{8,12},{9,13},{10,... | collective-permute-start | bytes 786440 | tf_op jit(solution)/shard_map/ppermute | solution.py:632
  23.7 0.0 collective-permute-done.8.refs_10_.refs_21_
  23.7 2.3 %collective-permute-start.11 = (bf16[32,4096]{1,0:T(8,128)(2,1)S(1)}, bf16[32,4096]{1,0:T(8,128)(2,1)S(1)}, u32[]{:S(2)}, u32[]{:S(2)}) collective-permute-start(bf16[32,4096]{1,0:T(8,128)(2,1)S(1)} %copy-done.2), channel_id=1, source_target_pairs={{0,6},{1,7},{2,4},{3,5},{4,2},{5,3},{6,0},{7,1},{8,14},{9,15},{10,... | collective-permute-start | bytes 786440 | tf_op jit(solution)/shard_map/ppermute | solution.py:632
  26.1 0.0 collective-permute-done.5.refs_4_.refs_15_
  26.1 0.5 collective-permute-start.9
  26.6 0.0 collective-permute-done.6.refs_6_.refs_17_
  26.6 12.1 %gram_and_first_panels.1 = (f32[768,768]{1,0:T(8,128)S(1)}, f32[8,128]{1,0:T(8,128)S(1)}, f32[3,2,128,128]{3,2,1,0:T(8,128)S(1)}, f32[128,128]{1,0:T(8,128)S(1)}) custom-call(s32[1]{0:T(128)} %bitcast.side_ref.refs_0_, f32[768,768]{1,0:T(8,128)S(1)} %get-tuple-element.39.refs_1_, f32[8,128]{1,0:T(8,128)S(1)} %get-tuple-element.40.refs_2_, ...), custom_call_target="tpu_custom_call" | custom-call | tf_op jit(solution)/shard_map/gram_and_first_panels/pallas_call | solution.py:418
  38.7 0.0 collective-permute-done.10
  38.7 0.0 collective-permute-done.11
  38.7 0.0 collective-permute-done.9
  38.7 0.0 collective-permute-done.12
  38.8 0.9 %fusion.1 = f32[128,256]{1,0:T(8,128)S(1)} fusion(bf16[128,4096]{1,0:T(8,128)(2,1)S(1)} %constant_dynamic-update-slice_fusion, bf16[256,4096]{1,0:T(8,128)(2,1)S(1)} %get-tuple-element.50), kind=kOutput, calls=%fused_computation.6 | convolution fusion | flops 268435456 | bytes 3276800 | tf_op jit(solution)/shard_map/dot_general | solution.py:674
  39.7 0.8 %fusion.2 = f32[128,256]{1,0:T(8,128)S(1)} fusion(bf16[128,4096]{1,0:T(8,128)(2,1)S(1)} %constant_dynamic-update-slice_fusion, bf16[256,4096]{1,0:T(8,128)(2,1)S(1)} %collective-permute-done.12), kind=kOutput, calls=%fused_computation.7 | convolution fusion | flops 268435456 | bytes 3276800 | tf_op jit(solution)/shard_map/dot_general | solution.py:674
  40.5 0.0 copy-start.1
  40.6 1.6 %collective-permute-start.13 = (f32[32,512]{1,0:T(8,128)S(1)}, f32[32,512]{1,0:T(8,128)S(1)}, u32[]{:S(2)}, u32[]{:S(2)}) collective-permute-start(f32[32,512]{1,0:T(8,128)S(1)} %get-tuple-element.63), channel_id=1, source_target_pairs={{0,2},{1,3},{2,0},{3,1},{4,6},{5,7},{6,4},{7,5},{8,10},{9,11},{10,... | collective-permute-start | bytes 196616 | tf_op jit(solution)/shard_map/ppermute | solution.py:632
  42.2 0.6 %collective-permute-start.14 = (f32[32,512]{1,0:T(8,128)S(1)}, f32[32,512]{1,0:T(8,128)S(1)}, u32[]{:S(2)}, u32[]{:S(2)}) collective-permute-start(f32[32,512]{1,0:T(8,128)S(1)} %get-tuple-element.62), channel_id=1, source_target_pairs={{0,4},{1,5},{2,6},{3,7},{4,0},{5,1},{6,2},{7,3},{8,12},{9,13},{10,... | collective-permute-start | bytes 196616 | tf_op jit(solution)/shard_map/ppermute | solution.py:632
  42.8 1.4 %collective-permute-start.15 = (f32[32,512]{1,0:T(8,128)S(1)}, f32[32,512]{1,0:T(8,128)S(1)}, u32[]{:S(2)}, u32[]{:S(2)}) collective-permute-start(f32[32,512]{1,0:T(8,128)S(1)} %get-tuple-element.61), channel_id=1, source_target_pairs={{0,6},{1,7},{2,4},{3,5},{4,2},{5,3},{6,0},{7,1},{8,14},{9,15},{10,... | collective-permute-start | bytes 196616 | tf_op jit(solution)/shard_map/ppermute | solution.py:632
  44.2 4.0 %middle_panels.1 = (f32[512,512]{1,0:T(8,128)S(1)}, f32[1,2,128,128]{3,2,1,0:T(8,128)S(1)}, f32[128,128]{1,0:T(8,128)S(1)}) custom-call(f32[768,768]{1,0:T(8,128)S(1)} %get-tuple-element.55.start_ref.refs_7_, f32[3,2,128,128]{3,2,1,0:T(8,128)S(1)} %get-tuple-element.56.early_ref.refs_8_, f32[128,128]{1,0:T(8,128)S(1)} %get-tuple-element.57.start_next_ref), custom_call_target="tpu_custom_call" | custom-call | tf_op jit(solution)/shard_map/middle_panels/pallas_call | solution.py:470
  48.2 0.0 collective-permute-done.13.refs_3_
  48.2 0.0 collective-permute-done.14.refs_4_
  48.2 0.0 collective-permute-done.15.refs_5_
  48.2 0.0 copy-done.1
  48.2 10.4 %last_panels_and_solution.1 = bf16[32,4096]{1,0:T(8,128)(2,1)} custom-call(s32[1]{0:T(128)} %bitcast.side_ref.refs_0_, s32[64]{0:T(128)S(1)} %copy-done.1, f32[32,512]{1,0:T(8,128)S(1)} %get-tuple-element.64.refs_2_, f32[32,512]{1,0:T(8,128)S(1)} %collective-permute-done.13.refs_3_, f32[32,512]{1,0:T(8,128)S(1)} %collective-permute-done.14.refs_4_, ...), custom_call_target="tpu_custom_call" | custom-call | tf_op jit(solution)/shard_map/last_panels_and_solution/pallas_call | solution.py:601
  (6 shorter events, 0.1 us)
Async XLA Ops:
  0.0 0.7 %copy-start = (s32[64]{0:T(128)S(1)}, s32[64]{0:T(128)}, u32[]{:S(2)}) copy-start(s32[64]{0:T(128)} %refs_1_.1) | copy-start | bytes 772
  0.7 21.6 %copy-start.2 = (bf16[32,4096]{1,0:T(8,128)(2,1)S(1)}, bf16[32,4096]{1,0:T(8,128)(2,1)}, u32[]{:S(2)}) copy-start(bf16[32,4096]{1,0:T(8,128)(2,1)} %param.4) | copy-start | bytes 786436
  3.1 35.6 %collective-permute-start.12 = (bf16[256,4096]{1,0:T(8,128)(2,1)}, bf16[256,4096]{1,0:T(8,128)(2,1)S(1)}, u32[]{:S(2)}, u32[]{:S(2)}) collective-permute-start(bf16[256,4096]{1,0:T(8,128)(2,1)} %refs_2_), channel_id=1, source_target_pairs={{0,1},{1,0},{2,3},{3,2},{4,5},{5,4},{6,7},{7,6},{8,9},{9,8},{10,11... | collective-permute-start | bytes 6291464 | tf_op jit(solution)/shard_map/ppermute | solution.py:632
  3.6 9.5 %collective-permute-start.3 = (bf16[400,256]{1,0:T(8,128)(2,1)S(1)}, bf16[400,256]{1,0:T(8,128)(2,1)S(1)}, u32[]{:S(2)}, u32[]{:S(2)}) collective-permute-start(bf16[400,256]{1,0:T(8,128)(2,1)S(1)} %get-tuple-element.38), channel_id=1, source_target_pairs={{0,6},{1,7},{2,4},{3,5},{4,2},{5,3},{6,0},{7,1},{8,14},{9,15},{10,... | collective-permute-start | bytes 614408 | tf_op jit(solution)/shard_map/ppermute | solution.py:632
  7.1 6.0 %collective-permute-start.2 = (bf16[784,256]{1,0:T(8,128)(2,1)S(1)}, bf16[784,256]{1,0:T(8,128)(2,1)S(1)}, u32[]{:S(2)}, u32[]{:S(2)}) collective-permute-start(bf16[784,256]{1,0:T(8,128)(2,1)S(1)} %get-tuple-element.34.refs_0_.refs_12_), channel_id=1, source_target_pairs={{0,1},{1,0},{2,3},{3,2},{4,5},{5,4},{6,7},{7,6},{8,9},{9,8},{10,11... | collective-permute-start | bytes 1204232 | tf_op jit(solution)/shard_map/ppermute | solution.py:632
  7.3 14.4 %collective-permute-start = (bf16[784,256]{1,0:T(8,128)(2,1)S(1)}, bf16[784,256]{1,0:T(8,128)(2,1)S(1)}, u32[]{:S(2)}, u32[]{:S(2)}) collective-permute-start(bf16[784,256]{1,0:T(8,128)(2,1)S(1)} %get-tuple-element.34.refs_0_.refs_12_), channel_id=1, source_target_pairs={{0,2},{1,3},{2,0},{3,1},{4,6},{5,7},{6,4},{7,5},{8,10},{9,11},{10,... | collective-permute-start | bytes 1204232 | tf_op jit(solution)/shard_map/ppermute | solution.py:632
  7.8 13.9 %collective-permute-start.1 = (bf16[784,256]{1,0:T(8,128)(2,1)S(1)}, bf16[784,256]{1,0:T(8,128)(2,1)S(1)}, u32[]{:S(2)}, u32[]{:S(2)}) collective-permute-start(bf16[784,256]{1,0:T(8,128)(2,1)S(1)} %get-tuple-element.34.refs_0_.refs_12_), channel_id=1, source_target_pairs={{0,4},{1,5},{2,6},{3,7},{4,0},{5,1},{6,2},{7,3},{8,12},{9,13},{10,... | collective-permute-start | bytes 1204232 | tf_op jit(solution)/shard_map/ppermute | solution.py:632
  13.1 8.6 %collective-permute-start.4 = (bf16[400,256]{1,0:T(8,128)(2,1)S(1)}, bf16[400,256]{1,0:T(8,128)(2,1)S(1)}, u32[]{:S(2)}, u32[]{:S(2)}) collective-permute-start(bf16[400,256]{1,0:T(8,128)(2,1)S(1)} %collective-permute-done.3.refs_7_.refs_18_), channel_id=1, source_target_pairs={{0,1},{1,0},{2,3},{3,2},{4,5},{5,4},{6,7},{7,6},{8,9},{9,8},{10,11... | collective-permute-start | bytes 614408 | tf_op jit(solution)/shard_map/ppermute | solution.py:632
  13.1 8.6 %collective-permute-start.7 = (bf16[400,256]{1,0:T(8,128)(2,1)S(1)}, bf16[400,256]{1,0:T(8,128)(2,1)S(1)}, u32[]{:S(2)}, u32[]{:S(2)}) collective-permute-start(bf16[400,256]{1,0:T(8,128)(2,1)S(1)} %collective-permute-done.3.refs_7_.refs_18_), channel_id=1, source_target_pairs={{0,8},{8,0},{16,24},{24,16},{1,9},{9,1},{17,25},{25,17},{2,10},{10... | collective-permute-start | bytes 614408 | tf_op jit(solution)/shard_map/ppermute | solution.py:635
  21.7 4.4 %collective-permute-start.5 = (bf16[784,256]{1,0:T(8,128)(2,1)S(1)}, bf16[784,256]{1,0:T(8,128)(2,1)S(1)}, u32[]{:S(2)}, u32[]{:S(2)}) collective-permute-start(bf16[784,256]{1,0:T(8,128)(2,1)S(1)} %collective-permute-done.refs_3_.refs_14_), channel_id=1, source_target_pairs={{0,1},{1,0},{2,3},{3,2},{4,5},{5,4},{6,7},{7,6},{8,9},{9,8},{10,11... | collective-permute-start | bytes 1204232 | tf_op jit(solution)/shard_map/ppermute | solution.py:632
  21.7 2.0 %collective-permute-start.8 = (bf16[400,256]{1,0:T(8,128)(2,1)S(1)}, bf16[400,256]{1,0:T(8,128)(2,1)S(1)}, u32[]{:S(2)}, u32[]{:S(2)}) collective-permute-start(bf16[400,256]{1,0:T(8,128)(2,1)S(1)} %collective-permute-done.7.refs_8_.refs_19_), channel_id=1, source_target_pairs={{0,1},{1,0},{2,3},{3,2},{4,5},{5,4},{6,7},{7,6},{8,9},{9,8},{10,11... | collective-permute-start | bytes 614408 | tf_op jit(solution)/shard_map/ppermute | solution.py:632
  22.2 4.4 %collective-permute-start.6 = (bf16[784,256]{1,0:T(8,128)(2,1)S(1)}, bf16[784,256]{1,0:T(8,128)(2,1)S(1)}, u32[]{:S(2)}, u32[]{:S(2)}) collective-permute-start(bf16[784,256]{1,0:T(8,128)(2,1)S(1)} %collective-permute-done.1.refs_5_.refs_16_), channel_id=1, source_target_pairs={{0,1},{1,0},{2,3},{3,2},{4,5},{5,4},{6,7},{7,6},{8,9},{9,8},{10,11... | collective-permute-start | bytes 1204232 | tf_op jit(solution)/shard_map/ppermute | solution.py:632
  22.3 16.4 %collective-permute-start.10 = (bf16[32,4096]{1,0:T(8,128)(2,1)S(1)}, bf16[32,4096]{1,0:T(8,128)(2,1)S(1)}, u32[]{:S(2)}, u32[]{:S(2)}) collective-permute-start(bf16[32,4096]{1,0:T(8,128)(2,1)S(1)} %copy-done.2), channel_id=1, source_target_pairs={{0,4},{1,5},{2,6},{3,7},{4,0},{5,1},{6,2},{7,3},{8,12},{9,13},{10,... | collective-permute-start | bytes 786440 | tf_op jit(solution)/shard_map/ppermute | solution.py:632
  23.7 15.0 %collective-permute-start.11 = (bf16[32,4096]{1,0:T(8,128)(2,1)S(1)}, bf16[32,4096]{1,0:T(8,128)(2,1)S(1)}, u32[]{:S(2)}, u32[]{:S(2)}) collective-permute-start(bf16[32,4096]{1,0:T(8,128)(2,1)S(1)} %copy-done.2), channel_id=1, source_target_pairs={{0,6},{1,7},{2,4},{3,5},{4,2},{5,3},{6,0},{7,1},{8,14},{9,15},{10,... | collective-permute-start | bytes 786440 | tf_op jit(solution)/shard_map/ppermute | solution.py:632
  26.1 12.6 %collective-permute-start.9 = (bf16[32,4096]{1,0:T(8,128)(2,1)S(1)}, bf16[32,4096]{1,0:T(8,128)(2,1)S(1)}, u32[]{:S(2)}, u32[]{:S(2)}) collective-permute-start(bf16[32,4096]{1,0:T(8,128)(2,1)S(1)} %copy-done.2), channel_id=1, source_target_pairs={{0,2},{1,3},{2,0},{3,1},{4,6},{5,7},{6,4},{7,5},{8,10},{9,11},{10,... | collective-permute-start | bytes 786440 | tf_op jit(solution)/shard_map/ppermute | solution.py:632
  40.5 7.7 %copy-start.1 = (s32[64]{0:T(128)S(1)}, s32[64]{0:T(128)}, u32[]{:S(2)}) copy-start(s32[64]{0:T(128)} %refs_1_.1) | copy-start | bytes 772
  40.6 7.6 %collective-permute-start.13 = (f32[32,512]{1,0:T(8,128)S(1)}, f32[32,512]{1,0:T(8,128)S(1)}, u32[]{:S(2)}, u32[]{:S(2)}) collective-permute-start(f32[32,512]{1,0:T(8,128)S(1)} %get-tuple-element.63), channel_id=1, source_target_pairs={{0,2},{1,3},{2,0},{3,1},{4,6},{5,7},{6,4},{7,5},{8,10},{9,11},{10,... | collective-permute-start | bytes 196616 | tf_op jit(solution)/shard_map/ppermute | solution.py:632
  42.2 6.0 %collective-permute-start.14 = (f32[32,512]{1,0:T(8,128)S(1)}, f32[32,512]{1,0:T(8,128)S(1)}, u32[]{:S(2)}, u32[]{:S(2)}) collective-permute-start(f32[32,512]{1,0:T(8,128)S(1)} %get-tuple-element.62), channel_id=1, source_target_pairs={{0,4},{1,5},{2,6},{3,7},{4,0},{5,1},{6,2},{7,3},{8,12},{9,13},{10,... | collective-permute-start | bytes 196616 | tf_op jit(solution)/shard_map/ppermute | solution.py:632
  42.8 5.4 %collective-permute-start.15 = (f32[32,512]{1,0:T(8,128)S(1)}, f32[32,512]{1,0:T(8,128)S(1)}, u32[]{:S(2)}, u32[]{:S(2)}) collective-permute-start(f32[32,512]{1,0:T(8,128)S(1)} %get-tuple-element.61), channel_id=1, source_target_pairs={{0,6},{1,7},{2,4},{3,5},{4,2},{5,3},{6,0},{7,1},{8,14},{9,15},{10,... | collective-permute-start | bytes 196616 | tf_op jit(solution)/shard_map/ppermute | solution.py:632

commit v3 on v1

--- a/solution.py
+++ b/solution.py
@@ -313,25 +313,44 @@
     return copies
 
 
+def halves(pieces):
+    return [piece for piece in pieces if isinstance(piece, tuple)]
+
+
 def piece_scratch(pieces, kept):
     tokens = sum((piece[0] if isinstance(piece, tuple) else piece).shape[1] for piece in pieces)
-    return pltpu.VMEM((kept + EXTRA, tokens), jnp.bfloat16), pltpu.SemaphoreType.DMA((3 * len(pieces),))
-
-
-def gram_columns(all_ref, kept, at, tile):
-    tokens = all_ref.shape[1]
+    return pltpu.VMEM((kept + EXTRA, max(tokens, 128)), jnp.bfloat16), pltpu.SemaphoreType.DMA((3 * len(pieces) + 1,))
+
+
+def piece_specs(pieces):
+    specs = []
+    for piece in pieces:
+        if isinstance(piece, tuple):
+            specs += [pl.BlockSpec(memory_space=pl.ANY)] * len(piece)
+        else:
+            specs.append(pl.BlockSpec(memory_space=pltpu.VMEM))
+    return specs
+
+
+def join_pieces(pieces, refs, side, all_ref, sem):
+    whole = sum(not isinstance(piece, tuple) for piece in pieces)
+    copies = place_pieces(pieces[whole:], refs[whole:], side, all_ref, sem)
+    return copies, list(refs[:whole]) + [all_ref] * (whole < len(pieces))
+
+
+def gram_columns(parts, low, high, at, tile):
     acc = None
-    for c in range(0, tokens, 2048):
-        d = min(c + 2048, tokens)
-        part = dot32(all_ref[:kept, c:d], all_ref[at:at + tile, c:d], NT)
-        acc = part if acc is None else acc + part
+    for part in parts:
+        value = dot32(part[low:high, :], part[at:at + tile, :], NT)
+        acc = value if acc is None else acc + value
     return acc
 
 
-def square_sum(all_ref, kept, rows):
+def square_sum(parts, kept, rows):
     total = jnp.float32(0.0)
-    for k in range(0, all_ref.shape[1], rows):
-        total = total + jnp.sum(all_ref[kept:, k:k + 1].astype(jnp.float32))
+    for part in parts:
+        for k in range(0, part.shape[1], rows):
+            total = total + jnp.sum(part[kept:, k:k + 1].astype(jnp.float32))
     return total
 
 
@@ -348,9 +367,9 @@
         fetch.start()
         for copy in copies:
             copy.wait()
-        squares_ref[...] = jnp.full(squares_ref.shape, square_sum(all_ref, kept, rows), jnp.float32)
+        squares_ref[...] = jnp.full(squares_ref.shape, square_sum([all_ref], kept, rows), jnp.float32)
         for at in range(0, kept, 256):
-            out_ref[:, at:at + 256] = gram_columns(all_ref, kept, at, 256)
+            out_ref[:, at:at + 256] = gram_columns([all_ref], 0, kept, at, 256)
         fetch.wait()
 
     return pl.pallas_call(
@@ -368,21 +387,21 @@
     )(*pieces, source)
 
 
-def first_kernel(features, rows, last, early_ref, squares_ref, *refs):
-    a_ref, scale_ref, factors_ref, next_ref, all_ref, w_ref, left_ref, right_ref = refs[-8:]
+def first_kernel(features, rows, last, parts, early_ref, squares_ref, *refs):
+    a_ref, scale_ref, factors_ref, next_ref, _, w_ref, left_ref, right_ref = refs[-8:]
     kept = a_ref.shape[0]
-    total = squares_ref[...] + square_sum(all_ref, kept, rows)
+    total = squares_ref[...] + square_sum(parts, kept, rows)
     scale_ref[...] = 1.0 / (0.01 * total / features)
     scale = scale_ref[0:1, 0:1]
 
     def gram(at, tile):
         row = lax.broadcasted_iota(jnp.int32, (kept, tile), 0)
         lane = lax.broadcasted_iota(jnp.int32, (kept, tile), 1)
-        value = early_ref[:, at:at + tile] + gram_columns(all_ref, kept, at, tile)
+        value = early_ref[:, at:at + tile] + gram_columns(parts, 0, kept, at, tile)
         a_ref[:, at:at + tile] = value * scale + jnp.where(row == lane + at, 1.0, 0.0)
 
     block = slice(0, PANEL)
-    corner = early_ref[block, block] + dot32(all_ref[block, :], all_ref[block, :], NT)
+    corner = early_ref[block, block] + gram_columns(parts, 0, PANEL, 0, PANEL)
     row = lax.broadcasted_iota(jnp.int32, (PANEL, PANEL), 0)
     lane = lax.broadcasted_iota(jnp.int32, (PANEL, PANEL), 1)
     next_ref[...] = corner * scale + jnp.where(row == lane, 1.0, 0.0)
@@ -398,14 +417,15 @@
 def first_part(side, early, squares, pieces, rows, features, last):
     kept = early.shape[0]
     count = len(flat(pieces))
-    all_scratch, sem_scratch = piece_scratch(pieces, kept)
+    all_scratch, sem_scratch = piece_scratch(halves(pieces), kept)
     vmem = pl.BlockSpec(memory_space=pltpu.VMEM)
 
     def body(*refs):
         side_ref, refs, sem = refs[0], refs[1:-1], refs[-1]
-        for copy in place_pieces(pieces, refs[2:count + 2], side_ref[0], refs[count + 6], sem):
+        copies, parts = join_pieces(pieces, refs[2:count + 2], side_ref[0], refs[count + 6], sem)
+        for copy in copies:
             copy.wait()
-        first_kernel(float(features), rows, last, *refs)
+        first_kernel(float(features), rows, last, parts, *refs)
 
     return pl.pallas_call(
         body,
@@ -415,7 +435,7 @@
             factors_shape(last),
             jax.ShapeDtypeStruct((PANEL, PANEL), jnp.float32),
         ],
-        in_specs=[pl.BlockSpec(memory_space=pltpu.SMEM)] + [vmem] * 2 + [pl.BlockSpec(memory_space=pl.ANY)] * count,
+        in_specs=[pl.BlockSpec(memory_space=pltpu.SMEM)] + [vmem] * 2 + piece_specs(pieces),
         out_specs=[vmem] * 4,
         scratch_shapes=[
             all_scratch,
@@ -468,10 +488,10 @@
     )(a, factors, follow)
 
 
-def last_kernel(chips, begin, middle, copies, flags_ref, *refs):
+def last_kernel(chips, begin, middle, copies, parts, flags_ref, *refs):
     projected, refs = refs[:chips], refs[chips:]
     scale_ref, whole_ref, early_ref, start_ref, mid_ref, start_next_ref = refs[:6]
-    out_ref, index_ref, wide_out_ref, all_ref, late_ref, a_ref, next_ref = refs[-10:-3]
+    out_ref, index_ref, wide_out_ref, _, late_ref, a_ref, next_ref = refs[-10:-3]
     work = refs[-3:]
     own, features = out_ref.shape
     blocks = flags_ref.shape[0]
@@ -508,7 +528,12 @@
 
     def make_right():
         whole = jnp.concatenate([part[...] for part in projected], axis=1)
-        right = dot32(jnp.concatenate(split3(whole), axis=0), all_ref[:kept, :], NT)
+        stacked = jnp.concatenate(split3(whole), axis=0)
+        right, low = None, 0
+        for part in parts:
+            high = low + part.shape[1]
+            value = dot32(stacked[:, low:high], part[:kept, :], NT)
+            right, low = value if right is None else right + value, high
         held["right"] = right[:own] + right[own:2 * own] + right[2 * own:]
 
     def forward(p):
@@ -529,15 +554,13 @@
             value = base - dot_small(held["back"], factor(p), NT)
             held["back"] = jnp.concatenate([value, held["back"]], axis=1)
 
-    def await_pieces():
-        for copy in copies:
-            copy.wait()
-
+    for copy in copies:
+        copy.wait()
     for p in range(middle, last):
         tasks = settle(p - 1)
         if p == last - 1:
-            tasks += [await_pieces, make_right] + [functools.partial(forward, q) for q in range(p)]
-            tasks += [functools.partial(scaled, q) for q in range(p)]
+            tasks = [make_right] + [functools.partial(forward, q) for q in range(p - 1)] + tasks
+            tasks += [functools.partial(forward, p - 1)] + [functools.partial(scaled, q) for q in range(p)]
         panel(p, state, late_ref.at[p - middle], tasks)
     tasks = settle(last - 1)
     tasks += [functools.partial(forward, last - 1), functools.partial(scaled, last - 1)]
@@ -566,22 +589,23 @@
     chips = len(projected)
     kept = begun[1].shape[0]
     count = len(flat(pieces))
-    all_scratch, sem_scratch = piece_scratch(pieces, kept)
+    all_scratch, sem_scratch = piece_scratch(halves(pieces), kept)
     left = kept - (middle - 1) * PANEL
     vmem = pl.BlockSpec(memory_space=pltpu.VMEM)
-    anywhere = pl.BlockSpec(memory_space=pl.ANY)
 
     def body(*refs):
         refs, sem = refs[:-1], refs[-1]
         side_ref, refs = refs[0], refs[1:]
         ins = 1 + chips + len(begun)
-        copies = place_pieces(pieces, refs[ins:ins + count], side_ref[0], refs[ins + count + 3], sem)
-        last_kernel(chips, begin, middle, copies, *refs)
+        copies, parts = join_pieces(pieces, refs[ins:ins + count], side_ref[0], refs[ins + count + 3], sem)
+        last_kernel(chips, begin, middle, copies, parts, *refs)
 
     return pl.pallas_call(
         body,
         out_shape=jax.ShapeDtypeStruct((own, features), jnp.bfloat16),
-        in_specs=[pl.BlockSpec(memory_space=pltpu.SMEM)] * 2 + [vmem] * (chips + len(begun)) + [anywhere] * count,
+        in_specs=[pl.BlockSpec(memory_space=pltpu.SMEM)] * 2
+        + [vmem] * (chips + len(begun))
+        + piece_specs(pieces),
         out_specs=vmem,
         scratch_shapes=[
             pltpu.SMEM((blocks + 1,), jnp.int32),

time: 59 us -> 57.9 us (0.981)
  Pallas kernels: 30.6 us -> 29.3 us
    pallas_call x1, Pallas kernels: 10.6 us -> 9.56 us  [last_part(): pl.pallas_call(body, out_shape=jax.ShapeDtypeStruct((own, features), jnp....]
  transfers between devices with their start and end apart: 16 -> 16, of which waited for: 2 -> 3; matrix products, arithmetic and copies ran while one was open for 0% -> 0% of each run, Pallas kernels for 30% -> 30%
where the time goes in v3:
time: 57.9 us; the launch traced here: 57.8 us
  Pallas kernels  29.3 us (51%)
  starting transfers between devices  15.4 us (27%)
  waiting for transfers between devices  10.2 us (18%)
  matrix products  1.71 us (3%)
  local copies, waits for them, and re-layouts  0.76 us (1%)
    ppermute x15, starting transfers between devices, swap(): return lax.ppermute(x, 'dp', [(d, d ^ k) for d in range(n)])  13.5 us
    pallas_call x1, Pallas kernels, first_part(): pl.pallas_call(body, out_shape=[jax.ShapeDtypeStruct((kept, kept), jnp.fl...  11.7 us
    ppermute x15, waiting for transfers between devices, swap(): return lax.ppermute(x, 'dp', [(d, d ^ k) for d in range(n)])  10.2 us
    pallas_call x1, Pallas kernels, last_part(): pl.pallas_call(body, out_shape=jax.ShapeDtypeStruct((own, features), jnp....  9.56 us
    pallas_call x1, Pallas kernels, middle_part(): pl.pallas_call(functools.partial(middle_kernel, first, last), out_shape=[...  3.94 us
    pallas_call x1, Pallas kernels, select_kept(): pl.pallas_call(select_kernel, out_shape=[jax.ShapeDtypeStruct((kept + EXT...  2.39 us
    ppermute x1, starting transfers between devices, level(): lax.ppermute(x, 'section', [(d, d ^ 1) for d in range(mesh.shape['section...  1.97 us
    pallas_call x1, Pallas kernels, early_gram(): pl.pallas_call(body, out_shape=[jax.ShapeDtypeStruct((kept, kept), jnp.fl...  1.72 us
  transfers between devices with their start and end apart: 16, of which 3 were waited for; matrix products, arithmetic and copies ran while one was open for 0% of the time, Pallas kernels for 30%

profile of v3, /device:TPU:0, one launch (start us, length us, event | category | flops | bytes accessed | tf_op | source)
XLA Modules:
  0.0 57.8 jit_solution(17891657407926383737)
XLA Ops:
  0.0 0.0 copy-start
  0.0 0.7 %copy-done = s32[64]{0:T(128)S(1)} copy-done((s32[64]{0:T(128)S(1)}, s32[64]{0:T(128)}, u32[]{:S(2)}) %copy-start) | copy-done | bytes 280
  0.7 0.0 copy-start.2
  0.7 2.4 %select_kept.1 = (bf16[784,256]{1,0:T(8,128)(2,1)S(1)}, bf16[400,256]{1,0:T(8,128)(2,1)S(1)}) custom-call(s32[1]{0:T(128)} %bitcast.side_ref.refs_0_, s32[64]{0:T(128)S(1)} %copy-done, bf16[256,4096]{1,0:T(8,128)(2,1)} %refs_2_), custom_call_target="tpu_custom_call" | custom-call | tf_op jit(solution)/shard_map/select_kept/pallas_call | solution.py:90
  3.1 0.5 collective-permute-start.12
  3.6 3.5 %collective-permute-start.3 = (bf16[400,256]{1,0:T(8,128)(2,1)S(1)}, bf16[400,256]{1,0:T(8,128)(2,1)S(1)}, u32[]{:S(2)}, u32[]{:S(2)}) collective-permute-start(bf16[400,256]{1,0:T(8,128)(2,1)S(1)} %get-tuple-element.38), channel_id=1, source_target_pairs={{0,6},{1,7},{2,4},{3,5},{4,2},{5,3},{6,0},{7,1},{8,14},{9,15},{10,... | collective-permute-start | bytes 614408 | tf_op jit(solution)/shard_map/ppermute | solution.py:630
  7.1 0.2 collective-permute-start.2
  7.3 0.5 collective-permute-start
  7.8 0.3 collective-permute-start.1
  8.1 5.0 %collective-permute-done.3.refs_7_.refs_18_ = bf16[400,256]{1,0:T(8,128)(2,1)S(1)} collective-permute-done((bf16[400,256]{1,0:T(8,128)(2,1)S(1)}, bf16[400,256]{1,0:T(8,128)(2,1)S(1)}, u32[]{:S(2)}, u32[]{:S(2)}) %collective-permute-start.3) | collective-permute-done | bytes 204832 | tf_op jit(solution)/shard_map/ppermute | solution.py:630
  13.1 0.0 collective-permute-start.4
  13.1 0.0 collective-permute-done.2.refs_1_.refs_13_
  13.1 2.0 %collective-permute-start.7 = (bf16[400,256]{1,0:T(8,128)(2,1)S(1)}, bf16[400,256]{1,0:T(8,128)(2,1)S(1)}, u32[]{:S(2)}, u32[]{:S(2)}) collective-permute-start(bf16[400,256]{1,0:T(8,128)(2,1)S(1)} %collective-permute-done.3.refs_7_.refs_18_), channel_id=1, source_target_pairs={{0,8},{8,0},{16,24},{24,16},{1,9},{9,1},{17,25},{25,17},{2,10},{10... | collective-permute-start | bytes 614408 | tf_op jit(solution)/shard_map/ppermute | solution.py:633
  15.1 1.7 %early_gram.1 = (f32[768,768]{1,0:T(8,128)S(1)}, f32[8,128]{1,0:T(8,128)S(1)}, bf16[256,4096]{1,0:T(8,128)(2,1)S(1)}) custom-call(bf16[784,256]{1,0:T(8,128)(2,1)S(1)} %get-tuple-element.34.refs_0_.refs_12_, bf16[784,256]{1,0:T(8,128)(2,1)S(1)} %collective-permute-done.2.refs_1_.refs_13_, bf16[256,4096]{1,0:T(8,128)(2,1)} %refs_2_), custom_call_target="tpu_custom_call" | custom-call | tf_op jit(solution)/shard_map/early_gram/pallas_call | solution.py:375
  16.8 4.9 %collective-permute-done.refs_3_.refs_14_ = bf16[784,256]{1,0:T(8,128)(2,1)S(1)} collective-permute-done((bf16[784,256]{1,0:T(8,128)(2,1)S(1)}, bf16[784,256]{1,0:T(8,128)(2,1)S(1)}, u32[]{:S(2)}, u32[]{:S(2)}) %collective-permute-start) | collective-permute-done | bytes 401440 | tf_op jit(solution)/shard_map/ppermute | solution.py:630
  21.7 0.0 collective-permute-done.1.refs_5_.refs_16_
  21.7 0.0 collective-permute-done.4.refs_9_.refs_20_
  21.7 0.0 collective-permute-start.5
  21.7 0.0 collective-permute-done.7.refs_8_.refs_19_
  21.7 0.5 collective-permute-start.8
  22.2 0.1 collective-permute-start.6
  22.3 0.0 copy-done.2
  22.3 1.4 %collective-permute-start.10 = (bf16[32,4096]{1,0:T(8,128)(2,1)S(1)}, bf16[32,4096]{1,0:T(8,128)(2,1)S(1)}, u32[]{:S(2)}, u32[]{:S(2)}) collective-permute-start(bf16[32,4096]{1,0:T(8,128)(2,1)S(1)} %copy-done.2), channel_id=1, source_target_pairs={{0,4},{1,5},{2,6},{3,7},{4,0},{5,1},{6,2},{7,3},{8,12},{9,13},{10,... | collective-permute-start | bytes 786440 | tf_op jit(solution)/shard_map/ppermute | solution.py:630
  23.7 0.0 collective-permute-done.8.refs_10_.refs_21_
  23.7 2.3 %collective-permute-start.11 = (bf16[32,4096]{1,0:T(8,128)(2,1)S(1)}, bf16[32,4096]{1,0:T(8,128)(2,1)S(1)}, u32[]{:S(2)}, u32[]{:S(2)}) collective-permute-start(bf16[32,4096]{1,0:T(8,128)(2,1)S(1)} %copy-done.2), channel_id=1, source_target_pairs={{0,6},{1,7},{2,4},{3,5},{4,2},{5,3},{6,0},{7,1},{8,14},{9,15},{10,... | collective-permute-start | bytes 786440 | tf_op jit(solution)/shard_map/ppermute | solution.py:630
  26.1 0.0 collective-permute-done.5.refs_4_.refs_15_
  26.1 0.5 collective-permute-start.9
  26.6 0.0 collective-permute-done.6.refs_6_.refs_17_
  26.6 11.7 %gram_and_first_panels.1 = (f32[768,768]{1,0:T(8,128)S(1)}, f32[8,128]{1,0:T(8,128)S(1)}, f32[3,2,128,128]{3,2,1,0:T(8,128)S(1)}, f32[128,128]{1,0:T(8,128)S(1)}) custom-call(s32[1]{0:T(128)} %bitcast.side_ref.refs_0_, f32[768,768]{1,0:T(8,128)S(1)} %get-tuple-element.39.refs_1_, f32[8,128]{1,0:T(8,128)S(1)} %get-tuple-element.40.refs_2_, ...), custom_call_target="tpu_custom_call" | custom-call | tf_op jit(solution)/shard_map/gram_and_first_panels/pallas_call | solution.py:430
  38.3 0.0 collective-permute-done.10
  38.3 0.0 collective-permute-done.11
  38.3 0.2 collective-permute-done.9
  38.6 0.0 collective-permute-done.12
  38.7 0.9 %fusion.1 = f32[128,256]{1,0:T(8,128)S(1)} fusion(bf16[128,4096]{1,0:T(8,128)(2,1)S(1)} %constant_dynamic-update-slice_fusion, bf16[256,4096]{1,0:T(8,128)(2,1)S(1)} %get-tuple-element.50), kind=kOutput, calls=%fused_computation.6 | convolution fusion | flops 268435456 | bytes 3276800 | tf_op jit(solution)/shard_map/dot_general | solution.py:672
  39.6 0.8 %fusion.2 = f32[128,256]{1,0:T(8,128)S(1)} fusion(bf16[128,4096]{1,0:T(8,128)(2,1)S(1)} %constant_dynamic-update-slice_fusion, bf16[256,4096]{1,0:T(8,128)(2,1)S(1)} %collective-permute-done.12), kind=kOutput, calls=%fused_computation.7 | convolution fusion | flops 268435456 | bytes 3276800 | tf_op jit(solution)/shard_map/dot_general | solution.py:672
  40.4 0.0 copy-start.1
  40.5 1.6 %collective-permute-start.13 = (f32[32,512]{1,0:T(8,128)S(1)}, f32[32,512]{1,0:T(8,128)S(1)}, u32[]{:S(2)}, u32[]{:S(2)}) collective-permute-start(f32[32,512]{1,0:T(8,128)S(1)} %get-tuple-element.63), channel_id=1, source_target_pairs={{0,2},{1,3},{2,0},{3,1},{4,6},{5,7},{6,4},{7,5},{8,10},{9,11},{10,... | collective-permute-start | bytes 196616 | tf_op jit(solution)/shard_map/ppermute | solution.py:630
  42.0 0.6 %collective-permute-start.14 = (f32[32,512]{1,0:T(8,128)S(1)}, f32[32,512]{1,0:T(8,128)S(1)}, u32[]{:S(2)}, u32[]{:S(2)}) collective-permute-start(f32[32,512]{1,0:T(8,128)S(1)} %get-tuple-element.62), channel_id=1, source_target_pairs={{0,4},{1,5},{2,6},{3,7},{4,0},{5,1},{6,2},{7,3},{8,12},{9,13},{10,... | collective-permute-start | bytes 196616 | tf_op jit(solution)/shard_map/ppermute | solution.py:630
  42.6 1.4 %collective-permute-start.15 = (f32[32,512]{1,0:T(8,128)S(1)}, f32[32,512]{1,0:T(8,128)S(1)}, u32[]{:S(2)}, u32[]{:S(2)}) collective-permute-start(f32[32,512]{1,0:T(8,128)S(1)} %get-tuple-element.61), channel_id=1, source_target_pairs={{0,6},{1,7},{2,4},{3,5},{4,2},{5,3},{6,0},{7,1},{8,14},{9,15},{10,... | collective-permute-start | bytes 196616 | tf_op jit(solution)/shard_map/ppermute | solution.py:630
  44.0 3.9 %middle_panels.1 = (f32[512,512]{1,0:T(8,128)S(1)}, f32[1,2,128,128]{3,2,1,0:T(8,128)S(1)}, f32[128,128]{1,0:T(8,128)S(1)}) custom-call(f32[768,768]{1,0:T(8,128)S(1)} %get-tuple-element.55.start_ref.refs_7_, f32[3,2,128,128]{3,2,1,0:T(8,128)S(1)} %get-tuple-element.56.early_ref.refs_8_, f32[128,128]{1,0:T(8,128)S(1)} %get-tuple-element.57.start_next_ref), custom_call_target="tpu_custom_call" | custom-call | tf_op jit(solution)/shard_map/middle_panels/pallas_call | solution.py:476
  48.0 0.0 collective-permute-done.13.refs_3_
  48.0 0.0 collective-permute-done.14.refs_4_
  48.0 0.0 collective-permute-done.15.refs_5_
  48.0 0.0 copy-done.1
  48.0 9.6 %last_panels_and_solution.1 = bf16[32,4096]{1,0:T(8,128)(2,1)} custom-call(s32[1]{0:T(128)} %bitcast.side_ref.refs_0_, s32[64]{0:T(128)S(1)} %copy-done.1, f32[32,512]{1,0:T(8,128)S(1)} %get-tuple-element.64.refs_2_, f32[32,512]{1,0:T(8,128)S(1)} %collective-permute-done.13.refs_3_, f32[32,512]{1,0:T(8,128)S(1)} %collective-permute-done.14.refs_4_, ...), custom_call_target="tpu_custom_call" | custom-call | tf_op jit(solution)/shard_map/last_panels_and_solution/pallas_call | solution.py:603
  (6 shorter events, 0.1 us)
Async XLA Ops:
  0.0 0.7 %copy-start = (s32[64]{0:T(128)S(1)}, s32[64]{0:T(128)}, u32[]{:S(2)}) copy-start(s32[64]{0:T(128)} %refs_1_.1) | copy-start | bytes 772
  0.7 21.6 %copy-start.2 = (bf16[32,4096]{1,0:T(8,128)(2,1)S(1)}, bf16[32,4096]{1,0:T(8,128)(2,1)}, u32[]{:S(2)}) copy-start(bf16[32,4096]{1,0:T(8,128)(2,1)} %param.4) | copy-start | bytes 786436
  3.1 35.5 %collective-permute-start.12 = (bf16[256,4096]{1,0:T(8,128)(2,1)}, bf16[256,4096]{1,0:T(8,128)(2,1)S(1)}, u32[]{:S(2)}, u32[]{:S(2)}) collective-permute-start(bf16[256,4096]{1,0:T(8,128)(2,1)} %refs_2_), channel_id=1, source_target_pairs={{0,1},{1,0},{2,3},{3,2},{4,5},{5,4},{6,7},{7,6},{8,9},{9,8},{10,11... | collective-permute-start | bytes 6291464 | tf_op jit(solution)/shard_map/ppermute | solution.py:630
  3.6 9.5 %collective-permute-start.3 = (bf16[400,256]{1,0:T(8,128)(2,1)S(1)}, bf16[400,256]{1,0:T(8,128)(2,1)S(1)}, u32[]{:S(2)}, u32[]{:S(2)}) collective-permute-start(bf16[400,256]{1,0:T(8,128)(2,1)S(1)} %get-tuple-element.38), channel_id=1, source_target_pairs={{0,6},{1,7},{2,4},{3,5},{4,2},{5,3},{6,0},{7,1},{8,14},{9,15},{10,... | collective-permute-start | bytes 614408 | tf_op jit(solution)/shard_map/ppermute | solution.py:630
  7.1 6.0 %collective-permute-start.2 = (bf16[784,256]{1,0:T(8,128)(2,1)S(1)}, bf16[784,256]{1,0:T(8,128)(2,1)S(1)}, u32[]{:S(2)}, u32[]{:S(2)}) collective-permute-start(bf16[784,256]{1,0:T(8,128)(2,1)S(1)} %get-tuple-element.34.refs_0_.refs_12_), channel_id=1, source_target_pairs={{0,1},{1,0},{2,3},{3,2},{4,5},{5,4},{6,7},{7,6},{8,9},{9,8},{10,11... | collective-permute-start | bytes 1204232 | tf_op jit(solution)/shard_map/ppermute | solution.py:630
  7.3 14.4 %collective-permute-start = (bf16[784,256]{1,0:T(8,128)(2,1)S(1)}, bf16[784,256]{1,0:T(8,128)(2,1)S(1)}, u32[]{:S(2)}, u32[]{:S(2)}) collective-permute-start(bf16[784,256]{1,0:T(8,128)(2,1)S(1)} %get-tuple-element.34.refs_0_.refs_12_), channel_id=1, source_target_pairs={{0,2},{1,3},{2,0},{3,1},{4,6},{5,7},{6,4},{7,5},{8,10},{9,11},{10,... | collective-permute-start | bytes 1204232 | tf_op jit(solution)/shard_map/ppermute | solution.py:630
  7.8 13.9 %collective-permute-start.1 = (bf16[784,256]{1,0:T(8,128)(2,1)S(1)}, bf16[784,256]{1,0:T(8,128)(2,1)S(1)}, u32[]{:S(2)}, u32[]{:S(2)}) collective-permute-start(bf16[784,256]{1,0:T(8,128)(2,1)S(1)} %get-tuple-element.34.refs_0_.refs_12_), channel_id=1, source_target_pairs={{0,4},{1,5},{2,6},{3,7},{4,0},{5,1},{6,2},{7,3},{8,12},{9,13},{10,... | collective-permute-start | bytes 1204232 | tf_op jit(solution)/shard_map/ppermute | solution.py:630
  13.1 8.6 %collective-permute-start.4 = (bf16[400,256]{1,0:T(8,128)(2,1)S(1)}, bf16[400,256]{1,0:T(8,128)(2,1)S(1)}, u32[]{:S(2)}, u32[]{:S(2)}) collective-permute-start(bf16[400,256]{1,0:T(8,128)(2,1)S(1)} %collective-permute-done.3.refs_7_.refs_18_), channel_id=1, source_target_pairs={{0,1},{1,0},{2,3},{3,2},{4,5},{5,4},{6,7},{7,6},{8,9},{9,8},{10,11... | collective-permute-start | bytes 614408 | tf_op jit(solution)/shard_map/ppermute | solution.py:630
  13.1 8.6 %collective-permute-start.7 = (bf16[400,256]{1,0:T(8,128)(2,1)S(1)}, bf16[400,256]{1,0:T(8,128)(2,1)S(1)}, u32[]{:S(2)}, u32[]{:S(2)}) collective-permute-start(bf16[400,256]{1,0:T(8,128)(2,1)S(1)} %collective-permute-done.3.refs_7_.refs_18_), channel_id=1, source_target_pairs={{0,8},{8,0},{16,24},{24,16},{1,9},{9,1},{17,25},{25,17},{2,10},{10... | collective-permute-start | bytes 614408 | tf_op jit(solution)/shard_map/ppermute | solution.py:633
  21.7 4.4 %collective-permute-start.5 = (bf16[784,256]{1,0:T(8,128)(2,1)S(1)}, bf16[784,256]{1,0:T(8,128)(2,1)S(1)}, u32[]{:S(2)}, u32[]{:S(2)}) collective-permute-start(bf16[784,256]{1,0:T(8,128)(2,1)S(1)} %collective-permute-done.refs_3_.refs_14_), channel_id=1, source_target_pairs={{0,1},{1,0},{2,3},{3,2},{4,5},{5,4},{6,7},{7,6},{8,9},{9,8},{10,11... | collective-permute-start | bytes 1204232 | tf_op jit(solution)/shard_map/ppermute | solution.py:630
  21.7 2.0 %collective-permute-start.8 = (bf16[400,256]{1,0:T(8,128)(2,1)S(1)}, bf16[400,256]{1,0:T(8,128)(2,1)S(1)}, u32[]{:S(2)}, u32[]{:S(2)}) collective-permute-start(bf16[400,256]{1,0:T(8,128)(2,1)S(1)} %collective-permute-done.7.refs_8_.refs_19_), channel_id=1, source_target_pairs={{0,1},{1,0},{2,3},{3,2},{4,5},{5,4},{6,7},{7,6},{8,9},{9,8},{10,11... | collective-permute-start | bytes 614408 | tf_op jit(solution)/shard_map/ppermute | solution.py:630
  22.2 4.4 %collective-permute-start.6 = (bf16[784,256]{1,0:T(8,128)(2,1)S(1)}, bf16[784,256]{1,0:T(8,128)(2,1)S(1)}, u32[]{:S(2)}, u32[]{:S(2)}) collective-permute-start(bf16[784,256]{1,0:T(8,128)(2,1)S(1)} %collective-permute-done.1.refs_5_.refs_16_), channel_id=1, source_target_pairs={{0,1},{1,0},{2,3},{3,2},{4,5},{5,4},{6,7},{7,6},{8,9},{9,8},{10,11... | collective-permute-start | bytes 1204232 | tf_op jit(solution)/shard_map/ppermute | solution.py:630
  22.3 16.0 %collective-permute-start.10 = (bf16[32,4096]{1,0:T(8,128)(2,1)S(1)}, bf16[32,4096]{1,0:T(8,128)(2,1)S(1)}, u32[]{:S(2)}, u32[]{:S(2)}) collective-permute-start(bf16[32,4096]{1,0:T(8,128)(2,1)S(1)} %copy-done.2), channel_id=1, source_target_pairs={{0,4},{1,5},{2,6},{3,7},{4,0},{5,1},{6,2},{7,3},{8,12},{9,13},{10,... | collective-permute-start | bytes 786440 | tf_op jit(solution)/shard_map/ppermute | solution.py:630
  23.7 14.6 %collective-permute-start.11 = (bf16[32,4096]{1,0:T(8,128)(2,1)S(1)}, bf16[32,4096]{1,0:T(8,128)(2,1)S(1)}, u32[]{:S(2)}, u32[]{:S(2)}) collective-permute-start(bf16[32,4096]{1,0:T(8,128)(2,1)S(1)} %copy-done.2), channel_id=1, source_target_pairs={{0,6},{1,7},{2,4},{3,5},{4,2},{5,3},{6,0},{7,1},{8,14},{9,15},{10,... | collective-permute-start | bytes 786440 | tf_op jit(solution)/shard_map/ppermute | solution.py:630
  26.1 12.5 %collective-permute-start.9 = (bf16[32,4096]{1,0:T(8,128)(2,1)S(1)}, bf16[32,4096]{1,0:T(8,128)(2,1)S(1)}, u32[]{:S(2)}, u32[]{:S(2)}) collective-permute-start(bf16[32,4096]{1,0:T(8,128)(2,1)S(1)} %copy-done.2), channel_id=1, source_target_pairs={{0,2},{1,3},{2,0},{3,1},{4,6},{5,7},{6,4},{7,5},{8,10},{9,11},{10,... | collective-permute-start | bytes 786440 | tf_op jit(solution)/shard_map/ppermute | solution.py:630
  40.4 7.6 %copy-start.1 = (s32[64]{0:T(128)S(1)}, s32[64]{0:T(128)}, u32[]{:S(2)}) copy-start(s32[64]{0:T(128)} %refs_1_.1) | copy-start | bytes 772
  40.5 7.5 %collective-permute-start.13 = (f32[32,512]{1,0:T(8,128)S(1)}, f32[32,512]{1,0:T(8,128)S(1)}, u32[]{:S(2)}, u32[]{:S(2)}) collective-permute-start(f32[32,512]{1,0:T(8,128)S(1)} %get-tuple-element.63), channel_id=1, source_target_pairs={{0,2},{1,3},{2,0},{3,1},{4,6},{5,7},{6,4},{7,5},{8,10},{9,11},{10,... | collective-permute-start | bytes 196616 | tf_op jit(solution)/shard_map/ppermute | solution.py:630
  42.0 6.0 %collective-permute-start.14 = (f32[32,512]{1,0:T(8,128)S(1)}, f32[32,512]{1,0:T(8,128)S(1)}, u32[]{:S(2)}, u32[]{:S(2)}) collective-permute-start(f32[32,512]{1,0:T(8,128)S(1)} %get-tuple-element.62), channel_id=1, source_target_pairs={{0,4},{1,5},{2,6},{3,7},{4,0},{5,1},{6,2},{7,3},{8,12},{9,13},{10,... | collective-permute-start | bytes 196616 | tf_op jit(solution)/shard_map/ppermute | solution.py:630
  42.6 5.4 %collective-permute-start.15 = (f32[32,512]{1,0:T(8,128)S(1)}, f32[32,512]{1,0:T(8,128)S(1)}, u32[]{:S(2)}, u32[]{:S(2)}) collective-permute-start(f32[32,512]{1,0:T(8,128)S(1)} %get-tuple-element.61), channel_id=1, source_target_pairs={{0,6},{1,7},{2,4},{3,5},{4,2},{5,3},{6,0},{7,1},{8,14},{9,15},{10,... | collective-permute-start | bytes 196616 | tf_op jit(solution)/shard_map/ppermute | solution.py:630

commit v4 on v3

--- a/solution.py
+++ b/solution.py
@@ -347,11 +347,11 @@
 
 
 def square_sum(parts, kept, rows):
-    total = jnp.float32(0.0)
+    total = jnp.zeros((EXTRA, 128), jnp.float32)
     for part in parts:
         for k in range(0, part.shape[1], rows):
-            total = total + jnp.sum(part[kept:, k:k + 1].astype(jnp.float32))
-    return total
+            total = total + part[kept:, k:k + 128].astype(jnp.float32)
+    return jnp.broadcast_to(jnp.sum(total, axis=0, keepdims=True), (8, 128))
 
 
 def early_gram(pieces, source):
@@ -367,7 +367,7 @@
         fetch.start()
         for copy in copies:
             copy.wait()
-        squares_ref[...] = jnp.full(squares_ref.shape, square_sum([all_ref], kept, rows), jnp.float32)
+        squares_ref[...] = square_sum([all_ref], kept, rows)
         for at in range(0, kept, 256):
             out_ref[:, at:at + 256] = gram_columns([all_ref], 0, kept, at, 256)
         fetch.wait()
@@ -566,9 +566,11 @@
     tasks += [functools.partial(forward, last - 1), functools.partial(scaled, last - 1)]
     tasks += [functools.partial(backward, p) for p in reversed(range(last + 1))]
     lower, upper = factor_panel(next_ref[...], tasks)
-    tail = dot_small(dot_small(held["right"], lower, NT), upper)
+    lifted = dot_small(upper, held["back"][own:, :at])
+    inner_part = dot_small(held["right"], lower, NT)
+    tail = dot_small(inner_part, upper)
     scale = scale_ref[0:1, 0:1]
-    front = held["back"][:own, :at] + dot_small(tail, held["back"][own:, :at])
+    front = held["back"][:own, :at] + dot_small(inner_part, lifted)
     answer = [front[:, c:c + PANEL] * scale for c in range(0, at, PANEL)] + [tail * scale]
     place = lax.broadcasted_iota(jnp.int32, (own, 128), 1) // width
     for i in range(KEEP_BLK):

time: 57.9 us -> 58.2 us (level)
  no operation moved by 1% of the time
where the time goes in v4:
time: 58.2 us; the launch traced here: 58 us
  Pallas kernels  29.6 us (51%)
  starting transfers between devices  15.4 us (26%)
  waiting for transfers between devices  10.2 us (18%)
  matrix products  1.7 us (3%)
  local copies, waits for them, and re-layouts  0.76 us (1%)
    ppermute x15, starting transfers between devices, swap(): return lax.ppermute(x, 'dp', [(d, d ^ k) for d in range(n)])  13.5 us
    pallas_call x1, Pallas kernels, first_part(): pl.pallas_call(body, out_shape=[jax.ShapeDtypeStruct((kept, kept), jnp.fl...  11.7 us
    ppermute x15, waiting for transfers between devices, swap(): return lax.ppermute(x, 'dp', [(d, d ^ k) for d in range(n)])  10.2 us
    pallas_call x1, Pallas kernels, last_part(): pl.pallas_call(body, out_shape=jax.ShapeDtypeStruct((own, features), jnp....  9.82 us
    pallas_call x1, Pallas kernels, middle_part(): pl.pallas_call(functools.partial(middle_kernel, first, last), out_shape=[...  3.97 us
    pallas_call x1, Pallas kernels, select_kept(): pl.pallas_call(select_kernel, out_shape=[jax.ShapeDtypeStruct((kept + EXT...  2.39 us
    ppermute x1, starting transfers between devices, level(): lax.ppermute(x, 'section', [(d, d ^ 1) for d in range(mesh.shape['section...  1.97 us
    pallas_call x1, Pallas kernels, early_gram(): pl.pallas_call(body, out_shape=[jax.ShapeDtypeStruct((kept, kept), jnp.fl...  1.72 us
  transfers between devices with their start and end apart: 16, of which 3 were waited for; matrix products, arithmetic and copies ran while one was open for 0% of the time, Pallas kernels for 30%

profile of v4, /device:TPU:0, one launch (start us, length us, event | category | flops | bytes accessed | tf_op | source)
XLA Modules:
  0.0 58.0 jit_solution(12197017437683671556)
XLA Ops:
  0.0 0.0 copy-start
  0.0 0.7 %copy-done = s32[64]{0:T(128)S(1)} copy-done((s32[64]{0:T(128)S(1)}, s32[64]{0:T(128)}, u32[]{:S(2)}) %copy-start) | copy-done | bytes 280
  0.7 0.0 copy-start.2
  0.7 2.4 %select_kept.1 = (bf16[784,256]{1,0:T(8,128)(2,1)S(1)}, bf16[400,256]{1,0:T(8,128)(2,1)S(1)}) custom-call(s32[1]{0:T(128)} %bitcast.side_ref.refs_0_, s32[64]{0:T(128)S(1)} %copy-done, bf16[256,4096]{1,0:T(8,128)(2,1)} %refs_2_), custom_call_target="tpu_custom_call" | custom-call | tf_op jit(solution)/shard_map/select_kept/pallas_call | solution.py:90
  3.1 0.5 collective-permute-start.12
  3.6 3.5 %collective-permute-start.3 = (bf16[400,256]{1,0:T(8,128)(2,1)S(1)}, bf16[400,256]{1,0:T(8,128)(2,1)S(1)}, u32[]{:S(2)}, u32[]{:S(2)}) collective-permute-start(bf16[400,256]{1,0:T(8,128)(2,1)S(1)} %get-tuple-element.38), channel_id=1, source_target_pairs={{0,6},{1,7},{2,4},{3,5},{4,2},{5,3},{6,0},{7,1},{8,14},{9,15},{10,... | collective-permute-start | bytes 614408 | tf_op jit(solution)/shard_map/ppermute | solution.py:632
  7.1 0.2 collective-permute-start.2
  7.3 0.5 collective-permute-start
  7.8 0.3 collective-permute-start.1
  8.1 5.0 %collective-permute-done.3.refs_7_.refs_18_ = bf16[400,256]{1,0:T(8,128)(2,1)S(1)} collective-permute-done((bf16[400,256]{1,0:T(8,128)(2,1)S(1)}, bf16[400,256]{1,0:T(8,128)(2,1)S(1)}, u32[]{:S(2)}, u32[]{:S(2)}) %collective-permute-start.3) | collective-permute-done | bytes 204832 | tf_op jit(solution)/shard_map/ppermute | solution.py:632
  13.1 0.0 collective-permute-start.4
  13.1 0.0 collective-permute-done.2.refs_1_.refs_13_
  13.1 2.0 %collective-permute-start.7 = (bf16[400,256]{1,0:T(8,128)(2,1)S(1)}, bf16[400,256]{1,0:T(8,128)(2,1)S(1)}, u32[]{:S(2)}, u32[]{:S(2)}) collective-permute-start(bf16[400,256]{1,0:T(8,128)(2,1)S(1)} %collective-permute-done.3.refs_7_.refs_18_), channel_id=1, source_target_pairs={{0,8},{8,0},{16,24},{24,16},{1,9},{9,1},{17,25},{25,17},{2,10},{10... | collective-permute-start | bytes 614408 | tf_op jit(solution)/shard_map/ppermute | solution.py:635
  15.1 1.7 %early_gram.1 = (f32[768,768]{1,0:T(8,128)S(1)}, f32[8,128]{1,0:T(8,128)S(1)}, bf16[256,4096]{1,0:T(8,128)(2,1)S(1)}) custom-call(bf16[784,256]{1,0:T(8,128)(2,1)S(1)} %get-tuple-element.34.refs_0_.refs_12_, bf16[784,256]{1,0:T(8,128)(2,1)S(1)} %collective-permute-done.2.refs_1_.refs_13_, bf16[256,4096]{1,0:T(8,128)(2,1)} %refs_2_), custom_call_target="tpu_custom_call" | custom-call | tf_op jit(solution)/shard_map/early_gram/pallas_call | solution.py:375
  16.8 4.9 %collective-permute-done.refs_3_.refs_14_ = bf16[784,256]{1,0:T(8,128)(2,1)S(1)} collective-permute-done((bf16[784,256]{1,0:T(8,128)(2,1)S(1)}, bf16[784,256]{1,0:T(8,128)(2,1)S(1)}, u32[]{:S(2)}, u32[]{:S(2)}) %collective-permute-start) | collective-permute-done | bytes 401440 | tf_op jit(solution)/shard_map/ppermute | solution.py:632
  21.7 0.0 collective-permute-done.1.refs_5_.refs_16_
  21.7 0.0 collective-permute-done.4.refs_9_.refs_20_
  21.7 0.0 collective-permute-start.5
  21.7 0.0 collective-permute-done.7.refs_8_.refs_19_
  21.7 0.5 collective-permute-start.8
  22.2 0.1 collective-permute-start.6
  22.3 0.0 copy-done.2
  22.3 1.4 %collective-permute-start.10 = (bf16[32,4096]{1,0:T(8,128)(2,1)S(1)}, bf16[32,4096]{1,0:T(8,128)(2,1)S(1)}, u32[]{:S(2)}, u32[]{:S(2)}) collective-permute-start(bf16[32,4096]{1,0:T(8,128)(2,1)S(1)} %copy-done.2), channel_id=1, source_target_pairs={{0,4},{1,5},{2,6},{3,7},{4,0},{5,1},{6,2},{7,3},{8,12},{9,13},{10,... | collective-permute-start | bytes 786440 | tf_op jit(solution)/shard_map/ppermute | solution.py:632
  23.7 0.0 collective-permute-done.8.refs_10_.refs_21_
  23.7 2.3 %collective-permute-start.11 = (bf16[32,4096]{1,0:T(8,128)(2,1)S(1)}, bf16[32,4096]{1,0:T(8,128)(2,1)S(1)}, u32[]{:S(2)}, u32[]{:S(2)}) collective-permute-start(bf16[32,4096]{1,0:T(8,128)(2,1)S(1)} %copy-done.2), channel_id=1, source_target_pairs={{0,6},{1,7},{2,4},{3,5},{4,2},{5,3},{6,0},{7,1},{8,14},{9,15},{10,... | collective-permute-start | bytes 786440 | tf_op jit(solution)/shard_map/ppermute | solution.py:632
  26.1 0.0 collective-permute-done.5.refs_4_.refs_15_
  26.1 0.5 collective-permute-start.9
  26.6 0.0 collective-permute-done.6.refs_6_.refs_17_
  26.6 11.7 %gram_and_first_panels.1 = (f32[768,768]{1,0:T(8,128)S(1)}, f32[8,128]{1,0:T(8,128)S(1)}, f32[3,2,128,128]{3,2,1,0:T(8,128)S(1)}, f32[128,128]{1,0:T(8,128)S(1)}) custom-call(s32[1]{0:T(128)} %bitcast.side_ref.refs_0_, f32[768,768]{1,0:T(8,128)S(1)} %get-tuple-element.39.refs_1_, f32[8,128]{1,0:T(8,128)S(1)} %get-tuple-element.40.refs_2_, ...), custom_call_target="tpu_custom_call" | custom-call | tf_op jit(solution)/shard_map/gram_and_first_panels/pallas_call | solution.py:430
  38.3 0.0 collective-permute-done.10
  38.3 0.0 collective-permute-done.11
  38.3 0.3 collective-permute-done.9
  38.6 0.0 collective-permute-done.12
  38.7 0.9 %fusion.1 = f32[128,256]{1,0:T(8,128)S(1)} fusion(bf16[128,4096]{1,0:T(8,128)(2,1)S(1)} %constant_dynamic-update-slice_fusion, bf16[256,4096]{1,0:T(8,128)(2,1)S(1)} %get-tuple-element.50), kind=kOutput, calls=%fused_computation.6 | convolution fusion | flops 268435456 | bytes 3276800 | tf_op jit(solution)/shard_map/dot_general | solution.py:674
  39.6 0.8 %fusion.2 = f32[128,256]{1,0:T(8,128)S(1)} fusion(bf16[128,4096]{1,0:T(8,128)(2,1)S(1)} %constant_dynamic-update-slice_fusion, bf16[256,4096]{1,0:T(8,128)(2,1)S(1)} %collective-permute-done.12), kind=kOutput, calls=%fused_computation.7 | convolution fusion | flops 268435456 | bytes 3276800 | tf_op jit(solution)/shard_map/dot_general | solution.py:674
  40.4 0.0 copy-start.1
  40.5 1.6 %collective-permute-start.13 = (f32[32,512]{1,0:T(8,128)S(1)}, f32[32,512]{1,0:T(8,128)S(1)}, u32[]{:S(2)}, u32[]{:S(2)}) collective-permute-start(f32[32,512]{1,0:T(8,128)S(1)} %get-tuple-element.63), channel_id=1, source_target_pairs={{0,2},{1,3},{2,0},{3,1},{4,6},{5,7},{6,4},{7,5},{8,10},{9,11},{10,... | collective-permute-start | bytes 196616 | tf_op jit(solution)/shard_map/ppermute | solution.py:632
  42.0 0.6 %collective-permute-start.14 = (f32[32,512]{1,0:T(8,128)S(1)}, f32[32,512]{1,0:T(8,128)S(1)}, u32[]{:S(2)}, u32[]{:S(2)}) collective-permute-start(f32[32,512]{1,0:T(8,128)S(1)} %get-tuple-element.62), channel_id=1, source_target_pairs={{0,4},{1,5},{2,6},{3,7},{4,0},{5,1},{6,2},{7,3},{8,12},{9,13},{10,... | collective-permute-start | bytes 196616 | tf_op jit(solution)/shard_map/ppermute | solution.py:632
  42.6 1.4 %collective-permute-start.15 = (f32[32,512]{1,0:T(8,128)S(1)}, f32[32,512]{1,0:T(8,128)S(1)}, u32[]{:S(2)}, u32[]{:S(2)}) collective-permute-start(f32[32,512]{1,0:T(8,128)S(1)} %get-tuple-element.61), channel_id=1, source_target_pairs={{0,6},{1,7},{2,4},{3,5},{4,2},{5,3},{6,0},{7,1},{8,14},{9,15},{10,... | collective-permute-start | bytes 196616 | tf_op jit(solution)/shard_map/ppermute | solution.py:632
  44.0 4.0 %middle_panels.1 = (f32[512,512]{1,0:T(8,128)S(1)}, f32[1,2,128,128]{3,2,1,0:T(8,128)S(1)}, f32[128,128]{1,0:T(8,128)S(1)}) custom-call(f32[768,768]{1,0:T(8,128)S(1)} %get-tuple-element.55.start_ref.refs_7_, f32[3,2,128,128]{3,2,1,0:T(8,128)S(1)} %get-tuple-element.56.early_ref.refs_8_, f32[128,128]{1,0:T(8,128)S(1)} %get-tuple-element.57.start_next_ref), custom_call_target="tpu_custom_call" | custom-call | tf_op jit(solution)/shard_map/middle_panels/pallas_call | solution.py:476
  48.0 0.0 collective-permute-done.13.refs_3_
  48.0 0.0 collective-permute-done.14.refs_4_
  48.0 0.0 collective-permute-done.15.refs_5_
  48.0 0.0 copy-done.1
  48.0 9.8 %last_panels_and_solution.1 = bf16[32,4096]{1,0:T(8,128)(2,1)} custom-call(s32[1]{0:T(128)} %bitcast.side_ref.refs_0_, s32[64]{0:T(128)S(1)} %copy-done.1, f32[32,512]{1,0:T(8,128)S(1)} %get-tuple-element.64.refs_2_, f32[32,512]{1,0:T(8,128)S(1)} %collective-permute-done.13.refs_3_, f32[32,512]{1,0:T(8,128)S(1)} %collective-permute-done.14.refs_4_, ...), custom_call_target="tpu_custom_call" | custom-call | tf_op jit(solution)/shard_map/last_panels_and_solution/pallas_call | solution.py:605
  (6 shorter events, 0.1 us)
Async XLA Ops:
  0.0 0.7 %copy-start = (s32[64]{0:T(128)S(1)}, s32[64]{0:T(128)}, u32[]{:S(2)}) copy-start(s32[64]{0:T(128)} %refs_1_.1) | copy-start | bytes 772
  0.7 21.6 %copy-start.2 = (bf16[32,4096]{1,0:T(8,128)(2,1)S(1)}, bf16[32,4096]{1,0:T(8,128)(2,1)}, u32[]{:S(2)}) copy-start(bf16[32,4096]{1,0:T(8,128)(2,1)} %param.4) | copy-start | bytes 786436
  3.1 35.5 %collective-permute-start.12 = (bf16[256,4096]{1,0:T(8,128)(2,1)}, bf16[256,4096]{1,0:T(8,128)(2,1)S(1)}, u32[]{:S(2)}, u32[]{:S(2)}) collective-permute-start(bf16[256,4096]{1,0:T(8,128)(2,1)} %refs_2_), channel_id=1, source_target_pairs={{0,1},{1,0},{2,3},{3,2},{4,5},{5,4},{6,7},{7,6},{8,9},{9,8},{10,11... | collective-permute-start | bytes 6291464 | tf_op jit(solution)/shard_map/ppermute | solution.py:632
  3.6 9.5 %collective-permute-start.3 = (bf16[400,256]{1,0:T(8,128)(2,1)S(1)}, bf16[400,256]{1,0:T(8,128)(2,1)S(1)}, u32[]{:S(2)}, u32[]{:S(2)}) collective-permute-start(bf16[400,256]{1,0:T(8,128)(2,1)S(1)} %get-tuple-element.38), channel_id=1, source_target_pairs={{0,6},{1,7},{2,4},{3,5},{4,2},{5,3},{6,0},{7,1},{8,14},{9,15},{10,... | collective-permute-start | bytes 614408 | tf_op jit(solution)/shard_map/ppermute | solution.py:632
  7.1 6.0 %collective-permute-start.2 = (bf16[784,256]{1,0:T(8,128)(2,1)S(1)}, bf16[784,256]{1,0:T(8,128)(2,1)S(1)}, u32[]{:S(2)}, u32[]{:S(2)}) collective-permute-start(bf16[784,256]{1,0:T(8,128)(2,1)S(1)} %get-tuple-element.34.refs_0_.refs_12_), channel_id=1, source_target_pairs={{0,1},{1,0},{2,3},{3,2},{4,5},{5,4},{6,7},{7,6},{8,9},{9,8},{10,11... | collective-permute-start | bytes 1204232 | tf_op jit(solution)/shard_map/ppermute | solution.py:632
  7.3 14.4 %collective-permute-start = (bf16[784,256]{1,0:T(8,128)(2,1)S(1)}, bf16[784,256]{1,0:T(8,128)(2,1)S(1)}, u32[]{:S(2)}, u32[]{:S(2)}) collective-permute-start(bf16[784,256]{1,0:T(8,128)(2,1)S(1)} %get-tuple-element.34.refs_0_.refs_12_), channel_id=1, source_target_pairs={{0,2},{1,3},{2,0},{3,1},{4,6},{5,7},{6,4},{7,5},{8,10},{9,11},{10,... | collective-permute-start | bytes 1204232 | tf_op jit(solution)/shard_map/ppermute | solution.py:632
  7.8 13.9 %collective-permute-start.1 = (bf16[784,256]{1,0:T(8,128)(2,1)S(1)}, bf16[784,256]{1,0:T(8,128)(2,1)S(1)}, u32[]{:S(2)}, u32[]{:S(2)}) collective-permute-start(bf16[784,256]{1,0:T(8,128)(2,1)S(1)} %get-tuple-element.34.refs_0_.refs_12_), channel_id=1, source_target_pairs={{0,4},{1,5},{2,6},{3,7},{4,0},{5,1},{6,2},{7,3},{8,12},{9,13},{10,... | collective-permute-start | bytes 1204232 | tf_op jit(solution)/shard_map/ppermute | solution.py:632
  13.1 8.6 %collective-permute-start.4 = (bf16[400,256]{1,0:T(8,128)(2,1)S(1)}, bf16[400,256]{1,0:T(8,128)(2,1)S(1)}, u32[]{:S(2)}, u32[]{:S(2)}) collective-permute-start(bf16[400,256]{1,0:T(8,128)(2,1)S(1)} %collective-permute-done.3.refs_7_.refs_18_), channel_id=1, source_target_pairs={{0,1},{1,0},{2,3},{3,2},{4,5},{5,4},{6,7},{7,6},{8,9},{9,8},{10,11... | collective-permute-start | bytes 614408 | tf_op jit(solution)/shard_map/ppermute | solution.py:632
  13.1 8.6 %collective-permute-start.7 = (bf16[400,256]{1,0:T(8,128)(2,1)S(1)}, bf16[400,256]{1,0:T(8,128)(2,1)S(1)}, u32[]{:S(2)}, u32[]{:S(2)}) collective-permute-start(bf16[400,256]{1,0:T(8,128)(2,1)S(1)} %collective-permute-done.3.refs_7_.refs_18_), channel_id=1, source_target_pairs={{0,8},{8,0},{16,24},{24,16},{1,9},{9,1},{17,25},{25,17},{2,10},{10... | collective-permute-start | bytes 614408 | tf_op jit(solution)/shard_map/ppermute | solution.py:635
  21.7 4.4 %collective-permute-start.5 = (bf16[784,256]{1,0:T(8,128)(2,1)S(1)}, bf16[784,256]{1,0:T(8,128)(2,1)S(1)}, u32[]{:S(2)}, u32[]{:S(2)}) collective-permute-start(bf16[784,256]{1,0:T(8,128)(2,1)S(1)} %collective-permute-done.refs_3_.refs_14_), channel_id=1, source_target_pairs={{0,1},{1,0},{2,3},{3,2},{4,5},{5,4},{6,7},{7,6},{8,9},{9,8},{10,11... | collective-permute-start | bytes 1204232 | tf_op jit(solution)/shard_map/ppermute | solution.py:632
  21.7 2.0 %collective-permute-start.8 = (bf16[400,256]{1,0:T(8,128)(2,1)S(1)}, bf16[400,256]{1,0:T(8,128)(2,1)S(1)}, u32[]{:S(2)}, u32[]{:S(2)}) collective-permute-start(bf16[400,256]{1,0:T(8,128)(2,1)S(1)} %collective-permute-done.7.refs_8_.refs_19_), channel_id=1, source_target_pairs={{0,1},{1,0},{2,3},{3,2},{4,5},{5,4},{6,7},{7,6},{8,9},{9,8},{10,11... | collective-permute-start | bytes 614408 | tf_op jit(solution)/shard_map/ppermute | solution.py:632
  22.2 4.4 %collective-permute-start.6 = (bf16[784,256]{1,0:T(8,128)(2,1)S(1)}, bf16[784,256]{1,0:T(8,128)(2,1)S(1)}, u32[]{:S(2)}, u32[]{:S(2)}) collective-permute-start(bf16[784,256]{1,0:T(8,128)(2,1)S(1)} %collective-permute-done.1.refs_5_.refs_16_), channel_id=1, source_target_pairs={{0,1},{1,0},{2,3},{3,2},{4,5},{5,4},{6,7},{7,6},{8,9},{9,8},{10,11... | collective-permute-start | bytes 1204232 | tf_op jit(solution)/shard_map/ppermute | solution.py:632
  22.3 16.0 %collective-permute-start.10 = (bf16[32,4096]{1,0:T(8,128)(2,1)S(1)}, bf16[32,4096]{1,0:T(8,128)(2,1)S(1)}, u32[]{:S(2)}, u32[]{:S(2)}) collective-permute-start(bf16[32,4096]{1,0:T(8,128)(2,1)S(1)} %copy-done.2), channel_id=1, source_target_pairs={{0,4},{1,5},{2,6},{3,7},{4,0},{5,1},{6,2},{7,3},{8,12},{9,13},{10,... | collective-permute-start | bytes 786440 | tf_op jit(solution)/shard_map/ppermute | solution.py:632
  23.7 14.6 %collective-permute-start.11 = (bf16[32,4096]{1,0:T(8,128)(2,1)S(1)}, bf16[32,4096]{1,0:T(8,128)(2,1)S(1)}, u32[]{:S(2)}, u32[]{:S(2)}) collective-permute-start(bf16[32,4096]{1,0:T(8,128)(2,1)S(1)} %copy-done.2), channel_id=1, source_target_pairs={{0,6},{1,7},{2,4},{3,5},{4,2},{5,3},{6,0},{7,1},{8,14},{9,15},{10,... | collective-permute-start | bytes 786440 | tf_op jit(solution)/shard_map/ppermute | solution.py:632
  26.1 12.5 %collective-permute-start.9 = (bf16[32,4096]{1,0:T(8,128)(2,1)S(1)}, bf16[32,4096]{1,0:T(8,128)(2,1)S(1)}, u32[]{:S(2)}, u32[]{:S(2)}) collective-permute-start(bf16[32,4096]{1,0:T(8,128)(2,1)S(1)} %copy-done.2), channel_id=1, source_target_pairs={{0,2},{1,3},{2,0},{3,1},{4,6},{5,7},{6,4},{7,5},{8,10},{9,11},{10,... | collective-permute-start | bytes 786440 | tf_op jit(solution)/shard_map/ppermute | solution.py:632
  40.4 7.6 %copy-start.1 = (s32[64]{0:T(128)S(1)}, s32[64]{0:T(128)}, u32[]{:S(2)}) copy-start(s32[64]{0:T(128)} %refs_1_.1) | copy-start | bytes 772
  40.5 7.5 %collective-permute-start.13 = (f32[32,512]{1,0:T(8,128)S(1)}, f32[32,512]{1,0:T(8,128)S(1)}, u32[]{:S(2)}, u32[]{:S(2)}) collective-permute-start(f32[32,512]{1,0:T(8,128)S(1)} %get-tuple-element.63), channel_id=1, source_target_pairs={{0,2},{1,3},{2,0},{3,1},{4,6},{5,7},{6,4},{7,5},{8,10},{9,11},{10,... | collective-permute-start | bytes 196616 | tf_op jit(solution)/shard_map/ppermute | solution.py:632
  42.0 6.0 %collective-permute-start.14 = (f32[32,512]{1,0:T(8,128)S(1)}, f32[32,512]{1,0:T(8,128)S(1)}, u32[]{:S(2)}, u32[]{:S(2)}) collective-permute-start(f32[32,512]{1,0:T(8,128)S(1)} %get-tuple-element.62), channel_id=1, source_target_pairs={{0,4},{1,5},{2,6},{3,7},{4,0},{5,1},{6,2},{7,3},{8,12},{9,13},{10,... | collective-permute-start | bytes 196616 | tf_op jit(solution)/shard_map/ppermute | solution.py:632
  42.6 5.4 %collective-permute-start.15 = (f32[32,512]{1,0:T(8,128)S(1)}, f32[32,512]{1,0:T(8,128)S(1)}, u32[]{:S(2)}, u32[]{:S(2)}) collective-permute-start(f32[32,512]{1,0:T(8,128)S(1)} %get-tuple-element.61), channel_id=1, source_target_pairs={{0,6},{1,7},{2,4},{3,5},{4,2},{5,3},{6,0},{7,1},{8,14},{9,15},{10,... | collective-permute-start | bytes 196616 | tf_op jit(solution)/shard_map/ppermute | solution.py:632

commit v5 on v3

--- a/solution.py
+++ b/solution.py
@@ -193,12 +193,14 @@
         spread_in = [sublane_row(pivot_rows, j) for j in range(SUB)]
         spread, forward, cross, beyond, entry = solve_small(entry, spread_in, cross, beyond, ahead)
         for i in range(s + 1, count):
+            value = jnp.where(inside, 0.0, rows[i])
             if i <= s + 2:
-                columns, lines = (cross if i == s + 1 else beyond), forward
+                columns = cross if i == s + 1 else beyond
+                value = value - tree_sum([columns[j] * forward[j] for j in range(SUB)])
             else:
-                columns, lines = [lane_column(rows[i], base + j) for j in range(SUB)], spread
-            change = tree_sum([columns[j] * lines[j] for j in range(SUB)])
-            rows[i] = jnp.where(inside, 0.0, rows[i]) - change
+                for j in range(SUB):
+                    value = value - lane_column(rows[i], base + j) * spread[j]
+            rows[i] = value
         new = spread[SUB - 1]
         for j in range(SUB - 1):
             new = jnp.where(sub == j, spread[j], new)

time: 57.9 us -> 58 us (level)
  no operation moved by 1% of the time
where the time goes in v5:
time: 58 us; the launch traced here: 57.8 us
  Pallas kernels  29.5 us (51%)
  starting transfers between devices  15.4 us (27%)
  waiting for transfers between devices  10.1 us (17%)
  matrix products  1.71 us (3%)
  local copies, waits for them, and re-layouts  0.76 us (1%)
    ppermute x15, starting transfers between devices, swap(): return lax.ppermute(x, 'dp', [(d, d ^ k) for d in range(n)])  13.5 us
    pallas_call x1, Pallas kernels, first_part(): pl.pallas_call(body, out_shape=[jax.ShapeDtypeStruct((kept, kept), jnp.fl...  11.8 us
    ppermute x15, waiting for transfers between devices, swap(): return lax.ppermute(x, 'dp', [(d, d ^ k) for d in range(n)])  10.1 us
    pallas_call x1, Pallas kernels, last_part(): pl.pallas_call(body, out_shape=jax.ShapeDtypeStruct((own, features), jnp....  9.51 us
    pallas_call x1, Pallas kernels, middle_part(): pl.pallas_call(functools.partial(middle_kernel, first, last), out_shape=[...  4.06 us
    pallas_call x1, Pallas kernels, select_kept(): pl.pallas_call(select_kernel, out_shape=[jax.ShapeDtypeStruct((kept + EXT...  2.39 us
    ppermute x1, starting transfers between devices, level(): lax.ppermute(x, 'section', [(d, d ^ 1) for d in range(mesh.shape['section...  1.97 us
    pallas_call x1, Pallas kernels, early_gram(): pl.pallas_call(body, out_shape=[jax.ShapeDtypeStruct((kept, kept), jnp.fl...  1.72 us
  transfers between devices with their start and end apart: 16, of which 3 were waited for; matrix products, arithmetic and copies ran while one was open for 0% of the time, Pallas kernels for 30%

profile of v5, /device:TPU:0, one launch (start us, length us, event | category | flops | bytes accessed | tf_op | source)
XLA Modules:
  0.0 57.8 jit_solution(11122973133344491537)
XLA Ops:
  0.0 0.0 copy-start
  0.0 0.7 %copy-done = s32[64]{0:T(128)S(1)} copy-done((s32[64]{0:T(128)S(1)}, s32[64]{0:T(128)}, u32[]{:S(2)}) %copy-start) | copy-done | bytes 280
  0.7 0.0 copy-start.2
  0.7 2.4 %select_kept.1 = (bf16[784,256]{1,0:T(8,128)(2,1)S(1)}, bf16[400,256]{1,0:T(8,128)(2,1)S(1)}) custom-call(s32[1]{0:T(128)} %bitcast.side_ref.refs_0_, s32[64]{0:T(128)S(1)} %copy-done, bf16[256,4096]{1,0:T(8,128)(2,1)} %refs_2_), custom_call_target="tpu_custom_call" | custom-call | tf_op jit(solution)/shard_map/select_kept/pallas_call | solution.py:90
  3.1 0.5 collective-permute-start.12
  3.6 3.5 %collective-permute-start.3 = (bf16[400,256]{1,0:T(8,128)(2,1)S(1)}, bf16[400,256]{1,0:T(8,128)(2,1)S(1)}, u32[]{:S(2)}, u32[]{:S(2)}) collective-permute-start(bf16[400,256]{1,0:T(8,128)(2,1)S(1)} %get-tuple-element.38), channel_id=1, source_target_pairs={{0,6},{1,7},{2,4},{3,5},{4,2},{5,3},{6,0},{7,1},{8,14},{9,15},{10,... | collective-permute-start | bytes 614408 | tf_op jit(solution)/shard_map/ppermute | solution.py:632
  7.1 0.2 collective-permute-start.2
  7.3 0.5 collective-permute-start
  7.8 0.3 collective-permute-start.1
  8.1 5.0 %collective-permute-done.3.refs_7_.refs_18_ = bf16[400,256]{1,0:T(8,128)(2,1)S(1)} collective-permute-done((bf16[400,256]{1,0:T(8,128)(2,1)S(1)}, bf16[400,256]{1,0:T(8,128)(2,1)S(1)}, u32[]{:S(2)}, u32[]{:S(2)}) %collective-permute-start.3) | collective-permute-done | bytes 204832 | tf_op jit(solution)/shard_map/ppermute | solution.py:632
  13.1 0.0 collective-permute-start.4
  13.1 0.0 collective-permute-done.2.refs_1_.refs_13_
  13.1 2.0 %collective-permute-start.7 = (bf16[400,256]{1,0:T(8,128)(2,1)S(1)}, bf16[400,256]{1,0:T(8,128)(2,1)S(1)}, u32[]{:S(2)}, u32[]{:S(2)}) collective-permute-start(bf16[400,256]{1,0:T(8,128)(2,1)S(1)} %collective-permute-done.3.refs_7_.refs_18_), channel_id=1, source_target_pairs={{0,8},{8,0},{16,24},{24,16},{1,9},{9,1},{17,25},{25,17},{2,10},{10... | collective-permute-start | bytes 614408 | tf_op jit(solution)/shard_map/ppermute | solution.py:635
  15.1 1.7 %early_gram.1 = (f32[768,768]{1,0:T(8,128)S(1)}, f32[8,128]{1,0:T(8,128)S(1)}, bf16[256,4096]{1,0:T(8,128)(2,1)S(1)}) custom-call(bf16[784,256]{1,0:T(8,128)(2,1)S(1)} %get-tuple-element.34.refs_0_.refs_12_, bf16[784,256]{1,0:T(8,128)(2,1)S(1)} %collective-permute-done.2.refs_1_.refs_13_, bf16[256,4096]{1,0:T(8,128)(2,1)} %refs_2_), custom_call_target="tpu_custom_call" | custom-call | tf_op jit(solution)/shard_map/early_gram/pallas_call | solution.py:377
  16.8 4.9 %collective-permute-done.refs_3_.refs_14_ = bf16[784,256]{1,0:T(8,128)(2,1)S(1)} collective-permute-done((bf16[784,256]{1,0:T(8,128)(2,1)S(1)}, bf16[784,256]{1,0:T(8,128)(2,1)S(1)}, u32[]{:S(2)}, u32[]{:S(2)}) %collective-permute-start) | collective-permute-done | bytes 401440 | tf_op jit(solution)/shard_map/ppermute | solution.py:632
  21.7 0.0 collective-permute-done.1.refs_5_.refs_16_
  21.7 0.0 collective-permute-done.4.refs_9_.refs_20_
  21.7 0.0 collective-permute-start.5
  21.7 0.0 collective-permute-done.7.refs_8_.refs_19_
  21.7 0.5 collective-permute-start.8
  22.2 0.1 collective-permute-start.6
  22.3 0.0 copy-done.2
  22.3 1.4 %collective-permute-start.10 = (bf16[32,4096]{1,0:T(8,128)(2,1)S(1)}, bf16[32,4096]{1,0:T(8,128)(2,1)S(1)}, u32[]{:S(2)}, u32[]{:S(2)}) collective-permute-start(bf16[32,4096]{1,0:T(8,128)(2,1)S(1)} %copy-done.2), channel_id=1, source_target_pairs={{0,4},{1,5},{2,6},{3,7},{4,0},{5,1},{6,2},{7,3},{8,12},{9,13},{10,... | collective-permute-start | bytes 786440 | tf_op jit(solution)/shard_map/ppermute | solution.py:632
  23.7 0.0 collective-permute-done.8.refs_10_.refs_21_
  23.7 2.3 %collective-permute-start.11 = (bf16[32,4096]{1,0:T(8,128)(2,1)S(1)}, bf16[32,4096]{1,0:T(8,128)(2,1)S(1)}, u32[]{:S(2)}, u32[]{:S(2)}) collective-permute-start(bf16[32,4096]{1,0:T(8,128)(2,1)S(1)} %copy-done.2), channel_id=1, source_target_pairs={{0,6},{1,7},{2,4},{3,5},{4,2},{5,3},{6,0},{7,1},{8,14},{9,15},{10,... | collective-permute-start | bytes 786440 | tf_op jit(solution)/shard_map/ppermute | solution.py:632
  26.1 0.0 collective-permute-done.5.refs_4_.refs_15_
  26.1 0.5 collective-permute-start.9
  26.6 0.0 collective-permute-done.6.refs_6_.refs_17_
  26.6 11.8 %gram_and_first_panels.1 = (f32[768,768]{1,0:T(8,128)S(1)}, f32[8,128]{1,0:T(8,128)S(1)}, f32[3,2,128,128]{3,2,1,0:T(8,128)S(1)}, f32[128,128]{1,0:T(8,128)S(1)}) custom-call(s32[1]{0:T(128)} %bitcast.side_ref.refs_0_, f32[768,768]{1,0:T(8,128)S(1)} %get-tuple-element.39.refs_1_, f32[8,128]{1,0:T(8,128)S(1)} %get-tuple-element.40.refs_2_, ...), custom_call_target="tpu_custom_call" | custom-call | tf_op jit(solution)/shard_map/gram_and_first_panels/pallas_call | solution.py:432
  38.4 0.0 collective-permute-done.10
  38.4 0.0 collective-permute-done.11
  38.4 0.2 collective-permute-done.9
  38.6 0.0 collective-permute-done.12
  38.7 0.9 %fusion.1 = f32[128,256]{1,0:T(8,128)S(1)} fusion(bf16[128,4096]{1,0:T(8,128)(2,1)S(1)} %constant_dynamic-update-slice_fusion, bf16[256,4096]{1,0:T(8,128)(2,1)S(1)} %get-tuple-element.50), kind=kOutput, calls=%fused_computation.6 | convolution fusion | flops 268435456 | bytes 3276800 | tf_op jit(solution)/shard_map/dot_general | solution.py:674
  39.6 0.8 %fusion.2 = f32[128,256]{1,0:T(8,128)S(1)} fusion(bf16[128,4096]{1,0:T(8,128)(2,1)S(1)} %constant_dynamic-update-slice_fusion, bf16[256,4096]{1,0:T(8,128)(2,1)S(1)} %collective-permute-done.12), kind=kOutput, calls=%fused_computation.7 | convolution fusion | flops 268435456 | bytes 3276800 | tf_op jit(solution)/shard_map/dot_general | solution.py:674
  40.4 0.0 copy-start.1
  40.5 1.6 %collective-permute-start.13 = (f32[32,512]{1,0:T(8,128)S(1)}, f32[32,512]{1,0:T(8,128)S(1)}, u32[]{:S(2)}, u32[]{:S(2)}) collective-permute-start(f32[32,512]{1,0:T(8,128)S(1)} %get-tuple-element.63), channel_id=1, source_target_pairs={{0,2},{1,3},{2,0},{3,1},{4,6},{5,7},{6,4},{7,5},{8,10},{9,11},{10,... | collective-permute-start | bytes 196616 | tf_op jit(solution)/shard_map/ppermute | solution.py:632
  42.0 0.6 %collective-permute-start.14 = (f32[32,512]{1,0:T(8,128)S(1)}, f32[32,512]{1,0:T(8,128)S(1)}, u32[]{:S(2)}, u32[]{:S(2)}) collective-permute-start(f32[32,512]{1,0:T(8,128)S(1)} %get-tuple-element.62), channel_id=1, source_target_pairs={{0,4},{1,5},{2,6},{3,7},{4,0},{5,1},{6,2},{7,3},{8,12},{9,13},{10,... | collective-permute-start | bytes 196616 | tf_op jit(solution)/shard_map/ppermute | solution.py:632
  42.6 1.4 %collective-permute-start.15 = (f32[32,512]{1,0:T(8,128)S(1)}, f32[32,512]{1,0:T(8,128)S(1)}, u32[]{:S(2)}, u32[]{:S(2)}) collective-permute-start(f32[32,512]{1,0:T(8,128)S(1)} %get-tuple-element.61), channel_id=1, source_target_pairs={{0,6},{1,7},{2,4},{3,5},{4,2},{5,3},{6,0},{7,1},{8,14},{9,15},{10,... | collective-permute-start | bytes 196616 | tf_op jit(solution)/shard_map/ppermute | solution.py:632
  44.0 4.1 %middle_panels.1 = (f32[512,512]{1,0:T(8,128)S(1)}, f32[1,2,128,128]{3,2,1,0:T(8,128)S(1)}, f32[128,128]{1,0:T(8,128)S(1)}) custom-call(f32[768,768]{1,0:T(8,128)S(1)} %get-tuple-element.55.start_ref.refs_7_, f32[3,2,128,128]{3,2,1,0:T(8,128)S(1)} %get-tuple-element.56.early_ref.refs_8_, f32[128,128]{1,0:T(8,128)S(1)} %get-tuple-element.57.start_next_ref), custom_call_target="tpu_custom_call" | custom-call | tf_op jit(solution)/shard_map/middle_panels/pallas_call | solution.py:478
  48.1 0.0 collective-permute-done.13.refs_3_
  48.1 0.0 collective-permute-done.14.refs_4_
  48.1 0.0 collective-permute-done.15.refs_5_
  48.1 0.0 copy-done.1
  48.1 9.5 %last_panels_and_solution.1 = bf16[32,4096]{1,0:T(8,128)(2,1)} custom-call(s32[1]{0:T(128)} %bitcast.side_ref.refs_0_, s32[64]{0:T(128)S(1)} %copy-done.1, f32[32,512]{1,0:T(8,128)S(1)} %get-tuple-element.64.refs_2_, f32[32,512]{1,0:T(8,128)S(1)} %collective-permute-done.13.refs_3_, f32[32,512]{1,0:T(8,128)S(1)} %collective-permute-done.14.refs_4_, ...), custom_call_target="tpu_custom_call" | custom-call | tf_op jit(solution)/shard_map/last_panels_and_solution/pallas_call | solution.py:605
  (6 shorter events, 0.1 us)
Async XLA Ops:
  0.0 0.7 %copy-start = (s32[64]{0:T(128)S(1)}, s32[64]{0:T(128)}, u32[]{:S(2)}) copy-start(s32[64]{0:T(128)} %refs_1_.1) | copy-start | bytes 772
  0.7 21.6 %copy-start.2 = (bf16[32,4096]{1,0:T(8,128)(2,1)S(1)}, bf16[32,4096]{1,0:T(8,128)(2,1)}, u32[]{:S(2)}) copy-start(bf16[32,4096]{1,0:T(8,128)(2,1)} %param.4) | copy-start | bytes 786436
  3.1 35.5 %collective-permute-start.12 = (bf16[256,4096]{1,0:T(8,128)(2,1)}, bf16[256,4096]{1,0:T(8,128)(2,1)S(1)}, u32[]{:S(2)}, u32[]{:S(2)}) collective-permute-start(bf16[256,4096]{1,0:T(8,128)(2,1)} %refs_2_), channel_id=1, source_target_pairs={{0,1},{1,0},{2,3},{3,2},{4,5},{5,4},{6,7},{7,6},{8,9},{9,8},{10,11... | collective-permute-start | bytes 6291464 | tf_op jit(solution)/shard_map/ppermute | solution.py:632
  3.6 9.5 %collective-permute-start.3 = (bf16[400,256]{1,0:T(8,128)(2,1)S(1)}, bf16[400,256]{1,0:T(8,128)(2,1)S(1)}, u32[]{:S(2)}, u32[]{:S(2)}) collective-permute-start(bf16[400,256]{1,0:T(8,128)(2,1)S(1)} %get-tuple-element.38), channel_id=1, source_target_pairs={{0,6},{1,7},{2,4},{3,5},{4,2},{5,3},{6,0},{7,1},{8,14},{9,15},{10,... | collective-permute-start | bytes 614408 | tf_op jit(solution)/shard_map/ppermute | solution.py:632
  7.1 6.0 %collective-permute-start.2 = (bf16[784,256]{1,0:T(8,128)(2,1)S(1)}, bf16[784,256]{1,0:T(8,128)(2,1)S(1)}, u32[]{:S(2)}, u32[]{:S(2)}) collective-permute-start(bf16[784,256]{1,0:T(8,128)(2,1)S(1)} %get-tuple-element.34.refs_0_.refs_12_), channel_id=1, source_target_pairs={{0,1},{1,0},{2,3},{3,2},{4,5},{5,4},{6,7},{7,6},{8,9},{9,8},{10,11... | collective-permute-start | bytes 1204232 | tf_op jit(solution)/shard_map/ppermute | solution.py:632
  7.3 14.4 %collective-permute-start = (bf16[784,256]{1,0:T(8,128)(2,1)S(1)}, bf16[784,256]{1,0:T(8,128)(2,1)S(1)}, u32[]{:S(2)}, u32[]{:S(2)}) collective-permute-start(bf16[784,256]{1,0:T(8,128)(2,1)S(1)} %get-tuple-element.34.refs_0_.refs_12_), channel_id=1, source_target_pairs={{0,2},{1,3},{2,0},{3,1},{4,6},{5,7},{6,4},{7,5},{8,10},{9,11},{10,... | collective-permute-start | bytes 1204232 | tf_op jit(solution)/shard_map/ppermute | solution.py:632
  7.8 13.9 %collective-permute-start.1 = (bf16[784,256]{1,0:T(8,128)(2,1)S(1)}, bf16[784,256]{1,0:T(8,128)(2,1)S(1)}, u32[]{:S(2)}, u32[]{:S(2)}) collective-permute-start(bf16[784,256]{1,0:T(8,128)(2,1)S(1)} %get-tuple-element.34.refs_0_.refs_12_), channel_id=1, source_target_pairs={{0,4},{1,5},{2,6},{3,7},{4,0},{5,1},{6,2},{7,3},{8,12},{9,13},{10,... | collective-permute-start | bytes 1204232 | tf_op jit(solution)/shard_map/ppermute | solution.py:632
  13.1 8.6 %collective-permute-start.4 = (bf16[400,256]{1,0:T(8,128)(2,1)S(1)}, bf16[400,256]{1,0:T(8,128)(2,1)S(1)}, u32[]{:S(2)}, u32[]{:S(2)}) collective-permute-start(bf16[400,256]{1,0:T(8,128)(2,1)S(1)} %collective-permute-done.3.refs_7_.refs_18_), channel_id=1, source_target_pairs={{0,1},{1,0},{2,3},{3,2},{4,5},{5,4},{6,7},{7,6},{8,9},{9,8},{10,11... | collective-permute-start | bytes 614408 | tf_op jit(solution)/shard_map/ppermute | solution.py:632
  13.1 8.6 %collective-permute-start.7 = (bf16[400,256]{1,0:T(8,128)(2,1)S(1)}, bf16[400,256]{1,0:T(8,128)(2,1)S(1)}, u32[]{:S(2)}, u32[]{:S(2)}) collective-permute-start(bf16[400,256]{1,0:T(8,128)(2,1)S(1)} %collective-permute-done.3.refs_7_.refs_18_), channel_id=1, source_target_pairs={{0,8},{8,0},{16,24},{24,16},{1,9},{9,1},{17,25},{25,17},{2,10},{10... | collective-permute-start | bytes 614408 | tf_op jit(solution)/shard_map/ppermute | solution.py:635
  21.7 4.4 %collective-permute-start.5 = (bf16[784,256]{1,0:T(8,128)(2,1)S(1)}, bf16[784,256]{1,0:T(8,128)(2,1)S(1)}, u32[]{:S(2)}, u32[]{:S(2)}) collective-permute-start(bf16[784,256]{1,0:T(8,128)(2,1)S(1)} %collective-permute-done.refs_3_.refs_14_), channel_id=1, source_target_pairs={{0,1},{1,0},{2,3},{3,2},{4,5},{5,4},{6,7},{7,6},{8,9},{9,8},{10,11... | collective-permute-start | bytes 1204232 | tf_op jit(solution)/shard_map/ppermute | solution.py:632
  21.7 2.0 %collective-permute-start.8 = (bf16[400,256]{1,0:T(8,128)(2,1)S(1)}, bf16[400,256]{1,0:T(8,128)(2,1)S(1)}, u32[]{:S(2)}, u32[]{:S(2)}) collective-permute-start(bf16[400,256]{1,0:T(8,128)(2,1)S(1)} %collective-permute-done.7.refs_8_.refs_19_), channel_id=1, source_target_pairs={{0,1},{1,0},{2,3},{3,2},{4,5},{5,4},{6,7},{7,6},{8,9},{9,8},{10,11... | collective-permute-start | bytes 614408 | tf_op jit(solution)/shard_map/ppermute | solution.py:632
  22.2 4.4 %collective-permute-start.6 = (bf16[784,256]{1,0:T(8,128)(2,1)S(1)}, bf16[784,256]{1,0:T(8,128)(2,1)S(1)}, u32[]{:S(2)}, u32[]{:S(2)}) collective-permute-start(bf16[784,256]{1,0:T(8,128)(2,1)S(1)} %collective-permute-done.1.refs_5_.refs_16_), channel_id=1, source_target_pairs={{0,1},{1,0},{2,3},{3,2},{4,5},{5,4},{6,7},{7,6},{8,9},{9,8},{10,11... | collective-permute-start | bytes 1204232 | tf_op jit(solution)/shard_map/ppermute | solution.py:632
  22.3 16.1 %collective-permute-start.10 = (bf16[32,4096]{1,0:T(8,128)(2,1)S(1)}, bf16[32,4096]{1,0:T(8,128)(2,1)S(1)}, u32[]{:S(2)}, u32[]{:S(2)}) collective-permute-start(bf16[32,4096]{1,0:T(8,128)(2,1)S(1)} %copy-done.2), channel_id=1, source_target_pairs={{0,4},{1,5},{2,6},{3,7},{4,0},{5,1},{6,2},{7,3},{8,12},{9,13},{10,... | collective-permute-start | bytes 786440 | tf_op jit(solution)/shard_map/ppermute | solution.py:632
  23.7 14.7 %collective-permute-start.11 = (bf16[32,4096]{1,0:T(8,128)(2,1)S(1)}, bf16[32,4096]{1,0:T(8,128)(2,1)S(1)}, u32[]{:S(2)}, u32[]{:S(2)}) collective-permute-start(bf16[32,4096]{1,0:T(8,128)(2,1)S(1)} %copy-done.2), channel_id=1, source_target_pairs={{0,6},{1,7},{2,4},{3,5},{4,2},{5,3},{6,0},{7,1},{8,14},{9,15},{10,... | collective-permute-start | bytes 786440 | tf_op jit(solution)/shard_map/ppermute | solution.py:632
  26.1 12.5 %collective-permute-start.9 = (bf16[32,4096]{1,0:T(8,128)(2,1)S(1)}, bf16[32,4096]{1,0:T(8,128)(2,1)S(1)}, u32[]{:S(2)}, u32[]{:S(2)}) collective-permute-start(bf16[32,4096]{1,0:T(8,128)(2,1)S(1)} %copy-done.2), channel_id=1, source_target_pairs={{0,2},{1,3},{2,0},{3,1},{4,6},{5,7},{6,4},{7,5},{8,10},{9,11},{10,... | collective-permute-start | bytes 786440 | tf_op jit(solution)/shard_map/ppermute | solution.py:632
  40.4 7.7 %copy-start.1 = (s32[64]{0:T(128)S(1)}, s32[64]{0:T(128)}, u32[]{:S(2)}) copy-start(s32[64]{0:T(128)} %refs_1_.1) | copy-start | bytes 772
  40.5 7.6 %collective-permute-start.13 = (f32[32,512]{1,0:T(8,128)S(1)}, f32[32,512]{1,0:T(8,128)S(1)}, u32[]{:S(2)}, u32[]{:S(2)}) collective-permute-start(f32[32,512]{1,0:T(8,128)S(1)} %get-tuple-element.63), channel_id=1, source_target_pairs={{0,2},{1,3},{2,0},{3,1},{4,6},{5,7},{6,4},{7,5},{8,10},{9,11},{10,... | collective-permute-start | bytes 196616 | tf_op jit(solution)/shard_map/ppermute | solution.py:632
  42.0 6.1 %collective-permute-start.14 = (f32[32,512]{1,0:T(8,128)S(1)}, f32[32,512]{1,0:T(8,128)S(1)}, u32[]{:S(2)}, u32[]{:S(2)}) collective-permute-start(f32[32,512]{1,0:T(8,128)S(1)} %get-tuple-element.62), channel_id=1, source_target_pairs={{0,4},{1,5},{2,6},{3,7},{4,0},{5,1},{6,2},{7,3},{8,12},{9,13},{10,... | collective-permute-start | bytes 196616 | tf_op jit(solution)/shard_map/ppermute | solution.py:632
  42.6 5.5 %collective-permute-start.15 = (f32[32,512]{1,0:T(8,128)S(1)}, f32[32,512]{1,0:T(8,128)S(1)}, u32[]{:S(2)}, u32[]{:S(2)}) collective-permute-start(f32[32,512]{1,0:T(8,128)S(1)} %get-tuple-element.61), channel_id=1, source_target_pairs={{0,6},{1,7},{2,4},{3,5},{4,2},{5,3},{6,0},{7,1},{8,14},{9,15},{10,... | collective-permute-start | bytes 196616 | tf_op jit(solution)/shard_map/ppermute | solution.py:632
